TPU v7x, 256 devices: a whole 4x4x8 slice. The times are simulated.
256 devices in a mesh: row: 8 (over y, core), col: 32 (over z, x).
Axes of the slice: x: 4, y: 4, z: 8, core: 2. Of those that a mesh axis runs over, the one named last changes fastest.
Arguments:
- layer_input: bfloat16 [512, 8192], P('row', 'col'), may hold values from -36 to 36, as said below
- norm_gain: float32 [8192], P('col'), may hold values from 0.1 to 1.9
- w_gate: bfloat16 [8192, 14336], P('col', 'row'), may hold values from -0.09375 to 0.09375
- w_up: bfloat16 [8192, 14336], P('col', 'row'), may hold values from -0.09375 to 0.09375
- w_down: bfloat16 [14336, 8192], P('row', 'col'), may hold values from -0.09375 to 0.09375
- mask_gate: int32 [64, 112], P('col', 'row'), may hold values 0 or 1
- mask_up: int32 [64, 112], P('col', 'row'), may hold values 0 or 1
- mask_down: int32 [112, 64], P('row', 'col'), may hold values 0 or 1
- out_grad: bfloat16 [512, 8192], P('row', 'col'), may hold values from -6 to 6
Outputs:
- layer_out: bfloat16 [512, 8192], P('row', 'col')
- input_grad: bfloat16 [512, 8192], P('row', 'col')
- gain_grad: float32 [8192], P('col')
- gate_wgrad: bfloat16 [8192, 14336], P('col', 'row')
- up_wgrad: bfloat16 [8192, 14336], P('col', 'row')
- down_wgrad: bfloat16 [14336, 8192], P('row', 'col')
Inputs may be any that keep to these rules, and one draw needn't show every extreme that they name: `layer_input`: the layer input's rows and features have scales that differ by up to a factor of ten.
All inputs are finite; a program needn't handle non-finite values. No bound on the sum of `mask_gate` or of `mask_up` or of `mask_down` on one device may be relied on, other than what follows from the above.
Results may differ from a plain program's by a relative error of at most 0.02.
Values may be sent and summed in bfloat16 or wider, within the bound.
No kernel may reach another device: no remote copies, remote signals or barrier semaphores. Data moves between devices by JAX's collectives and lax.ppermute only.
A program may use at most 192 MiB of HBM per device.

v0:
```python
import jax
import jax.numpy as jnp
from jax import lax
from jax.sharding import Mesh
from jax.sharding import PartitionSpec as P

D = 8192
COL = ("col_0", "col_1")


norm_eps = 1e-05


def from_everyone(shard, axis):
    copies = jnp.broadcast_to(shard, (lax.axis_size(axis), *shard.shape))
    return lax.all_to_all(copies, axis, split_axis=0, concat_axis=0, tiled=True)


def over_copies(shard, axis):
    everything = from_everyone(shard, axis)
    return jnp.sum(everything, axis=0)


def in_order(pieces, dim):
    pieces = jnp.moveaxis(pieces, 0, dim)
    lengths = pieces.shape
    return pieces.reshape(*lengths[:dim], lengths[dim] * lengths[dim + 1], *lengths[dim + 2 :])


def gathered_copies(shard, axis, dim):
    return in_order(from_everyone(shard, axis), dim)


def scatter_axes(shard, axes, dim):
    for axis in axes:
        shard = lax.psum_scatter(shard, axis, scatter_dimension=dim, tiled=True)
    return shard


def gathered_by_axis(shard, axes, dim):
    out = shard
    for number in range(len(axes) - 1, -1, -1):
        out = lax.all_gather(out, axes[number], axis=dim, tiled=True)
    return out


def in_blocks(shard, dim, count):
    before, after = (shard.shape[:dim], shard.shape[dim + 1 :])
    return jnp.moveaxis(shard.reshape(*before, count, -1, *after), dim, 0)


def sent_and_summed(shard, axis, dim):
    count = lax.axis_size(axis)
    pieces = lax.all_to_all(in_blocks(shard, dim, count), axis, 0, 0, tiled=True)
    return jnp.sum(pieces.astype(jnp.float32), axis=0)


def sum_by_axis(terms, axes):
    total = terms.astype(jnp.bfloat16)
    for axis in axes:
        total = lax.psum_scatter(total, axis, scatter_dimension=0, tiled=True)
    return total.astype(jnp.float32)


def side_by_side(arrays, axis, dim, along):
    both = jnp.concatenate(arrays, axis=along)
    out, at, done = (lax.all_gather(both, axis, axis=dim, tiled=True), 0, [])
    for a in arrays:
        done.append(lax.slice_in_dim(out, at, at + a.shape[along], axis=along))
        at += a.shape[along]
    return tuple(done)


def apply_mask(weight, mask):
    block_rows, block_cols = mask.shape
    row_count, col_count = weight.shape
    blocks = weight.reshape(
        block_rows, row_count // block_rows, block_cols, col_count // block_cols
    )
    keep = mask.astype(weight.dtype)[:, None, :, None]
    return (blocks * keep).reshape(row_count, col_count)


def contract_rows(left, right):
    return lax.dot_general(
        left, right, (((0,), (0,)), ((), ())), preferred_element_type=jnp.float32
    )


def contract_cols(left, right):
    return lax.dot_general(
        left, right, (((1,), (1,)), ((), ())), preferred_element_type=jnp.float32
    )


def shards(layer_input, norm_gain, w_gate, w_up, w_down, mask_gate, mask_up, mask_down, out_grad):
    x_float = layer_input.astype(jnp.float32)
    squares = jnp.sum(x_float * x_float, axis=1)
    totals = over_copies(squares, COL)
    scale = lax.rsqrt(totals / D + norm_eps)[:, None]
    normed = (x_float * scale * norm_gain[None, :]).astype(jnp.bfloat16)
    eff_gate = apply_mask(w_gate, mask_gate)
    eff_up = apply_mask(w_up, mask_up)
    eff_down = apply_mask(w_down, mask_down)
    normed_all = gathered_copies(normed, "row", 0)
    gate_part = jnp.dot(normed_all, eff_gate, preferred_element_type=jnp.float32)
    up_part = jnp.dot(normed_all, eff_up, preferred_element_type=jnp.float32)
    gate_mine, up_mine = (scatter_axes(gate_part, COL, 0), scatter_axes(up_part, COL, 0))
    act_mine = (jax.nn.silu(gate_mine) * up_mine).astype(jnp.bfloat16)
    act_all = gathered_by_axis(act_mine, COL, 0)
    down_part = jnp.dot(act_all, eff_down, preferred_element_type=jnp.float32)
    down_sum = sent_and_summed(down_part.astype(jnp.bfloat16), "row", 0)
    layer_out = (x_float + down_sum).astype(jnp.bfloat16)
    grad_all = gathered_copies(out_grad, "row", 0)
    act_grad = sum_by_axis(contract_cols(grad_all, eff_down), COL)
    down_wgrad = apply_mask(contract_rows(act_all, grad_all), mask_down).astype(jnp.bfloat16)
    sig = jax.nn.sigmoid(gate_mine)
    gate_grad = (act_grad * up_mine * sig * (1.0 + gate_mine * (1.0 - sig))).astype(jnp.bfloat16)
    up_grad = (act_grad * gate_mine * sig).astype(jnp.bfloat16)
    gate_grad_all, up_grad_all = side_by_side((gate_grad, up_grad), COL, 0, 1)
    gate_wgrad = apply_mask(contract_rows(normed_all, gate_grad_all), mask_gate).astype(
        jnp.bfloat16
    )
    up_wgrad = apply_mask(contract_rows(normed_all, up_grad_all), mask_up).astype(jnp.bfloat16)
    normed_grad = sent_and_summed(
        (contract_cols(gate_grad_all, eff_gate) + contract_cols(up_grad_all, eff_up)).astype(
            jnp.bfloat16
        ),
        "row",
        0,
    )
    gain_part = jnp.sum(normed_grad * x_float * scale, axis=0)
    dot_part = jnp.sum(normed_grad * norm_gain[None, :] * x_float, axis=1)
    gain_grad = over_copies(gain_part, "row")
    dots = over_copies(dot_part, COL)[:, None]
    input_grad = (
        out_grad.astype(jnp.float32)
        + scale * norm_gain[None, :] * normed_grad
        - x_float * scale * scale * scale * dots / D
    ).astype(jnp.bfloat16)
    return (layer_out, input_grad, gain_grad, gate_wgrad, up_wgrad, down_wgrad)


def solution(mesh):
    torus = Mesh(mesh.devices.reshape(mesh.shape["row"], 8, 4), ("row", "col_0", "col_1"))
    placed = (
        P("row", COL),
        P(COL),
        P(COL, "row"),
        P(COL, "row"),
        P("row", COL),
        P(COL, "row"),
        P(COL, "row"),
        P("row", COL),
        P("row", COL),
    )
    return jax.shard_map(
        shards,
        mesh=torus,
        in_specs=placed,
        out_specs=(
            P("row", COL),
            P("row", COL),
            P(COL),
            P(COL, "row"),
            P(COL, "row"),
            P("row", COL),
        ),
        check_vma=False,
    )
```

profile of v0, /device:TPU:1, one launch (start us, length us, event | category | flops | bytes accessed | tf_op | source)
XLA Modules:
  0.0 438.2 jit_solution(2829851463294816744)
XLA Ops:
  8.7 6.6 %all-to-all-start.3 = ((bf16[8,64,256]{2,1,0:T(8,128)(2,1)}), bf16[8,64,256]{2,1,0:T(8,128)(2,1)S(1)}, u32[]{:S(2)}, u32[]{:S(2)}) async-start(bf16[8,64,256]{2,1,0:T(8,128)(2,1)} %broadcast_in_dim.12), calls=%async_computation.7 | async-start | bytes 524288 | tf_op jit(solution)/shard_map/all_to_all | solution.py:16
  16.1 5.7 %all-to-all-done.3 = bf16[8,64,256]{2,1,0:T(8,128)(2,1)S(1)} async-done(((bf16[8,64,256]{2,1,0:T(8,128)(2,1)}), bf16[8,64,256]{2,1,0:T(8,128)(2,1)S(1)}, u32[]{:S(2)}, u32[]{:S(2)}) %all-to-all-start.3) | async-done | bytes 262176 | tf_op jit(solution)/shard_map/all_to_all | solution.py:16
  22.4 2.0 fusion
  25.3 18.8 %all_to_all.38 = f32[32,1,64]{2,1,0:T(1,128)S(1)} all-to-all(f32[32,1,64]{2,1,0:T(1,128)S(1)} %broadcast_in_dim.10), channel_id=1, replica_groups=mesh['row'=8,'col_0'=8,'col_1'=4] {'col_0','col_1'}, dimensions={0} | all-to-all | bytes 16384 | tf_op jit(solution)/shard_map/all_to_all | solution.py:16
  44.9 5.9 %all-to-all-start.1 = ((bf16[8,64,256]{2,1,0:T(8,128)(2,1)}), bf16[8,64,256]{2,1,0:T(8,128)(2,1)S(1)}, u32[]{:S(2)}, u32[]{:S(2)}) async-start(bf16[8,64,256]{2,1,0:T(8,128)(2,1)} %broadcast_in_dim.11), calls=%async_computation.1 | async-start | bytes 524288 | tf_op jit(solution)/shard_map/all_to_all | solution.py:16
  51.5 5.9 %all-to-all-done.1 = bf16[8,64,256]{2,1,0:T(8,128)(2,1)S(1)} async-done(((bf16[8,64,256]{2,1,0:T(8,128)(2,1)}), bf16[8,64,256]{2,1,0:T(8,128)(2,1)S(1)}, u32[]{:S(2)}, u32[]{:S(2)}) %all-to-all-start.1) | async-done | bytes 262176 | tf_op jit(solution)/shard_map/all_to_all | solution.py:16
  57.9 2.5 fusion.12
  61.2 2.2 copy.59
  64.9 3.7 fusion.11
  69.2 48.9 %reduce-scatter.11.cloned.1.call-done = f32[64,1792]{1,0:T(8,128)} async-done(((f32[512,1792]{1,0:T(8,128)}), f32[64,1792]{1,0:T(8,128)}) %reduce-scatter.11.cloned.1.call-update) | async-done | bytes 458768 | tf_op jit(solution)/shard_map/reduce_scatter | solution.py:36
  118.2 51.9 %reduce-scatter.7.cloned.1.call-done = f32[64,1792]{1,0:T(8,128)} async-done(((f32[512,1792]{1,0:T(8,128)}), f32[64,1792]{1,0:T(8,128)}) %reduce-scatter.7.cloned.1.call-update) | async-done | bytes 458768 | tf_op jit(solution)/shard_map/reduce_scatter | solution.py:36
  170.2 22.2 %reduce-scatter.17.cloned.1.call-done = bf16[16,1792]{1,0:T(8,128)(2,1)} async-done(((bf16[64,1792]{1,0:T(8,128)(2,1)}), bf16[16,1792]{1,0:T(8,128)(2,1)}) %reduce-scatter.17.cloned.1.call-update) | async-done | bytes 57360 | tf_op jit(solution)/shard_map/reduce_scatter | solution.py:61
  192.3 26.6 %reduce-scatter.13.cloned.1.call-done = f32[16,1792]{1,0:T(8,128)} async-done(((f32[64,1792]{1,0:T(8,128)}), f32[16,1792]{1,0:T(8,128)}) %reduce-scatter.13.cloned.1.call-update) | async-done | bytes 114704 | tf_op jit(solution)/shard_map/reduce_scatter | solution.py:36
  219.0 25.7 %reduce-scatter.9.cloned.1.call-done = f32[16,1792]{1,0:T(8,128)} async-done(((f32[64,1792]{1,0:T(8,128)}), f32[16,1792]{1,0:T(8,128)}) %reduce-scatter.9.cloned.1.call-update) | async-done | bytes 114704 | tf_op jit(solution)/shard_map/reduce_scatter | solution.py:36
  245.7 10.6 %all_gather.9 = bf16[64,1792]{1,0:T(8,128)(2,1)} all-gather(bf16[16,1792]{1,0:T(8,128)(2,1)S(1)} %get-tuple-element.29), channel_id=1, replica_groups=mesh['row'=8,'col_0'=8,'col_1'=4] {'col_1'}, dimensions={0}, use_global_device_ids=true | all-gather | bytes 286720 | tf_op jit(solution)/shard_map/all_gather | solution.py:43
  258.2 38.8 %all-gather.3.cloned.1.call-done = bf16[512,1792]{1,0:T(8,128)(2,1)} async-done(((bf16[64,1792]{1,0:T(8,128)(2,1)}), bf16[512,1792]{1,0:T(8,128)(2,1)}) %all-gather.3.cloned.1.call-update) | async-done | bytes 1835024 | tf_op jit(solution)/shard_map/all_gather | solution.py:43
  297.0 3.9 copy.71
  300.9 2.8 convolution_convert_fusion.1
  303.7 8.6 %all-to-all-start.2 = ((bf16[8,64,256]{2,1,0:T(8,128)(2,1)}), bf16[8,64,256]{2,1,0:T(8,128)(2,1)S(1)}, u32[]{:S(2)}, u32[]{:S(2)}) async-start(bf16[8,64,256]{2,1,0:T(8,128)(2,1)} %bitcast.103), calls=%async_computation.6 | async-start | bytes 524288 | tf_op jit(solution)/shard_map/all_to_all | solution.py:54
  312.4 2.2 multiply_convert_fusion
  316.5 2.3 all-to-all-done.2
  318.9 60.9 %all-gather.5.cloned.1.call-done = bf16[512,3584]{1,0:T(8,128)(2,1)} async-done(((bf16[16,3584]{1,0:T(8,128)(2,1)}), bf16[512,3584]{1,0:T(8,128)(2,1)}) %all-gather.5.cloned.1.call-update) | async-done | bytes 3670032 | tf_op jit(solution)/shard_map/all_gather | solution.py:67
  379.8 3.5 slice_bitcast_fusion
  383.4 3.8 copy.69
  387.2 2.5 fusion.1
  391.9 8.2 %all-to-all-start.4 = ((bf16[8,64,256]{2,1,0:T(8,128)(2,1)}), bf16[8,64,256]{2,1,0:T(8,128)(2,1)S(1)}, u32[]{:S(2)}, u32[]{:S(2)}) async-start(bf16[8,64,256]{2,1,0:T(8,128)(2,1)} %bitcast.5), calls=%async_computation.10 | async-start | bytes 524288 | tf_op jit(solution)/shard_map/all_to_all | solution.py:54
  400.2 2.3 copy.67
  402.5 2.3 multiply_convert_fusion.1
  407.4 4.3 all-to-all-start.6
  413.6 2.7 all-to-all-done.6
  417.0 5.1 %all-to-all-start.5 = ((f32[32,1,64]{2,1,0:T(1,128)}), f32[32,1,64]{2,1,0:T(1,128)S(1)}, u32[]{:S(2)}, u32[]{:S(2)}) async-start(f32[32,1,64]{2,1,0:T(1,128)} %broadcast_in_dim.13), calls=%async_computation.11 | async-start | bytes 32768 | tf_op jit(solution)/shard_map/all_to_all | solution.py:16
  424.3 6.2 %all-to-all-done.5 = f32[32,1,64]{2,1,0:T(1,128)S(1)} async-done(((f32[32,1,64]{2,1,0:T(1,128)}), f32[32,1,64]{2,1,0:T(1,128)S(1)}, u32[]{:S(2)}, u32[]{:S(2)}) %all-to-all-start.5) | async-done | bytes 8224 | tf_op jit(solution)/shard_map/all_to_all | solution.py:16
  (83 shorter events, 24.1 us)
Async XLA Ops:
  7.2 15.2 %copy-start.7 = (bf16[1792,256]{1,0:T(8,128)(2,1)S(1)}, bf16[1792,256]{1,0:T(8,128)(2,1)}, u32[]{:S(2)}) copy-start(bf16[1792,256]{1,0:T(8,128)(2,1)} %param.13) | copy-start | bytes 2752516
  8.7 13.1 %all-to-all-start.3 = ((bf16[8,64,256]{2,1,0:T(8,128)(2,1)}), bf16[8,64,256]{2,1,0:T(8,128)(2,1)S(1)}, u32[]{:S(2)}, u32[]{:S(2)}) async-start(bf16[8,64,256]{2,1,0:T(8,128)(2,1)} %broadcast_in_dim.12), calls=%async_computation.7 | async-start | bytes 524288 | tf_op jit(solution)/shard_map/all_to_all | solution.py:16
  15.3 53.4 %reduce-scatter.15.cloned.1.call-start = ((), (), s32[]{:S(2)}) async-start(), calls=%async_computation.18 | async-start | bytes 2064384 | tf_op jit(solution)/shard_map/reduce_scatter | solution.py:61
  24.4 0.8 copy-start.9
  24.4 19.7 %copy-start.11 = (f32[256]{0:T(256)S(1)}, f32[256]{0:T(256)}, u32[]{:S(2)}) copy-start(f32[256]{0:T(256)} %param.10) | copy-start | bytes 3076
  24.4 26.4 %copy-start.12 = (s32[2,14]{1,0:T(2,128)S(1)}, s32[2,14]{1,0:T(2,128)}, u32[]{:S(2)}) copy-start(s32[2,14]{1,0:T(2,128)} %param.15) | copy-start | bytes 340
  24.4 26.6 %copy-start.6 = (bf16[256,1792]{1,0:T(8,128)(2,1)S(1)}, bf16[256,1792]{1,0:T(8,128)(2,1)}, u32[]{:S(2)}) copy-start(bf16[256,1792]{1,0:T(8,128)(2,1)} %param.12) | copy-start | bytes 2752516
  44.9 12.4 %all-to-all-start.1 = ((bf16[8,64,256]{2,1,0:T(8,128)(2,1)}), bf16[8,64,256]{2,1,0:T(8,128)(2,1)S(1)}, u32[]{:S(2)}, u32[]{:S(2)}) async-start(bf16[8,64,256]{2,1,0:T(8,128)(2,1)} %broadcast_in_dim.11), calls=%async_computation.1 | async-start | bytes 524288 | tf_op jit(solution)/shard_map/all_to_all | solution.py:16
  50.8 67.3 %reduce-scatter.11.cloned.1.call-start = ((), (), s32[]{:S(2)}) async-start(), calls=%async_computation.15 | async-start | bytes 4128768 | tf_op jit(solution)/shard_map/reduce_scatter | solution.py:36
  57.9 5.5 %copy-start.2 = (bf16[2,128,14,128]{1,0,3,2:T(2,128)(2,1)}, bf16[2,128,14,128]{1,0,3,2:T(2,128)(2,1)S(1)}, u32[]{:S(2)}) copy-start(bf16[2,128,14,128]{1,0,3,2:T(2,128)(2,1)S(1)} %mul.164) | copy-start | bytes 2752516
  60.4 0.7 copy-start.13
  60.4 109.7 %reduce-scatter.7.cloned.1.call-start = ((), (), s32[]{:S(2)}) async-start(), calls=%async_computation.13 | async-start | bytes 4128768 | tf_op jit(solution)/shard_map/reduce_scatter | solution.py:36
  63.9 0.9 copy-start.4
  68.6 123.7 %reduce-scatter.17.cloned.1.call-start = ((), (), s32[]{:S(2)}) async-start(), calls=%async_computation.19 | async-start | bytes 286720 | tf_op jit(solution)/shard_map/reduce_scatter | solution.py:61
  69.2 149.8 %reduce-scatter.13.cloned.1.call-start = ((), (), s32[]{:S(2)}) async-start(), calls=%async_computation.16 | async-start | bytes 573440 | tf_op jit(solution)/shard_map/reduce_scatter | solution.py:36
  118.2 126.5 %reduce-scatter.9.cloned.1.call-start = ((), (), s32[]{:S(2)}) async-start(), calls=%async_computation.14 | async-start | bytes 573440 | tf_op jit(solution)/shard_map/reduce_scatter | solution.py:36
  170.1 126.9 %all-gather.3.cloned.1.call-start = ((), (), s32[]{:S(2)}) async-start(), calls=%async_computation.17 | async-start | bytes 2064384 | tf_op jit(solution)/shard_map/all_gather | solution.py:43
  256.3 123.5 %all-gather.5.cloned.1.call-start = ((), (), s32[]{:S(2)}) async-start(), calls=%async_computation.20 | async-start | bytes 3784704 | tf_op jit(solution)/shard_map/all_gather | solution.py:67
  297.0 3.9 copy-start.8
  303.7 15.1 %all-to-all-start.2 = ((bf16[8,64,256]{2,1,0:T(8,128)(2,1)}), bf16[8,64,256]{2,1,0:T(8,128)(2,1)S(1)}, u32[]{:S(2)}, u32[]{:S(2)}) async-start(bf16[8,64,256]{2,1,0:T(8,128)(2,1)} %bitcast.103), calls=%async_computation.6 | async-start | bytes 524288 | tf_op jit(solution)/shard_map/all_to_all | solution.py:54
  387.2 2.9 copy-start.1
  387.2 3.1 copy-start.3
  387.2 3.4 copy-start.5
  391.9 14.7 %all-to-all-start.4 = ((bf16[8,64,256]{2,1,0:T(8,128)(2,1)}), bf16[8,64,256]{2,1,0:T(8,128)(2,1)S(1)}, u32[]{:S(2)}, u32[]{:S(2)}) async-start(bf16[8,64,256]{2,1,0:T(8,128)(2,1)} %bitcast.5), calls=%async_computation.10 | async-start | bytes 524288 | tf_op jit(solution)/shard_map/all_to_all | solution.py:54
  402.5 9.2 %copy-start = (bf16[1792,512]{1,0:T(8,128)(2,1)S(1)}, bf16[1792,512]{1,0:T(8,128)(2,1)}, u32[]{:S(2)}) copy-start(bf16[1792,512]{1,0:T(8,128)(2,1)} %copy.67) | copy-start | bytes 5505028
  407.4 8.9 %all-to-all-start.6 = ((f32[8,1,256]{2,1,0:T(1,128)}), f32[8,1,256]{2,1,0:T(1,128)S(1)}, u32[]{:S(2)}, u32[]{:S(2)}) async-start(f32[8,1,256]{2,1,0:T(1,128)} %broadcast_in_dim.14), calls=%async_computation.12 | async-start | bytes 16384 | tf_op jit(solution)/shard_map/all_to_all | solution.py:16
  417.0 13.6 %all-to-all-start.5 = ((f32[32,1,64]{2,1,0:T(1,128)}), f32[32,1,64]{2,1,0:T(1,128)S(1)}, u32[]{:S(2)}, u32[]{:S(2)}) async-start(f32[32,1,64]{2,1,0:T(1,128)} %broadcast_in_dim.13), calls=%async_computation.11 | async-start | bytes 32768 | tf_op jit(solution)/shard_map/all_to_all | solution.py:16
  422.1 8.5 %copy-start.10 = (bf16[64,256]{1,0:T(8,128)(2,1)S(1)}, bf16[64,256]{1,0:T(8,128)(2,1)}, u32[]{:S(2)}) copy-start(bf16[64,256]{1,0:T(8,128)(2,1)} %param.17) | copy-start | bytes 98308
Sparse Core Ops, SparseCore 0:
  24.5 38.1 reduce-scatter.14
  65.2 52.8 reduce-scatter.10
  120.7 49.3 reduce-scatter.6
  172.5 19.8 reduce-scatter.16
  194.9 24.0 reduce-scatter.12
  221.4 23.2 reduce-scatter.8
  256.4 40.4 all-gather.2
  299.9 79.9 all-gather.4
where the time goes:
time: 439 us; the launch traced here: 438 us
  waiting for transfers between devices  300 us (68%)
  starting transfers between devices  38.9 us (9%)
  local copies, waits for them, and re-layouts  30.9 us (7%)
  blocking collectives  29.4 us (7%)
  matrix products  20.1 us (5%)
  between operations  14.3 us (3%)
    reduce_scatter x4, waiting for transfers between devices, scatter_axes(): shard = lax.psum_scatter(shard, axis, scatter_dimension=dim, tiled=True)  153 us
    all_gather x1, waiting for transfers between devices, side_by_side(): out, at, done = (lax.all_gather(both, axis, axis=dim, tiled=True), 0, [])  60.9 us
    all_gather x1, waiting for transfers between devices, gathered_by_axis(): out = lax.all_gather(out, axes[number], axis=dim, tiled=True)  38.8 us
    reduce_scatter x2, waiting for transfers between devices, sum_by_axis(): total = lax.psum_scatter(total, axis, scatter_dimension=0, tiled=True)  22.2 us
    all_to_all x4, starting transfers between devices, from_everyone(): return lax.all_to_all(copies, axis, split_axis=0, concat_axis=0, tiled=True)  21.8 us
    all_to_all x4, waiting for transfers between devices, from_everyone(): return lax.all_to_all(copies, axis, split_axis=0, concat_axis=0, tiled=True)  20.5 us
    all_to_all x1, blocking collectives, from_everyone(): return lax.all_to_all(copies, axis, split_axis=0, concat_axis=0, tiled=True)  18.8 us
    all_to_all x2, starting transfers between devices, sent_and_summed(): lax.all_to_all(in_blocks(shard, dim, count), axis, 0, 0, tiled=True)  16.9 us
  transfers between devices with their start and end apart: 14, of which 13 were waited for; matrix products, arithmetic and copies ran while one was open for 8% of the time, Pallas kernels for 0%

commit v1 on v0

v1 whole, which is shorter than its diff:
```python
import jax
import jax.numpy as jnp
from jax import lax
from jax.experimental import pallas as pl
from jax.experimental.pallas import tpu as pltpu
from jax.sharding import Mesh
from jax.sharding import PartitionSpec as P

D = 8192
BLK = 128
NZ, NX = 8, 4
COL = ("col_0", "col_1")
ALL = ("row", "col_0", "col_1")
norm_eps = 1e-05

f32 = jnp.float32
bf16 = jnp.bfloat16
VMEM_BYTES = 56 * 1024 * 1024


def vmem():
    return pl.BlockSpec(memory_space=pltpu.VMEM)


def smem():
    return pl.BlockSpec(memory_space=pltpu.SMEM)


def call(kernel, outs, in_specs, scratch, flops, nbytes, args):
    return pl.pallas_call(
        kernel,
        out_shape=outs,
        in_specs=in_specs,
        out_specs=tuple(vmem() for _ in outs),
        scratch_shapes=scratch,
        compiler_params=pltpu.CompilerParams(vmem_limit_bytes=VMEM_BYTES),
        cost_estimate=pl.CostEstimate(flops=flops, bytes_accessed=nbytes, transcendentals=0),
    )(*args)


def natural_row(pos, k, j):
    return pl.multiple_of(
        lax.rem(pos[0] + k, NZ) * (NX * 16) + lax.rem(pos[1] + j, NX) * 16, 16
    )


def nn(a, b):
    return jnp.dot(a, b, preferred_element_type=f32)


def nt(a, b):
    return lax.dot_general(a, b, (((1,), (1,)), ((), ())), preferred_element_type=f32)


def tn(a, b):
    return lax.dot_general(a, b, (((0,), (0,)), ((), ())), preferred_element_type=f32)


def partials_kernel(
    pos, mg, mu, md, rows, gain, wg, wu, wd, part_a, part_b, eff_g, eff_u, eff_d, la, lb
):
    for w, m, e in ((wg, mg, eff_g), (wu, mu, eff_u), (wd, md, eff_d)):
        for a in range(w.shape[0] // BLK):
            for b in range(w.shape[1] // BLK):
                r, c = slice(a * BLK, (a + 1) * BLK), slice(b * BLK, (b + 1) * BLK)
                e[r, c] = w[r, c] * m[a, b].astype(f32).astype(bf16)
    width = gain.shape[1]
    for k in range(NZ):
        for j in range(NX):
            at = pl.ds(natural_row(pos, k, j), 16)
            to_a = slice((j * NZ + k) * 16, (j * NZ + k) * 16 + 16)
            to_b = slice((k * NX + j) * 16, (k * NX + j) * 16 + 16)
            x = (rows[at, :width].astype(f32) * gain[...]).astype(bf16)
            g = rows[at, width:]
            la[to_a, :width] = x
            lb[to_b, :width] = x
            la[to_a, width:] = g
            lb[to_b, width:] = g
    half = wg.shape[1] // 2
    for left, part, at in ((lb, part_b, half), (la, part_a, 0)):
        cols = slice(at, at + half)
        for t in range(0, left.shape[0], 128):
            tok = slice(t, t + 128)
            x, g = left[tok, :width], left[tok, width:]
            part[tok, :half] = nn(x, eff_g[:, cols]).astype(bf16)
            part[tok, half : 2 * half] = nn(x, eff_u[:, cols]).astype(bf16)
            part[tok, 2 * half :] = nt(g, eff_d[cols, :]).astype(bf16)


def features_kernel(
    pos, rows, scale, ga, gb, eff_g, eff_u, eff_d, both, gain_part, da, na, db, nb
):
    half = ga.shape[1] // 3
    width = eff_g.shape[0]
    for hid, d, n, at in ((ga, da, na, 0), (gb, db, nb, half)):
        cols = slice(at, at + half)
        for t in range(0, hid.shape[0], 128):
            tok = slice(t, t + 128)
            d[tok, :] = nn(hid[tok, :half], eff_d[cols, :])
            n[tok, :] = nt(hid[tok, half : 2 * half], eff_g[:, cols]) + nt(
                hid[tok, 2 * half :], eff_u[:, cols]
            )
    total = jnp.zeros((16, width), f32)
    for k in range(NZ):
        for j in range(NX):
            at = pl.ds(natural_row(pos, k, j), 16)
            in_a = slice((j * NZ + k) * 16, (j * NZ + k) * 16 + 16)
            in_b = slice((k * NX + j) * 16, (k * NX + j) * 16 + 16)
            both[at, :width] = (da[in_a, :] + db[in_b, :]).astype(bf16)
            grad = na[in_a, :] + nb[in_b, :]
            both[at, width:] = grad.astype(bf16)
            total += grad * rows[at, :width].astype(f32) * scale[at, :]
    gain_part[...] = jnp.sum(total, axis=0, keepdims=True)


def weights_kernel(
    pos, mg, mu, md, rows, gain, scale, ga, gb, out_g, out_u, out_d, la, lb
):
    width = gain.shape[1]
    for k in range(NZ):
        for j in range(NX):
            at = pl.ds(natural_row(pos, k, j), 16)
            to_a = slice((j * NZ + k) * 16, (j * NZ + k) * 16 + 16)
            to_b = slice((k * NX + j) * 16, (k * NX + j) * 16 + 16)
            x = (rows[at, :width].astype(f32) * scale[at, :] * gain[...]).astype(bf16)
            g = rows[at, width:]
            la[to_a, :width] = x
            lb[to_b, :width] = x
            la[to_a, width:] = g
            lb[to_b, width:] = g
    half = ga.shape[1] // 3
    for hid, left, at in ((ga, la, 0), (gb, lb, half)):
        normed, grad = left[:, :width], left[:, width:]
        for c in range(0, half, BLK):
            b = (at + c) // BLK
            gw = tn(normed, hid[:, half + c : half + c + BLK])
            uw = tn(normed, hid[:, 2 * half + c : 2 * half + c + BLK])
            dw = tn(hid[:, c : c + BLK], grad)
            to = slice(at + c, at + c + BLK)
            for a in range(width // BLK):
                r = slice(a * BLK, (a + 1) * BLK)
                out_g[r, to] = (gw[r, :] * mg[a, b].astype(f32)).astype(bf16)
                out_u[r, to] = (uw[r, :] * mu[a, b].astype(f32)).astype(bf16)
                out_d[to, r] = (dw[:, r] * md[b, a].astype(f32)).astype(bf16)


def send(v, axis, step):
    n = lax.axis_size(axis)
    return lax.ppermute(v, axis, [(i, (i + step) % n) for i in range(n)])


def up32(v):
    return v.astype(f32)


def add_top(piece, got, h):
    return jnp.concatenate([(up32(piece[:h]) + up32(got)).astype(bf16), piece[h:].astype(bf16)])


def add_bottom(piece, got, h):
    return jnp.concatenate([piece[:h].astype(bf16), (up32(piece[h:]) + up32(got)).astype(bf16)])


def plus(piece, got):
    return (up32(piece) + up32(got)).astype(bf16)


def reduce_ring(pieces, axis):
    n = len(pieces)
    far = pieces[n // 2].astype(bf16)
    h = far.shape[0] // 2
    right, left = send(far[:h], axis, 1), send(far[h:], axis, -1)
    for away in range(n // 2 - 1, 0, -1):
        to_right, to_left = pieces[away], pieces[n - away]
        if away == n // 2 - 1:
            right = send(add_top(to_right, right, h), axis, 1)
            left = send(add_bottom(to_left, left, h), axis, -1)
        else:
            right = send(plus(to_right, right), axis, 1)
            left = send(plus(to_left, left), axis, -1)
    return up32(pieces[0]) + up32(right) + up32(left)


def gather_ring(shard, axis):
    n = lax.axis_size(axis)
    h = shard.shape[0] // 2
    pieces = [None] * n
    pieces[0] = shard
    right = left = shard
    for away in range(1, n // 2):
        right, left = send(right, axis, 1), send(left, axis, -1)
        pieces[n - away], pieces[away] = right, left
    pieces[n // 2] = jnp.concatenate([send(right[:h], axis, 1), send(left[h:], axis, -1)])
    return jnp.concatenate(pieces)


def cut(v, n):
    m = v.shape[0] // n
    return [v[i * m : (i + 1) * m] for i in range(n)]


def hidden_grads(sums, scale):
    half = sums.shape[1] // 3
    gate, up = sums[:, :half] * scale, sums[:, half : 2 * half] * scale
    act_grad = sums[:, 2 * half :]
    sig = jax.nn.sigmoid(gate)
    act = (gate * sig * up).astype(bf16)
    gate_grad = (act_grad * up * sig * (1.0 + gate * (1.0 - sig))).astype(bf16)
    up_grad = (act_grad * gate * sig).astype(bf16)
    dots = jnp.sum(up32(gate_grad) * gate + up32(up_grad) * up, axis=1)
    return jnp.concatenate([act, gate_grad, up_grad], axis=1), dots


def from_everyone(shard, axis):
    copies = jnp.broadcast_to(shard, (lax.axis_size(axis), *shard.shape))
    return lax.all_to_all(copies, axis, split_axis=0, concat_axis=0, tiled=True)


def shards(layer_input, norm_gain, w_gate, w_up, w_down, mask_gate, mask_up, mask_down, out_grad):
    row, z, x = (lax.axis_index(a) for a in ALL)
    pos = jnp.stack([z, x]).astype(jnp.int32)
    gain = norm_gain[None, :]
    mine, width = layer_input.shape
    hidden = w_gate.shape[1]
    rows = from_everyone(jnp.concatenate([layer_input, out_grad], axis=1), "row")
    rows = rows.reshape(-1, 2 * width)
    tokens = rows.shape[0]
    wide = 3 * hidden // 2
    part = jax.ShapeDtypeStruct((tokens, wide), bf16)
    dots_flops = 2 * tokens * width * hidden * 3
    part_a, part_b, eff_gate, eff_up, eff_down = call(
        partials_kernel,
        (
            part,
            part,
            jax.ShapeDtypeStruct(w_gate.shape, bf16),
            jax.ShapeDtypeStruct(w_up.shape, bf16),
            jax.ShapeDtypeStruct(w_down.shape, bf16),
        ),
        [smem()] * 4 + [vmem()] * 5,
        [pltpu.VMEM((tokens, 2 * width), bf16)] * 2,
        dots_flops,
        12_000_000,
        (pos, mask_gate, mask_up, mask_down, rows, gain, w_gate, w_up, w_down),
    )
    squares = jnp.sum(jnp.square(up32(rows[:, :width])), axis=1)
    scale_all = lax.rsqrt(lax.psum(squares, COL) / D + norm_eps)[:, None]

    sums_b = reduce_ring(cut(reduce_ring(cut(part_b, NZ), "col_0"), NX), "col_1")
    sums_a = reduce_ring(cut(reduce_ring(cut(part_a, NX), "col_1"), NZ), "col_0")
    own = z * (NX * 16) + x * 16
    scale_own = lax.dynamic_slice_in_dim(scale_all, own, 16, 0)
    hid_a, dots_a = hidden_grads(sums_a, scale_own)
    hid_b, dots_b = hidden_grads(sums_b, scale_own)
    dots_all = lax.psum(
        lax.dynamic_update_slice_in_dim(jnp.zeros((tokens,), f32), dots_a + dots_b, own, 0), ALL
    )
    all_a = gather_ring(gather_ring(hid_a, "col_0"), "col_1")
    all_b = gather_ring(gather_ring(hid_b, "col_1"), "col_0")

    both, gain_part = call(
        features_kernel,
        (
            jax.ShapeDtypeStruct((tokens, 2 * width), bf16),
            jax.ShapeDtypeStruct((1, width), f32),
        ),
        [smem()] + [vmem()] * 7,
        [pltpu.VMEM((tokens, width), f32)] * 4,
        dots_flops,
        12_000_000,
        (pos, rows, scale_all, all_a, all_b, eff_gate, eff_up, eff_down),
    )
    got = lax.all_to_all(both.reshape(-1, mine, 2 * width), "row", 0, 0, tiled=True)
    gain_grad = jnp.sum(from_everyone(gain_part, "row"), axis=(0, 1))
    gate_wgrad, up_wgrad, down_wgrad = call(
        weights_kernel,
        (
            jax.ShapeDtypeStruct(w_gate.shape, bf16),
            jax.ShapeDtypeStruct(w_up.shape, bf16),
            jax.ShapeDtypeStruct(w_down.shape, bf16),
        ),
        [smem()] * 4 + [vmem()] * 5,
        [pltpu.VMEM((tokens, 2 * width), bf16)] * 2,
        dots_flops,
        12_000_000,
        (pos, mask_gate, mask_up, mask_down, rows, gain, scale_all, all_a, all_b),
    )
    got = jnp.sum(up32(got), axis=0)
    x_float = up32(layer_input)
    layer_out = (x_float + got[:, :width]).astype(bf16)
    scale = lax.dynamic_slice_in_dim(scale_all, row * mine, mine, 0)
    dots = lax.dynamic_slice_in_dim(dots_all, row * mine, mine, 0)[:, None]
    input_grad = (
        up32(out_grad) + scale * gain * got[:, width:] - x_float * scale * scale * dots / D
    ).astype(bf16)
    return (layer_out, input_grad, gain_grad, gate_wgrad, up_wgrad, down_wgrad)


def solution(mesh):
    torus = Mesh(mesh.devices.reshape(mesh.shape["row"], NZ, NX), ALL)
    placed = (
        P("row", COL),
        P(COL),
        P(COL, "row"),
        P(COL, "row"),
        P("row", COL),
        P(COL, "row"),
        P(COL, "row"),
        P("row", COL),
        P("row", COL),
    )
    return jax.shard_map(
        shards,
        mesh=torus,
        in_specs=placed,
        out_specs=(
            P("row", COL),
            P("row", COL),
            P(COL),
            P(COL, "row"),
            P(COL, "row"),
            P("row", COL),
        ),
        check_vma=False,
    )
```

time: 439 us -> 360 us (0.82)
  waiting for transfers between devices: 300 us -> 46.2 us
  blocking collectives: 29.4 us -> 173 us
  starting transfers between devices: 38.9 us -> 83.3 us
  Pallas kernels: 0 us -> 21.8 us
  matrix products: 20.1 us -> 0 us
  between operations: 14.3 us -> 1.31 us
  local copies, waits for them, and re-layouts: 30.9 us -> 18.5 us
  other arithmetic: 4.19 us -> 11.3 us
    reduce_scatter x6 -> x0, waiting for transfers between devices: 175 us -> none  [the longest x4 153 us: scatter_axes(): shard = lax.psum_scatter(shard, axis, scatter_dimension=dim, tiled=True)]
    psum x0 -> x2, blocking collectives: none -> 137 us  [the longest x1 78.3 us: shards(): lax.psum(lax.dynamic_update_slice_in_dim(jnp.zeros((tokens,), f32), dots_...]
    all_gather x2 -> x0, waiting for transfers between devices: 99.7 us -> none  [the longest x1 60.9 us: side_by_side(): out, at, done = (lax.all_gather(both, axis, axis=dim, tiled=True), 0, [])]
    ppermute x0 -> x48, starting transfers between devices: none -> 72.5 us  [send(): return lax.ppermute(v, axis, [(i, (i + step) % n) for i in range(n)])]
    ppermute x0 -> x48, waiting for transfers between devices: none -> 38.7 us  [send(): return lax.ppermute(v, axis, [(i, (i + step) % n) for i in range(n)])]
    pallas_call x0 -> x3, Pallas kernels: none -> 21.8 us  [call(): pl.pallas_call(kernel, out_shape=outs, in_specs=in_specs, out_specs=tuple...]
    dot_general x9 -> x0, matrix products: 20.1 us -> none  [the longest x3 5.88 us: contract_cols(): lax.dot_general(left, right, (((1,), (1,)), ((), ())), preferred_element_...]
    all_to_all x1, blocking collectives: 18.8 us -> 36.1 us  [from_everyone(): return lax.all_to_all(copies, axis, split_axis=0, concat_axis=0, tiled=True)]
  transfers between devices with their start and end apart: 14 -> 50, of which waited for: 13 -> 15; matrix products, arithmetic and copies ran while one was open for 8% -> 6% of each run, Pallas kernels for 0% -> 2%
where the time goes in v1:
time: 360 us; the launch traced here: 355 us
  blocking collectives  173 us (48%)
  starting transfers between devices  83.3 us (23%)
  waiting for transfers between devices  46.2 us (13%)
  Pallas kernels  21.8 us (6%)
  local copies, waits for them, and re-layouts  18.5 us (5%)
  other arithmetic  11.3 us (3%)
    psum x1, blocking collectives, shards(): lax.psum(lax.dynamic_update_slice_in_dim(jnp.zeros((tokens,), f32), dots_...  78.3 us
    ppermute x48, starting transfers between devices, send(): return lax.ppermute(v, axis, [(i, (i + step) % n) for i in range(n)])  72.5 us
    psum x1, blocking collectives, shards(): scale_all = lax.rsqrt(lax.psum(squares, COL) / D + norm_eps)[:, None]  58.5 us
    ppermute x48, waiting for transfers between devices, send(): return lax.ppermute(v, axis, [(i, (i + step) % n) for i in range(n)])  38.7 us
    all_to_all x1, blocking collectives, from_everyone(): return lax.all_to_all(copies, axis, split_axis=0, concat_axis=0, tiled=True)  36.1 us
    pallas_call x3, Pallas kernels, call(): pl.pallas_call(kernel, out_shape=outs, in_specs=in_specs, out_specs=tuple...  21.8 us
    unnamed x39, local copies, waits for them, and re-layouts  11.1 us
    all_to_all x1, waiting for transfers between devices, from_everyone(): return lax.all_to_all(copies, axis, split_axis=0, concat_axis=0, tiled=True)  7.51 us
  transfers between devices with their start and end apart: 50, of which 15 were waited for; matrix products, arithmetic and copies ran while one was open for 6% of the time, Pallas kernels for 2%

profile of v1, /device:TPU:1, one launch (start us, length us, event | category | flops | bytes accessed | tf_op | source)
XLA Modules:
  0.0 355.4 jit_solution(16688943874193712734)
XLA Ops:
  2.2 6.6 %all-to-all-start = ((bf16[8,64,512]{2,1,0:T(8,128)(2,1)}), bf16[8,64,512]{2,1,0:T(8,128)(2,1)S(1)}, u32[]{:S(2)}, u32[]{:S(2)}) async-start(bf16[8,64,512]{2,1,0:T(8,128)(2,1)} %broadcast_in_dim.16), calls=%async_computation | async-start | bytes 1048576 | tf_op jit(solution)/shard_map/all_to_all | solution.py:216
  10.9 7.5 %all-to-all-done = bf16[8,64,512]{2,1,0:T(8,128)(2,1)S(1)} async-done(((bf16[8,64,512]{2,1,0:T(8,128)(2,1)}), bf16[8,64,512]{2,1,0:T(8,128)(2,1)S(1)}, u32[]{:S(2)}, u32[]{:S(2)}) %all-to-all-start) | async-done | bytes 524320 | tf_op jit(solution)/shard_map/all_to_all | solution.py:216
  19.2 7.6 %shard_map.136 = (bf16[512,2688]{1,0:T(8,128)(2,1)}, bf16[512,2688]{1,0:T(8,128)(2,1)}, bf16[256,1792]{1,0:T(8,128)(2,1)}, bf16[256,1792]{1,0:T(8,128)(2,1)}, bf16[1792,256]{1,0:T(8,128)(2,1)}) custom-call(s32[2]{0:T(128)} %pad_add_fusion.pos, s32[2,14]{1,0:T(2,128)} %mg.3, s32[2,14]{1,0:T(2,128)} %mu.3, s32[14,2]{1,0:T(8,128)} %copy.25.md, ...), custom_call_target="tpu_custom_call" | custom-call | flops 1409286144 | bytes 12000000 | tf_op jit(solution)/shard_map/pallas_call | solution.py:30
  26.8 2.4 fusion.19
  29.7 2.1 collective-permute-start.2
  33.7 3.9 %collective-permute-start.28 = (bf16[32,2688]{1,0:T(8,128)(2,1)}, bf16[32,2688]{1,0:T(8,128)(2,1)}, u32[]{:S(2)}, u32[]{:S(2)}) collective-permute-start(bf16[32,2688]{1,0:T(8,128)(2,1)} %get-tuple-element.47), channel_id=1, source_target_pairs={{0,28},{4,0},{8,4},{12,8},{16,12},{20,16},{24,20},{28,24},{1,29},{... | collective-permute-start | bytes 516104 | tf_op jit(solution)/shard_map/ppermute | solution.py:149
  37.7 58.5 %psum.14 = f32[512]{0:T(512)S(1)} all-reduce(f32[512]{0:T(512)S(1)} %multiply_reduce_fusion), channel_id=1, replica_groups=mesh['row'=8,'col_0'=8,'col_1'=4] {'col_0','col_1'}, use_global_device_ids=true, to_apply=%region_1.0 | all-reduce | flops 512 | bytes 4096 | tf_op jit(solution)/shard_map/psum | solution.py:247
  99.4 2.7 collective-permute-start.29
  103.8 2.7 collective-permute-start.3
  106.7 8.0 %collective-permute-done.1 = bf16[128,2688]{1,0:T(8,128)(2,1)S(1)} collective-permute-done((bf16[128,2688]{1,0:T(8,128)(2,1)S(1)}, bf16[128,2688]{1,0:T(8,128)(2,1)S(1)}, u32[]{:S(2)}, u32[]{:S(2)}) %collective-permute-start.1) | collective-permute-done | bytes 688160 | tf_op jit(solution)/shard_map/ppermute | solution.py:149
  116.3 3.0 collective-permute-start.8
  121.3 3.0 collective-permute-start.9
  124.3 3.8 %collective-permute-done.5 = bf16[16,2688]{1,0:T(8,128)(2,1)S(1)} collective-permute-done((bf16[16,2688]{1,0:T(8,128)(2,1)S(1)}, bf16[16,2688]{1,0:T(8,128)(2,1)S(1)}, u32[]{:S(2)}, u32[]{:S(2)}) %collective-permute-start.5) | collective-permute-done | bytes 86048 | tf_op jit(solution)/shard_map/ppermute | solution.py:149
  136.3 5.7 %collective-permute-start.34 = (bf16[8,2688]{1,0:T(8,128)(2,1)S(1)}, bf16[8,2688]{1,0:T(8,128)(2,1)S(1)}, u32[]{:S(2)}, u32[]{:S(2)}) collective-permute-start(bf16[8,2688]{1,0:T(8,128)(2,1)S(1)} %get-tuple-element.61), channel_id=1, source_target_pairs={{0,3},{1,0},{2,1},{3,2},{4,7},{5,4},{6,5},{7,6},{8,11},{9,8},{10,9... | collective-permute-start | bytes 129032 | tf_op jit(solution)/shard_map/ppermute | solution.py:149
  142.1 2.8 collective-permute-start.11
  145.1 2.7 collective-permute-start.35
  150.6 2.7 collective-permute-start.36
  153.2 8.6 %collective-permute-start.37 = (bf16[16,2688]{1,0:T(8,128)(2,1)S(1)}, bf16[16,2688]{1,0:T(8,128)(2,1)S(1)}, u32[]{:S(2)}, u32[]{:S(2)}) collective-permute-start(bf16[16,2688]{1,0:T(8,128)(2,1)S(1)} %get-tuple-element.74), channel_id=1, source_target_pairs={{0,1},{1,2},{2,3},{3,0},{4,5},{5,6},{6,7},{7,4},{8,9},{9,10},{10,1... | collective-permute-start | bytes 258056 | tf_op jit(solution)/shard_map/ppermute | solution.py:149
  166.4 2.7 collective-permute-start.39
  174.1 2.7 collective-permute-start.40
  176.8 2.7 collective-permute-start.14
  180.2 5.1 %collective-permute-done.17 = bf16[16,2688]{1,0:T(8,128)(2,1)S(1)} collective-permute-done((bf16[16,2688]{1,0:T(8,128)(2,1)S(1)}, bf16[16,2688]{1,0:T(8,128)(2,1)S(1)}, u32[]{:S(2)}, u32[]{:S(2)}) %collective-permute-start.17) | collective-permute-done | bytes 86048 | tf_op jit(solution)/shard_map/ppermute | solution.py:149
  185.3 2.7 collective-permute-start.19
  196.6 6.5 %collective-permute-done.41 = bf16[64,2688]{1,0:T(8,128)(2,1)S(1)} collective-permute-done((bf16[64,2688]{1,0:T(8,128)(2,1)S(1)}, bf16[64,2688]{1,0:T(8,128)(2,1)S(1)}, u32[]{:S(2)}, u32[]{:S(2)}) %collective-permute-start.41) | collective-permute-done | bytes 344096 | tf_op jit(solution)/shard_map/ppermute | solution.py:149
  208.4 3.6 %collective-permute-done.45 = bf16[64,2688]{1,0:T(8,128)(2,1)S(1)} collective-permute-done((bf16[64,2688]{1,0:T(8,128)(2,1)S(1)}, bf16[64,2688]{1,0:T(8,128)(2,1)S(1)}, u32[]{:S(2)}, u32[]{:S(2)}) %collective-permute-start.45) | collective-permute-done | bytes 344096 | tf_op jit(solution)/shard_map/ppermute | solution.py:149
  212.2 2.7 collective-permute-start.47
  214.9 2.7 collective-permute-done.46
  220.1 7.1 %shard_map.137 = (bf16[512,512]{1,0:T(8,128)(2,1)}, f32[1,256]{1,0:T(1,128)}) custom-call(s32[2]{0:T(128)} %pad_add_fusion.pos, bf16[512,512]{1,0:T(8,128)(2,1)} %bitcast.9, f32[512,1]{1,0:T(8,128)} %copy.26.scale, bf16[512,2688]{1,0:T(8,128)(2,1)} %copy-done.2, bf16[512,2688]{1,0:T(8,128)(2,1)} %copy-done, bf16[256,1792]{1,0:T(8,128)(2,1)} %get-tuple-element.18.eff_g, ...), custom_call_target="tpu_custom_call" | custom-call | flops 1409286144 | bytes 12000000 | tf_op jit(solution)/shard_map/pallas_call | solution.py:30
  227.9 36.1 %all_to_all.15 = f32[8,1,256]{2,1,0:T(1,128)S(1)} all-to-all(f32[8,1,256]{2,1,0:T(1,128)S(1)} %broadcast_in_dim.20), channel_id=1, replica_groups=mesh['row'=8,'col_0'=8,'col_1'=4] {'row'}, dimensions={0} | all-to-all | bytes 16384 | tf_op jit(solution)/shard_map/all_to_all | solution.py:216
  264.1 4.1 %all-to-all-start.1 = ((bf16[8,64,512]{2,1,0:T(8,128)(2,1)}), bf16[8,64,512]{2,1,0:T(8,128)(2,1)S(1)}, u32[]{:S(2)}, u32[]{:S(2)}) async-start(bf16[8,64,512]{2,1,0:T(8,128)(2,1)} %bitcast.11), calls=%async_computation.1 | async-start | bytes 1048576 | tf_op jit(solution)/shard_map/all_to_all | solution.py:273
  268.3 78.3 %psum.15 = f32[512]{0:T(512)S(1)} all-reduce(f32[512]{0:T(512)S(1)} %add_dynamic-update-slice_fusion), channel_id=1, replica_groups=mesh['row'=8,'col_0'=8,'col_1'=4] {'row','col_0','col_1'}, use_global_device_ids=true, to_apply=%region_5.0 | all-reduce | flops 512 | bytes 4096 | tf_op jit(solution)/shard_map/psum | solution.py:255
  346.7 7.1 %shard_map.138 = (bf16[256,1792]{1,0:T(8,128)(2,1)}, bf16[256,1792]{1,0:T(8,128)(2,1)}, bf16[1792,256]{1,0:T(8,128)(2,1)}) custom-call(s32[2]{0:T(128)} %pad_add_fusion.pos, s32[2,14]{1,0:T(2,128)} %mg.3, s32[2,14]{1,0:T(2,128)} %mu.3, s32[14,2]{1,0:T(8,128)} %copy.25.md, bf16[512,512]{1,0:T(8,128)(2,1)} %bitcast.10, f32[1,256]{1,0:T(1,128)} %bitcast.14, ...), custom_call_target="tpu_custom_call" | custom-call | flops 1409286144 | bytes 12000000 | tf_op jit(solution)/shard_map/pallas_call | solution.py:30
  (169 shorter events, 55.3 us)
Async XLA Ops:
  2.2 16.1 %all-to-all-start = ((bf16[8,64,512]{2,1,0:T(8,128)(2,1)}), bf16[8,64,512]{2,1,0:T(8,128)(2,1)S(1)}, u32[]{:S(2)}, u32[]{:S(2)}) async-start(bf16[8,64,512]{2,1,0:T(8,128)(2,1)} %broadcast_in_dim.16), calls=%async_computation | async-start | bytes 1048576 | tf_op jit(solution)/shard_map/all_to_all | solution.py:216
  29.2 72.9 %collective-permute-start = (bf16[64,2688]{1,0:T(8,128)(2,1)}, bf16[64,2688]{1,0:T(8,128)(2,1)}, u32[]{:S(2)}, u32[]{:S(2)}) collective-permute-start(bf16[64,2688]{1,0:T(8,128)(2,1)} %get-tuple-element.38), channel_id=1, source_target_pairs={{0,1},{1,2},{2,3},{3,0},{4,5},{5,6},{6,7},{7,4},{8,9},{9,10},{10,1... | collective-permute-start | bytes 1032200 | tf_op jit(solution)/shard_map/ppermute | solution.py:149
  29.7 72.4 %collective-permute-start.2 = (bf16[64,2688]{1,0:T(8,128)(2,1)}, bf16[64,2688]{1,0:T(8,128)(2,1)}, u32[]{:S(2)}, u32[]{:S(2)}) collective-permute-start(bf16[64,2688]{1,0:T(8,128)(2,1)} %get-tuple-element.39), channel_id=1, source_target_pairs={{0,3},{1,0},{2,1},{3,2},{4,7},{5,4},{6,5},{7,6},{8,11},{9,8},{10,9... | collective-permute-start | bytes 1032200 | tf_op jit(solution)/shard_map/ppermute | solution.py:149
  32.8 63.5 %collective-permute-start.24 = (bf16[32,2688]{1,0:T(8,128)(2,1)}, bf16[32,2688]{1,0:T(8,128)(2,1)}, u32[]{:S(2)}, u32[]{:S(2)}) collective-permute-start(bf16[32,2688]{1,0:T(8,128)(2,1)} %get-tuple-element.46), channel_id=1, source_target_pairs={{0,4},{4,8},{8,12},{12,16},{16,20},{20,24},{24,28},{28,0},{1,5},{5... | collective-permute-start | bytes 516104 | tf_op jit(solution)/shard_map/ppermute | solution.py:149
  33.7 62.6 %collective-permute-start.28 = (bf16[32,2688]{1,0:T(8,128)(2,1)}, bf16[32,2688]{1,0:T(8,128)(2,1)}, u32[]{:S(2)}, u32[]{:S(2)}) collective-permute-start(bf16[32,2688]{1,0:T(8,128)(2,1)} %get-tuple-element.47), channel_id=1, source_target_pairs={{0,28},{4,0},{8,4},{12,8},{16,12},{20,16},{24,20},{28,24},{1,29},{... | collective-permute-start | bytes 516104 | tf_op jit(solution)/shard_map/ppermute | solution.py:149
  98.3 8.2 %collective-permute-start.25 = (bf16[64,2688]{1,0:T(8,128)(2,1)S(1)}, bf16[64,2688]{1,0:T(8,128)(2,1)S(1)}, u32[]{:S(2)}, u32[]{:S(2)}) collective-permute-start(bf16[64,2688]{1,0:T(8,128)(2,1)S(1)} %pad_maximum_fusion.2), channel_id=1, source_target_pairs={{0,4},{4,8},{8,12},{12,16},{16,20},{20,24},{24,28},{28,0},{1,5},{5... | collective-permute-start | bytes 1032200 | tf_op jit(solution)/shard_map/ppermute | solution.py:149
  99.4 19.9 %collective-permute-start.29 = (bf16[64,2688]{1,0:T(8,128)(2,1)S(1)}, bf16[64,2688]{1,0:T(8,128)(2,1)S(1)}, u32[]{:S(2)}, u32[]{:S(2)}) collective-permute-start(bf16[64,2688]{1,0:T(8,128)(2,1)S(1)} %pad_maximum_fusion.3), channel_id=1, source_target_pairs={{0,28},{4,0},{8,4},{12,8},{16,12},{20,16},{24,20},{28,24},{1,29},{... | collective-permute-start | bytes 1032200 | tf_op jit(solution)/shard_map/ppermute | solution.py:149
  103.6 11.1 %collective-permute-start.1 = (bf16[128,2688]{1,0:T(8,128)(2,1)S(1)}, bf16[128,2688]{1,0:T(8,128)(2,1)S(1)}, u32[]{:S(2)}, u32[]{:S(2)}) collective-permute-start(bf16[128,2688]{1,0:T(8,128)(2,1)S(1)} %pad_maximum_fusion), channel_id=1, source_target_pairs={{0,1},{1,2},{2,3},{3,0},{4,5},{5,6},{6,7},{7,4},{8,9},{9,10},{10,1... | collective-permute-start | bytes 2064392 | tf_op jit(solution)/shard_map/ppermute | solution.py:149
  103.8 11.0 %collective-permute-start.3 = (bf16[128,2688]{1,0:T(8,128)(2,1)S(1)}, bf16[128,2688]{1,0:T(8,128)(2,1)S(1)}, u32[]{:S(2)}, u32[]{:S(2)}) collective-permute-start(bf16[128,2688]{1,0:T(8,128)(2,1)S(1)} %pad_maximum_fusion.1), channel_id=1, source_target_pairs={{0,3},{1,0},{2,1},{3,2},{4,7},{5,4},{6,5},{7,6},{8,11},{9,8},{10,9... | collective-permute-start | bytes 2064392 | tf_op jit(solution)/shard_map/ppermute | solution.py:149
  106.6 12.6 %collective-permute-start.26 = (bf16[64,2688]{1,0:T(8,128)(2,1)S(1)}, bf16[64,2688]{1,0:T(8,128)(2,1)S(1)}, u32[]{:S(2)}, u32[]{:S(2)}) collective-permute-start(bf16[64,2688]{1,0:T(8,128)(2,1)S(1)} %add_convert_fusion.3), channel_id=1, source_target_pairs={{0,4},{4,8},{8,12},{12,16},{16,20},{20,24},{24,28},{28,0},{1,5},{5... | collective-permute-start | bytes 1032200 | tf_op jit(solution)/shard_map/ppermute | solution.py:149
  119.4 10.3 %collective-permute-start.30 = (bf16[64,2688]{1,0:T(8,128)(2,1)S(1)}, bf16[64,2688]{1,0:T(8,128)(2,1)S(1)}, u32[]{:S(2)}, u32[]{:S(2)}) collective-permute-start(bf16[64,2688]{1,0:T(8,128)(2,1)S(1)} %get-tuple-element.43), channel_id=1, source_target_pairs={{0,28},{4,0},{8,4},{12,8},{16,12},{20,16},{24,20},{28,24},{1,29},{... | collective-permute-start | bytes 1032200 | tf_op jit(solution)/shard_map/ppermute | solution.py:149
  119.5 14.8 %collective-permute-start.27 = (bf16[64,2688]{1,0:T(8,128)(2,1)S(1)}, bf16[64,2688]{1,0:T(8,128)(2,1)S(1)}, u32[]{:S(2)}, u32[]{:S(2)}) collective-permute-start(bf16[64,2688]{1,0:T(8,128)(2,1)S(1)} %get-tuple-element.42), channel_id=1, source_target_pairs={{0,4},{4,8},{8,12},{12,16},{16,20},{20,24},{24,28},{28,0},{1,5},{5... | collective-permute-start | bytes 1032200 | tf_op jit(solution)/shard_map/ppermute | solution.py:149
  121.3 9.8 %collective-permute-start.9 = (bf16[16,2688]{1,0:T(8,128)(2,1)S(1)}, bf16[16,2688]{1,0:T(8,128)(2,1)S(1)}, u32[]{:S(2)}, u32[]{:S(2)}) collective-permute-start(bf16[16,2688]{1,0:T(8,128)(2,1)S(1)} %pad_maximum_fusion.5), channel_id=1, source_target_pairs={{0,28},{4,0},{8,4},{12,8},{16,12},{20,16},{24,20},{28,24},{1,29},{... | collective-permute-start | bytes 258056 | tf_op jit(solution)/shard_map/ppermute | solution.py:149
  132.8 9.2 %collective-permute-start.10 = (bf16[16,2688]{1,0:T(8,128)(2,1)S(1)}, bf16[16,2688]{1,0:T(8,128)(2,1)S(1)}, u32[]{:S(2)}, u32[]{:S(2)}) collective-permute-start(bf16[16,2688]{1,0:T(8,128)(2,1)S(1)} %get-tuple-element.51), channel_id=1, source_target_pairs={{0,28},{4,0},{8,4},{12,8},{16,12},{20,16},{24,20},{28,24},{1,29},{... | collective-permute-start | bytes 258056 | tf_op jit(solution)/shard_map/ppermute | solution.py:149
  133.4 14.3 %collective-permute-start.7 = (bf16[16,2688]{1,0:T(8,128)(2,1)S(1)}, bf16[16,2688]{1,0:T(8,128)(2,1)S(1)}, u32[]{:S(2)}, u32[]{:S(2)}) collective-permute-start(bf16[16,2688]{1,0:T(8,128)(2,1)S(1)} %get-tuple-element.50), channel_id=1, source_target_pairs={{0,4},{4,8},{8,12},{12,16},{16,20},{20,24},{24,28},{28,0},{1,5},{5... | collective-permute-start | bytes 258056 | tf_op jit(solution)/shard_map/ppermute | solution.py:149
  136.2 8.7 %collective-permute-start.32 = (bf16[8,2688]{1,0:T(8,128)(2,1)S(1)}, bf16[8,2688]{1,0:T(8,128)(2,1)S(1)}, u32[]{:S(2)}, u32[]{:S(2)}) collective-permute-start(bf16[8,2688]{1,0:T(8,128)(2,1)S(1)} %get-tuple-element.60), channel_id=1, source_target_pairs={{0,1},{1,2},{2,3},{3,0},{4,5},{5,6},{6,7},{7,4},{8,9},{9,10},{10,1... | collective-permute-start | bytes 129032 | tf_op jit(solution)/shard_map/ppermute | solution.py:149
  136.3 8.6 %collective-permute-start.34 = (bf16[8,2688]{1,0:T(8,128)(2,1)S(1)}, bf16[8,2688]{1,0:T(8,128)(2,1)S(1)}, u32[]{:S(2)}, u32[]{:S(2)}) collective-permute-start(bf16[8,2688]{1,0:T(8,128)(2,1)S(1)} %get-tuple-element.61), channel_id=1, source_target_pairs={{0,3},{1,0},{2,1},{3,2},{4,7},{5,4},{6,5},{7,6},{8,11},{9,8},{10,9... | collective-permute-start | bytes 129032 | tf_op jit(solution)/shard_map/ppermute | solution.py:149
  150.6 15.8 %collective-permute-start.36 = (bf16[16,2688]{1,0:T(8,128)(2,1)S(1)}, bf16[16,2688]{1,0:T(8,128)(2,1)S(1)}, u32[]{:S(2)}, u32[]{:S(2)}) collective-permute-start(bf16[16,2688]{1,0:T(8,128)(2,1)S(1)} %get-tuple-element.74), channel_id=1, source_target_pairs={{0,3},{1,0},{2,1},{3,2},{4,7},{5,4},{6,5},{7,6},{8,11},{9,8},{10,9... | collective-permute-start | bytes 258056 | tf_op jit(solution)/shard_map/ppermute | solution.py:149
  153.2 13.2 %collective-permute-start.37 = (bf16[16,2688]{1,0:T(8,128)(2,1)S(1)}, bf16[16,2688]{1,0:T(8,128)(2,1)S(1)}, u32[]{:S(2)}, u32[]{:S(2)}) collective-permute-start(bf16[16,2688]{1,0:T(8,128)(2,1)S(1)} %get-tuple-element.74), channel_id=1, source_target_pairs={{0,1},{1,2},{2,3},{3,0},{4,5},{5,6},{6,7},{7,4},{8,9},{9,10},{10,1... | collective-permute-start | bytes 258056 | tf_op jit(solution)/shard_map/ppermute | solution.py:149
  170.9 8.6 %collective-permute-start.16 = (bf16[16,2688]{1,0:T(8,128)(2,1)S(1)}, bf16[16,2688]{1,0:T(8,128)(2,1)S(1)}, u32[]{:S(2)}, u32[]{:S(2)}) collective-permute-start(bf16[16,2688]{1,0:T(8,128)(2,1)S(1)} %collective-permute-done.15), channel_id=1, source_target_pairs={{0,4},{4,8},{8,12},{12,16},{16,20},{20,24},{24,28},{28,0},{1,5},{5... | collective-permute-start | bytes 258056 | tf_op jit(solution)/shard_map/ppermute | solution.py:149
  174.1 20.8 %collective-permute-start.40 = (bf16[64,2688]{1,0:T(8,128)(2,1)}, bf16[64,2688]{1,0:T(8,128)(2,1)S(1)}, u32[]{:S(2)}, u32[]{:S(2)}) collective-permute-start(bf16[64,2688]{1,0:T(8,128)(2,1)} %get-tuple-element.68), channel_id=1, source_target_pairs={{0,28},{4,0},{8,4},{12,8},{16,12},{20,16},{24,20},{28,24},{1,29},{... | collective-permute-start | bytes 1032200 | tf_op jit(solution)/shard_map/ppermute | solution.py:149
  176.8 19.5 %collective-permute-start.43 = (bf16[64,2688]{1,0:T(8,128)(2,1)}, bf16[64,2688]{1,0:T(8,128)(2,1)S(1)}, u32[]{:S(2)}, u32[]{:S(2)}) collective-permute-start(bf16[64,2688]{1,0:T(8,128)(2,1)} %get-tuple-element.68), channel_id=1, source_target_pairs={{0,4},{4,8},{8,12},{12,16},{16,20},{20,24},{24,28},{28,0},{1,5},{5... | collective-permute-start | bytes 1032200 | tf_op jit(solution)/shard_map/ppermute | solution.py:149
  176.8 8.5 %collective-permute-start.14 = (bf16[16,2688]{1,0:T(8,128)(2,1)S(1)}, bf16[16,2688]{1,0:T(8,128)(2,1)S(1)}, u32[]{:S(2)}, u32[]{:S(2)}) collective-permute-start(bf16[16,2688]{1,0:T(8,128)(2,1)S(1)} %collective-permute-done.13), channel_id=1, source_target_pairs={{0,28},{4,0},{8,4},{12,8},{16,12},{20,16},{24,20},{28,24},{1,29},{... | collective-permute-start | bytes 258056 | tf_op jit(solution)/shard_map/ppermute | solution.py:149
  193.4 12.9 %collective-permute-start.20 = (bf16[128,2688]{1,0:T(8,128)(2,1)}, bf16[128,2688]{1,0:T(8,128)(2,1)S(1)}, u32[]{:S(2)}, u32[]{:S(2)}) collective-permute-start(bf16[128,2688]{1,0:T(8,128)(2,1)} %get-tuple-element.75), channel_id=1, source_target_pairs={{0,3},{1,0},{2,1},{3,2},{4,7},{5,4},{6,5},{7,6},{8,11},{9,8},{10,9... | collective-permute-start | bytes 2064392 | tf_op jit(solution)/shard_map/ppermute | solution.py:149
  193.8 11.5 %collective-permute-start.21 = (bf16[128,2688]{1,0:T(8,128)(2,1)}, bf16[128,2688]{1,0:T(8,128)(2,1)S(1)}, u32[]{:S(2)}, u32[]{:S(2)}) collective-permute-start(bf16[128,2688]{1,0:T(8,128)(2,1)} %get-tuple-element.75), channel_id=1, source_target_pairs={{0,1},{1,2},{2,3},{3,0},{4,5},{5,6},{6,7},{7,4},{8,9},{9,10},{10,1... | collective-permute-start | bytes 2064392 | tf_op jit(solution)/shard_map/ppermute | solution.py:149
  194.9 8.2 %collective-permute-start.41 = (bf16[64,2688]{1,0:T(8,128)(2,1)S(1)}, bf16[64,2688]{1,0:T(8,128)(2,1)S(1)}, u32[]{:S(2)}, u32[]{:S(2)}) collective-permute-start(bf16[64,2688]{1,0:T(8,128)(2,1)S(1)} %collective-permute-done.40), channel_id=1, source_target_pairs={{0,28},{4,0},{8,4},{12,8},{16,12},{20,16},{24,20},{28,24},{1,29},{... | collective-permute-start | bytes 1032200 | tf_op jit(solution)/shard_map/ppermute | solution.py:149
  196.2 8.0 %collective-permute-start.44 = (bf16[64,2688]{1,0:T(8,128)(2,1)S(1)}, bf16[64,2688]{1,0:T(8,128)(2,1)S(1)}, u32[]{:S(2)}, u32[]{:S(2)}) collective-permute-start(bf16[64,2688]{1,0:T(8,128)(2,1)S(1)} %collective-permute-done.43), channel_id=1, source_target_pairs={{0,4},{4,8},{8,12},{12,16},{16,20},{20,24},{24,28},{28,0},{1,5},{5... | collective-permute-start | bytes 1032200 | tf_op jit(solution)/shard_map/ppermute | solution.py:149
  203.1 9.0 %collective-permute-start.42 = (bf16[64,2688]{1,0:T(8,128)(2,1)S(1)}, bf16[64,2688]{1,0:T(8,128)(2,1)S(1)}, u32[]{:S(2)}, u32[]{:S(2)}) collective-permute-start(bf16[64,2688]{1,0:T(8,128)(2,1)S(1)} %collective-permute-done.41), channel_id=1, source_target_pairs={{0,28},{4,0},{8,4},{12,8},{16,12},{20,16},{24,20},{28,24},{1,29},{... | collective-permute-start | bytes 1032200 | tf_op jit(solution)/shard_map/ppermute | solution.py:149
  204.2 7.8 %collective-permute-start.45 = (bf16[64,2688]{1,0:T(8,128)(2,1)S(1)}, bf16[64,2688]{1,0:T(8,128)(2,1)S(1)}, u32[]{:S(2)}, u32[]{:S(2)}) collective-permute-start(bf16[64,2688]{1,0:T(8,128)(2,1)S(1)} %collective-permute-done.44), channel_id=1, source_target_pairs={{0,4},{4,8},{8,12},{12,16},{16,20},{20,24},{24,28},{28,0},{1,5},{5... | collective-permute-start | bytes 1032200 | tf_op jit(solution)/shard_map/ppermute | solution.py:149
  205.4 12.4 %collective-permute-start.22 = (bf16[64,2688]{1,0:T(8,128)(2,1)S(1)}, bf16[64,2688]{1,0:T(8,128)(2,1)S(1)}, u32[]{:S(2)}, u32[]{:S(2)}) collective-permute-start(bf16[64,2688]{1,0:T(8,128)(2,1)S(1)} %slice.271), channel_id=1, source_target_pairs={{0,1},{1,2},{2,3},{3,0},{4,5},{5,6},{6,7},{7,4},{8,9},{9,10},{10,1... | collective-permute-start | bytes 1032200 | tf_op jit(solution)/shard_map/ppermute | solution.py:149
  206.3 11.5 %collective-permute-start.23 = (bf16[64,2688]{1,0:T(8,128)(2,1)S(1)}, bf16[64,2688]{1,0:T(8,128)(2,1)S(1)}, u32[]{:S(2)}, u32[]{:S(2)}) collective-permute-start(bf16[64,2688]{1,0:T(8,128)(2,1)S(1)} %slice.272), channel_id=1, source_target_pairs={{0,3},{1,0},{2,1},{3,2},{4,7},{5,4},{6,5},{7,6},{8,11},{9,8},{10,9... | collective-permute-start | bytes 1032200 | tf_op jit(solution)/shard_map/ppermute | solution.py:149
  264.1 90.3 %all-to-all-start.1 = ((bf16[8,64,512]{2,1,0:T(8,128)(2,1)}), bf16[8,64,512]{2,1,0:T(8,128)(2,1)S(1)}, u32[]{:S(2)}, u32[]{:S(2)}) async-start(bf16[8,64,512]{2,1,0:T(8,128)(2,1)} %bitcast.11), calls=%async_computation.1 | async-start | bytes 1048576 | tf_op jit(solution)/shard_map/all_to_all | solution.py:273
  (27 other events, 165.8 us)

commit v2 on v1

v2 whole, which is shorter than its diff:
```python
import jax
import jax.numpy as jnp
from jax import lax
from jax.experimental import pallas as pl
from jax.experimental.pallas import tpu as pltpu
from jax.sharding import Mesh
from jax.sharding import PartitionSpec as P

D = 8192
BLK = 128
NZ, NX = 8, 4
HA, HB = 1024, 768
COL = ("col_0", "col_1")
ALL = ("row", "col_0", "col_1")
norm_eps = 1e-05

f32 = jnp.float32
bf16 = jnp.bfloat16
VMEM_BYTES = 56 * 1024 * 1024


def vmem():
    return pl.BlockSpec(memory_space=pltpu.VMEM)


def smem():
    return pl.BlockSpec(memory_space=pltpu.SMEM)


def call(kernel, outs, in_specs, scratch, flops, nbytes, args):
    return pl.pallas_call(
        kernel,
        out_shape=outs,
        in_specs=in_specs,
        out_specs=tuple(vmem() for _ in outs),
        scratch_shapes=scratch,
        compiler_params=pltpu.CompilerParams(vmem_limit_bytes=VMEM_BYTES),
        cost_estimate=pl.CostEstimate(flops=flops, bytes_accessed=nbytes, transcendentals=0),
    )(*args)


def nn(a, b):
    return jnp.dot(a, b, preferred_element_type=f32)


def nt(a, b):
    return lax.dot_general(a, b, (((1,), (1,)), ((), ())), preferred_element_type=f32)


def tn(a, b):
    return lax.dot_general(a, b, (((0,), (0,)), ((), ())), preferred_element_type=f32)


def parts3(v):
    hi = v.astype(bf16)
    rest = v - hi.astype(f32)
    mid = rest.astype(bf16)
    return hi, mid, (rest - mid.astype(f32)).astype(bf16)


def lane_sum(block, at):
    return sum(block[:, i : i + 1].astype(f32) for i in range(at, at + 3))


def pieces_of_tokens(z):
    for tz in range(NZ):
        k = lax.rem(tz - z + NZ, NZ)
        for tx in range(NX):
            nat = slice(tz * 64 + tx * 16, tz * 64 + tx * 16 + 16)
            in_a = slice((tx * NZ + tz) * 16, (tx * NZ + tz) * 16 + 16)
            in_b = pl.ds(pl.multiple_of(k * 64 + tx * 16, 16), 16)
            yield nat, in_a, in_b


def masks_kernel(mg, mu, md, wg, wu, wd, eff_g, eff_u, eff_d):
    for w, m, e in ((wg, mg, eff_g), (wu, mu, eff_u), (wd, md, eff_d)):
        for a in range(w.shape[0] // BLK):
            for b in range(w.shape[1] // BLK):
                r, c = slice(a * BLK, (a + 1) * BLK), slice(b * BLK, (b + 1) * BLK)
                e[r, c] = w[r, c] * m[a, b].astype(f32).astype(bf16)


def partials_kernel(pos, rows, gain, eff_g, eff_u, eff_d, part_a, part_b, la, lb):
    width = gain.shape[1]
    for nat, in_a, in_b in pieces_of_tokens(pos[1]):
        x = (rows[nat, :width].astype(f32) * gain[...]).astype(bf16)
        g = rows[nat, width:]
        sq = jnp.square(rows[nat, :width].astype(f32))
        part_b[in_b, 3 * HB :] = (sq[:, :BLK] + sq[:, BLK:]).astype(bf16)
        la[in_a, :width] = x
        lb[in_b, :width] = x
        la[in_a, width:] = g
        lb[in_b, width:] = g
    for left, part, at, half in ((lb, part_b, HA, HB), (la, part_a, 0, HA)):
        cols = slice(at, at + half)
        for t in range(0, left.shape[0], 128):
            tok = slice(t, t + 128)
            x, g = left[tok, :width], left[tok, width:]
            part[tok, :half] = nn(x, eff_g[:, cols]).astype(bf16)
            part[tok, half : 2 * half] = nn(x, eff_u[:, cols]).astype(bf16)
            part[tok, 2 * half : 3 * half] = nt(g, eff_d[cols, :]).astype(bf16)


def fetch_pieces(pieces, gb, sems):
    copies, at = [], 0
    for i, p in enumerate(pieces):
        copies.append(pltpu.make_async_copy(p, gb.at[pl.ds(at, p.shape[0])], sems.at[i]))
        copies[-1].start()
        at += p.shape[0]
    return copies


def features_kernel(pos, rows, ga, eff_g, eff_u, eff_d, *rest):
    pieces, (both, own_scale, gb, da, na, db, nb, sems) = rest[:-8], rest[-8:]
    copies = fetch_pieces(pieces, gb, sems)
    width = eff_g.shape[0]
    for hid, d, n, at, half in ((ga, da, na, 0, HA), (gb, db, nb, HA, HB)):
        if at:
            for c in copies:
                c.wait()
        cols = slice(at, at + half)
        for t in range(0, hid.shape[0], 128):
            tok = slice(t, t + 128)
            d[tok, :] = nn(hid[tok, :half], eff_d[cols, :])
            n[tok, :] = nt(hid[tok, half : 2 * half], eff_g[:, cols]) + nt(
                hid[tok, 2 * half : 3 * half], eff_u[:, cols]
            )
    total = jnp.zeros((16, width), f32)
    for nat, in_a, in_b in pieces_of_tokens(pos[1]):
        extra = ga[in_a, 3 * HA :]
        both[nat, :width] = (da[in_a, :] + db[in_b, :]).astype(bf16)
        grad = na[in_a, :] + nb[in_b, :]
        both[nat, width : 2 * width] = grad.astype(bf16)
        total += grad * rows[nat, :width].astype(f32) * lane_sum(extra, 0)
    gain_row = jnp.sum(total, axis=0, keepdims=True)
    lane = lax.broadcasted_iota(jnp.int32, (64, BLK), 1)
    line = lax.broadcasted_iota(jnp.int32, (64, BLK), 0)
    shared = jnp.zeros((64, BLK), f32)
    for c in range(width // 64):
        half_row = gain_row[:, (c // 2) * BLK : (c // 2 + 1) * BLK]
        picked = jnp.where(lane == line + 64 * (c % 2), half_row, 0.0)
        for i, v in enumerate(parts3(jnp.sum(picked, axis=1, keepdims=True))):
            shared = jnp.where(lane == 3 + 3 * c + i, v.astype(f32), shared)
    shared = shared.astype(bf16)
    lane16 = lax.broadcasted_iota(jnp.int32, (16, BLK), 1)
    for tz in range(NZ):
        for tx in range(NX):
            nat = slice(tz * 64 + tx * 16, tz * 64 + tx * 16 + 16)
            extra = ga[(tx * NZ + tz) * 16 : (tx * NZ + tz) * 16 + 16, 3 * HA :].astype(f32)
            moved = jnp.where(lane16 < 3, pltpu.roll(extra, BLK - 3, 1), 0.0)
            both[nat, 2 * width :] = shared[tx * 16 : tx * 16 + 16, :] + moved.astype(bf16)
    for tx in range(NX):
        at = pl.ds(pl.multiple_of(tx * 128 + pos[0] * 16, 16), 16)
        s = lane_sum(ga[at, 3 * HA :], 0)
        own_scale[tx * 16 : tx * 16 + 16, :] = jnp.broadcast_to(s, (16, BLK))


def weights_kernel(pos, mg, mu, md, rows, gain, ga, *rest):
    pieces, (out_g, out_u, out_d, gb, la, lb, sems) = rest[:-7], rest[-7:]
    copies = fetch_pieces(pieces, gb, sems)
    width = gain.shape[1]
    for nat, in_a, in_b in pieces_of_tokens(pos[1]):
        scale = lane_sum(ga[in_a, 3 * HA :], 0)
        x = (rows[nat, :width].astype(f32) * scale * gain[...]).astype(bf16)
        g = rows[nat, width:]
        la[in_a, :width] = x
        lb[in_b, :width] = x
        la[in_a, width:] = g
        lb[in_b, width:] = g
    for hid, left, at, half in ((ga, la, 0, HA), (gb, lb, HA, HB)):
        if at:
            for c in copies:
                c.wait()
        normed, grad = left[:, :width], left[:, width:]
        for c in range(0, half, BLK):
            b = (at + c) // BLK
            gw = tn(normed, hid[:, half + c : half + c + BLK])
            uw = tn(normed, hid[:, 2 * half + c : 2 * half + c + BLK])
            dw = tn(hid[:, c : c + BLK], grad)
            to = slice(at + c, at + c + BLK)
            for a in range(width // BLK):
                r = slice(a * BLK, (a + 1) * BLK)
                out_g[r, to] = (gw[r, :] * mg[a, b].astype(f32)).astype(bf16)
                out_u[r, to] = (uw[r, :] * mu[a, b].astype(f32)).astype(bf16)
                out_d[to, r] = (dw[:, r] * md[b, a].astype(f32)).astype(bf16)


def final_kernel(got, x, grad, gain, scale, layer_out, input_grad, gain_grad):
    width = gain.shape[1]
    s = got[0].astype(f32)
    for r in range(1, got.shape[0]):
        s = s + got[r].astype(f32)
    xf = x[...].astype(f32)
    layer_out[...] = (xf + s[:, :width]).astype(bf16)
    extra = s[:, 2 * width :]
    dots = lane_sum(extra, 0)
    sc = scale[:, :1]
    input_grad[...] = (
        grad[...].astype(f32)
        + sc * gain[...] * s[:, width : 2 * width]
        - xf * sc * sc * (dots / D)
    ).astype(bf16)
    lane = lax.broadcasted_iota(jnp.int32, (64, BLK), 1)
    line = lax.broadcasted_iota(jnp.int32, (64, BLK), 0)
    for h in range(width // BLK):
        spread = jnp.where(
            lane < 64,
            jnp.where(lane == line, lane_sum(extra, 3 + 6 * h), 0.0),
            jnp.where(lane == line + 64, lane_sum(extra, 6 + 6 * h), 0.0),
        )
        gain_grad[:, h * BLK : (h + 1) * BLK] = jnp.sum(spread, axis=0, keepdims=True)


def send(v, axis, step):
    n = lax.axis_size(axis)
    return lax.ppermute(v, axis, [(i, (i + step) % n) for i in range(n)])


def up32(v):
    return v.astype(f32)


def add_top(piece, got, h):
    return jnp.concatenate([(up32(piece[:h]) + up32(got)).astype(bf16), piece[h:].astype(bf16)])


def add_bottom(piece, got, h):
    return jnp.concatenate([piece[:h].astype(bf16), (up32(piece[h:]) + up32(got)).astype(bf16)])


def plus(piece, got):
    return (up32(piece) + up32(got)).astype(bf16)


def reduce_ring(pieces, axis):
    n = len(pieces)
    far = pieces[n // 2].astype(bf16)
    h = far.shape[0] // 2
    right, left = send(far[:h], axis, 1), send(far[h:], axis, -1)
    for away in range(n // 2 - 1, 0, -1):
        to_right, to_left = pieces[away], pieces[n - away]
        if away == n // 2 - 1:
            right = send(add_top(to_right, right, h), axis, 1)
            left = send(add_bottom(to_left, left, h), axis, -1)
        else:
            right = send(plus(to_right, right), axis, 1)
            left = send(plus(to_left, left), axis, -1)
    return up32(pieces[0]) + up32(right) + up32(left)


def gather_ring(shard, axis):
    n = lax.axis_size(axis)
    h = shard.shape[0] // 2
    from_right, from_left = [], []
    right = left = shard
    for _ in range(1, n // 2):
        right, left = send(right, axis, 1), send(left, axis, -1)
        from_left.insert(0, right)
        from_right.append(left)
    far = [send(right[:h], axis, 1), send(left[h:], axis, -1)]
    return [shard, *from_right, *far, *from_left]


def cut(v, n):
    m = v.shape[0] // n
    return [v[i * m : (i + 1) * m] for i in range(n)]


def hidden_grads(sums, half, scale):
    gate, up = sums[:, :half] * scale, sums[:, half : 2 * half] * scale
    act_grad = sums[:, 2 * half : 3 * half]
    sig = jax.nn.sigmoid(gate)
    act = (gate * sig * up).astype(bf16)
    gate_grad = (act_grad * up * sig * (1.0 + gate * (1.0 - sig))).astype(bf16)
    up_grad = (act_grad * gate * sig).astype(bf16)
    dots = jnp.sum(up32(gate_grad) * gate + up32(up_grad) * up, axis=1, keepdims=True)
    return [act, gate_grad, up_grad], dots


def split3(v):
    hi = lax.reduce_precision(v, 8, 7)
    mid = lax.reduce_precision(v - hi, 8, 7)
    return [hi, mid, v - hi - mid]


def exchange(v, axis):
    n = lax.axis_size(axis)
    got = lax.all_to_all(v.reshape(n, -1, v.shape[-1]), axis, 0, 0, tiled=True)
    return jnp.sum(up32(got), axis=0)


def from_everyone(shard, axis):
    copies = jnp.broadcast_to(shard, (lax.axis_size(axis), *shard.shape))
    got = lax.all_to_all(copies, axis, split_axis=0, concat_axis=0, tiled=True)
    return got.reshape(-1, shard.shape[-1])


def shape(v):
    return jax.ShapeDtypeStruct(v.shape, v.dtype)


def shards(layer_input, norm_gain, w_gate, w_up, w_down, mask_gate, mask_up, mask_down, out_grad):
    row, z = lax.axis_index("row"), lax.axis_index("col_0")
    pos = jnp.stack([row, z]).astype(jnp.int32)
    gain = norm_gain[None, :]
    mine, width = layer_input.shape
    hidden = w_gate.shape[1]
    rows = from_everyone(jnp.concatenate([layer_input, out_grad], axis=1), "row")
    tokens = rows.shape[0]
    flops = 2 * tokens * width * hidden * 3
    eff = call(
        masks_kernel,
        (shape(w_gate), shape(w_up), shape(w_down)),
        [smem()] * 3 + [vmem()] * 3,
        [],
        0,
        6_000_000,
        (mask_gate, mask_up, mask_down, w_gate, w_up, w_down),
    )
    part_a, part_b = call(
        partials_kernel,
        (
            jax.ShapeDtypeStruct((tokens, 3 * HA), bf16),
            jax.ShapeDtypeStruct((tokens, 3 * HB + BLK), bf16),
        ),
        [smem()] + [vmem()] * 5,
        [pltpu.VMEM((tokens, 2 * width), bf16)] * 2,
        flops,
        9_000_000,
        (pos, rows, gain, *eff),
    )
    sums_b = exchange(reduce_ring(cut(part_b, NZ), "col_0").astype(bf16), "col_1")
    sums_a = exchange(exchange(part_a, "col_1").astype(bf16), "col_0")
    squares = jnp.sum(sums_b[:, 3 * HB :], axis=1, keepdims=True)
    scale = lax.rsqrt(squares / D + norm_eps)
    hid_b, dots_b = hidden_grads(sums_b, HB, scale)
    hid_a, dots_a = hidden_grads(sums_a, HA, scale)
    extra = jnp.concatenate(split3(scale) + split3(dots_a + dots_b), axis=1)
    extra = jnp.pad(extra.astype(bf16), ((0, 0), (0, BLK - 6)))
    send_b = jnp.concatenate(hid_b, axis=1)
    send_a = jnp.concatenate([*hid_a, extra], axis=1)
    pieces_b = gather_ring(from_everyone(send_b, "col_1"), "col_0")
    all_a = from_everyone(from_everyone(send_a, "col_0"), "col_1")

    anywhere = [pl.BlockSpec(memory_space=pl.ANY)] * len(pieces_b)
    gb = pltpu.VMEM((tokens, 3 * HB), bf16)
    sems = pltpu.SemaphoreType.DMA((len(pieces_b),))
    both, own_scale = call(
        features_kernel,
        (
            jax.ShapeDtypeStruct((tokens, 2 * width + BLK), bf16),
            jax.ShapeDtypeStruct((mine, BLK), f32),
        ),
        [smem()] + [vmem()] * 5 + anywhere,
        [gb, *[pltpu.VMEM((tokens, width), f32)] * 4, sems],
        flops,
        9_000_000,
        (pos, rows, all_a, *eff, *pieces_b),
    )
    got = lax.all_to_all(both.reshape(-1, mine, both.shape[1]), "row", 0, 0, tiled=True)
    gate_wgrad, up_wgrad, down_wgrad = call(
        weights_kernel,
        (shape(w_gate), shape(w_up), shape(w_down)),
        [smem()] * 4 + [vmem()] * 3 + anywhere,
        [gb, *[pltpu.VMEM((tokens, 2 * width), bf16)] * 2, sems],
        flops,
        9_000_000,
        (pos, mask_gate, mask_up, mask_down, rows, gain, all_a, *pieces_b),
    )
    layer_out, input_grad, gain_grad = call(
        final_kernel,
        (shape(layer_input), shape(out_grad), shape(gain)),
        [vmem()] * 5,
        [],
        0,
        1_000_000,
        (got, layer_input, out_grad, gain, own_scale),
    )
    return (layer_out, input_grad, gain_grad[0], gate_wgrad, up_wgrad, down_wgrad)


def solution(mesh):
    torus = Mesh(mesh.devices.reshape(mesh.shape["row"], NZ, NX), ALL)
    placed = (
        P("row", COL),
        P(COL),
        P(COL, "row"),
        P(COL, "row"),
        P("row", COL),
        P(COL, "row"),
        P(COL, "row"),
        P("row", COL),
        P("row", COL),
    )
    return jax.shard_map(
        shards,
        mesh=torus,
        in_specs=placed,
        out_specs=(
            P("row", COL),
            P("row", COL),
            P(COL),
            P(COL, "row"),
            P(COL, "row"),
            P("row", COL),
        ),
        check_vma=False,
    )
```

time: 360 us -> 220 us (0.61)
  blocking collectives: 173 us -> 19.4 us
  waiting for transfers between devices: 46.2 us -> 89.3 us
  starting transfers between devices: 83.3 us -> 61 us
  local copies, waits for them, and re-layouts: 18.5 us -> 9.61 us
  Pallas kernels: 21.8 us -> 26.9 us
    psum x2 -> x0, blocking collectives: 137 us -> none  [the longest x1 78.3 us: shards(): lax.psum(lax.dynamic_update_slice_in_dim(jnp.zeros((tokens,), f32), dots_...]
    ppermute x48 -> x16, starting transfers between devices: 72.5 us -> 21.8 us  [send(): return lax.ppermute(v, axis, [(i, (i + step) % n) for i in range(n)])]
    all_to_all x2 -> x7, waiting for transfers between devices: 7.51 us -> 50.4 us  [the longest x3 36.4 us: exchange(): got = lax.all_to_all(v.reshape(n, -1, v.shape[-1]), axis, 0, 0, tiled=True)]
    all_to_all x2 -> x7, starting transfers between devices: 10.7 us -> 39.2 us  [the longest x3 13.8 us: from_everyone(): got = lax.all_to_all(copies, axis, split_axis=0, concat_axis=0, tiled=True)]
    all_to_all x1, blocking collectives: 36.1 us -> 19.4 us  [from_everyone(): got = lax.all_to_all(copies, axis, split_axis=0, concat_axis=0, tiled=True)]
    unnamed x39 -> x24, local copies, waits for them, and re-layouts: 11.1 us -> 4.83 us
    pallas_call x3 -> x5, Pallas kernels: 21.8 us -> 26.9 us  [call(): pl.pallas_call(kernel, out_shape=outs, in_specs=in_specs, out_specs=tuple...]
    convert_element_type x6 -> x3, other arithmetic: 0.42 us -> 4.13 us  [plus(): return (up32(piece) + up32(got)).astype(bf16)]
  transfers between devices with their start and end apart: 50 -> 23, of which waited for: 15 -> 16; matrix products, arithmetic and copies ran while one was open for 6% -> 5% of each run, Pallas kernels for 2% -> 5%
where the time goes in v2:
time: 220 us; the launch traced here: 219 us
  waiting for transfers between devices  89.3 us (41%)
  starting transfers between devices  61 us (28%)
  Pallas kernels  26.9 us (12%)
  blocking collectives  19.4 us (9%)
  other arithmetic  11.6 us (5%)
  local copies, waits for them, and re-layouts  9.61 us (4%)
    ppermute x16, waiting for transfers between devices, send(): return lax.ppermute(v, axis, [(i, (i + step) % n) for i in range(n)])  38.9 us
    all_to_all x3, waiting for transfers between devices, exchange(): got = lax.all_to_all(v.reshape(n, -1, v.shape[-1]), axis, 0, 0, tiled=True)  36.4 us
    pallas_call x5, Pallas kernels, call(): pl.pallas_call(kernel, out_shape=outs, in_specs=in_specs, out_specs=tuple...  26.9 us
    ppermute x16, starting transfers between devices, send(): return lax.ppermute(v, axis, [(i, (i + step) % n) for i in range(n)])  21.8 us
    all_to_all x1, blocking collectives, from_everyone(): got = lax.all_to_all(copies, axis, split_axis=0, concat_axis=0, tiled=True)  19.4 us
    all_to_all x3, starting transfers between devices, from_everyone(): got = lax.all_to_all(copies, axis, split_axis=0, concat_axis=0, tiled=True)  13.8 us
    all_to_all x1, starting transfers between devices, shards(): lax.all_to_all(both.reshape(-1, mine, both.shape[1]), 'row', 0, 0, tiled=...  13.6 us
    all_to_all x3, starting transfers between devices, exchange(): got = lax.all_to_all(v.reshape(n, -1, v.shape[-1]), axis, 0, 0, tiled=True)  11.8 us
  transfers between devices with their start and end apart: 23, of which 16 were waited for; matrix products, arithmetic and copies ran while one was open for 5% of the time, Pallas kernels for 5%

profile of v2, /device:TPU:1, one launch (start us, length us, event | category | flops | bytes accessed | tf_op | source)
XLA Modules:
  0.0 218.7 jit_solution(1382552491728285088)
XLA Ops:
  2.3 6.6 %all-to-all-start = ((bf16[8,64,512]{2,1,0:T(8,128)(2,1)}), bf16[8,64,512]{2,1,0:T(8,128)(2,1)S(1)}, u32[]{:S(2)}, u32[]{:S(2)}) async-start(bf16[8,64,512]{2,1,0:T(8,128)(2,1)} %broadcast_in_dim.18), calls=%async_computation | async-start | bytes 1048576 | tf_op jit(solution)/shard_map/all_to_all | solution.py:294
  10.2 3.8 %shard_map.136 = (bf16[256,1792]{1,0:T(8,128)(2,1)}, bf16[256,1792]{1,0:T(8,128)(2,1)}, bf16[1792,256]{1,0:T(8,128)(2,1)}) custom-call(s32[2,14]{1,0:T(2,128)} %mg.3, s32[2,14]{1,0:T(2,128)} %mu.3, s32[14,2]{1,0:T(8,128)} %copy.24.md, bf16[256,1792]{1,0:T(8,128)(2,1)} %wg.1, bf16[256,1792]{1,0:T(8,128)(2,1)} %wu.1, bf16[1792,256]{1,0:T(8,128)(2,1)} %wd.1), custom_call_target="tpu_custom_call" | custom-call | bytes 6000000 | tf_op jit(solution)/shard_map/pallas_call | solution.py:31
  14.6 3.8 %all-to-all-done = bf16[8,64,512]{2,1,0:T(8,128)(2,1)S(1)} async-done(((bf16[8,64,512]{2,1,0:T(8,128)(2,1)}), bf16[8,64,512]{2,1,0:T(8,128)(2,1)S(1)}, u32[]{:S(2)}, u32[]{:S(2)}) %all-to-all-start) | async-done | bytes 524320 | tf_op jit(solution)/shard_map/all_to_all | solution.py:294
  19.2 6.0 %shard_map.137 = (bf16[512,3072]{1,0:T(8,128)(2,1)}, bf16[512,2432]{1,0:T(8,128)(2,1)}) custom-call(s32[2]{0:T(128)} %pad_add_fusion.pos, bf16[512,512]{1,0:T(8,128)(2,1)} %bitcast.28, f32[1,256]{1,0:T(1,128)} %bitcast.40, bf16[256,1792]{1,0:T(8,128)(2,1)} %get-tuple-element.19.eff_g, bf16[256,1792]{1,0:T(8,128)(2,1)} %get-tuple-element.20.eff_u, ...), custom_call_target="tpu_custom_call" | custom-call | flops 1409286144 | bytes 9000000 | tf_op jit(solution)/shard_map/pallas_call | solution.py:31
  27.4 4.0 %collective-permute-start.4 = (bf16[32,2432]{1,0:T(8,128)(2,1)S(1)}, bf16[32,2432]{1,0:T(8,128)(2,1)S(1)}, u32[]{:S(2)}, u32[]{:S(2)}) collective-permute-start(bf16[32,2432]{1,0:T(8,128)(2,1)S(1)} %get-tuple-element.45), channel_id=1, source_target_pairs={{0,28},{4,0},{8,4},{12,8},{16,12},{20,16},{24,20},{28,24},{1,29},{... | collective-permute-start | bytes 466952 | tf_op jit(solution)/shard_map/ppermute | solution.py:216
  31.4 3.4 %collective-permute-done = bf16[32,2432]{1,0:T(8,128)(2,1)S(1)} collective-permute-done((bf16[32,2432]{1,0:T(8,128)(2,1)S(1)}, bf16[32,2432]{1,0:T(8,128)(2,1)S(1)}, u32[]{:S(2)}, u32[]{:S(2)}) %collective-permute-start) | collective-permute-done | bytes 155680 | tf_op jit(solution)/shard_map/ppermute | solution.py:216
  39.5 5.2 %collective-permute-done.1 = bf16[64,2432]{1,0:T(8,128)(2,1)S(1)} collective-permute-done((bf16[64,2432]{1,0:T(8,128)(2,1)S(1)}, bf16[64,2432]{1,0:T(8,128)(2,1)S(1)}, u32[]{:S(2)}, u32[]{:S(2)}) %collective-permute-start.1) | collective-permute-done | bytes 311328 | tf_op jit(solution)/shard_map/ppermute | solution.py:216
  46.5 4.0 %all-to-all-start.1 = ((bf16[4,128,3072]{2,1,0:T(8,128)(2,1)}), bf16[4,128,3072]{2,1,0:T(8,128)(2,1)S(1)}, u32[]{:S(2)}, u32[]{:S(2)}) async-start(bf16[4,128,3072]{2,1,0:T(8,128)(2,1)} %bitcast.32), calls=%async_computation.1 | async-start | bytes 6291456 | tf_op jit(solution)/shard_map/all_to_all | solution.py:288
  50.5 3.9 %collective-permute-done.2 = bf16[64,2432]{1,0:T(8,128)(2,1)} collective-permute-done((bf16[64,2432]{1,0:T(8,128)(2,1)}, bf16[64,2432]{1,0:T(8,128)(2,1)}, u32[]{:S(2)}, u32[]{:S(2)}) %collective-permute-start.2) | collective-permute-done | bytes 311328 | tf_op jit(solution)/shard_map/ppermute | solution.py:216
  57.3 4.6 %collective-permute-done.6 = bf16[64,2432]{1,0:T(8,128)(2,1)S(1)} collective-permute-done((bf16[64,2432]{1,0:T(8,128)(2,1)S(1)}, bf16[64,2432]{1,0:T(8,128)(2,1)S(1)}, u32[]{:S(2)}, u32[]{:S(2)}) %collective-permute-start.6) | collective-permute-done | bytes 311328 | tf_op jit(solution)/shard_map/ppermute | solution.py:216
  64.2 4.8 %collective-permute-done.7 = bf16[64,2432]{1,0:T(8,128)(2,1)S(1)} collective-permute-done((bf16[64,2432]{1,0:T(8,128)(2,1)S(1)}, bf16[64,2432]{1,0:T(8,128)(2,1)S(1)}, u32[]{:S(2)}, u32[]{:S(2)}) %collective-permute-start.7) | collective-permute-done | bytes 311328 | tf_op jit(solution)/shard_map/ppermute | solution.py:216
  70.9 14.6 %all-to-all-done.1 = bf16[4,128,3072]{2,1,0:T(8,128)(2,1)S(1)} async-done(((bf16[4,128,3072]{2,1,0:T(8,128)(2,1)}), bf16[4,128,3072]{2,1,0:T(8,128)(2,1)S(1)}, u32[]{:S(2)}, u32[]{:S(2)}) %all-to-all-start.1) | async-done | bytes 3145760 | tf_op jit(solution)/shard_map/all_to_all | solution.py:288
  85.4 3.5 %all-to-all-start.3 = ((bf16[4,16,2432]{2,1,0:T(8,128)(2,1)}), bf16[4,16,2432]{2,1,0:T(8,128)(2,1)S(1)}, u32[]{:S(2)}, u32[]{:S(2)}) async-start(bf16[4,16,2432]{2,1,0:T(8,128)(2,1)} %bitcast.38), calls=%async_computation.3 | async-start | bytes 622592 | tf_op jit(solution)/shard_map/all_to_all | solution.py:288
  90.6 4.1 %all-to-all-done.3 = bf16[4,16,2432]{2,1,0:T(8,128)(2,1)S(1)} async-done(((bf16[4,16,2432]{2,1,0:T(8,128)(2,1)}), bf16[4,16,2432]{2,1,0:T(8,128)(2,1)S(1)}, u32[]{:S(2)}, u32[]{:S(2)}) %all-to-all-start.3) | async-done | bytes 311328 | tf_op jit(solution)/shard_map/all_to_all | solution.py:288
  94.7 4.3 %all-to-all-start.2 = ((bf16[8,16,3072]{2,1,0:T(8,128)(2,1)}), bf16[8,16,3072]{2,1,0:T(8,128)(2,1)S(1)}, u32[]{:S(2)}, u32[]{:S(2)}) async-start(bf16[8,16,3072]{2,1,0:T(8,128)(2,1)} %bitcast.33), calls=%async_computation.2 | async-start | bytes 1572864 | tf_op jit(solution)/shard_map/all_to_all | solution.py:288
  99.4 17.7 %all-to-all-done.2 = bf16[8,16,3072]{2,1,0:T(8,128)(2,1)S(1)} async-done(((bf16[8,16,3072]{2,1,0:T(8,128)(2,1)}), bf16[8,16,3072]{2,1,0:T(8,128)(2,1)S(1)}, u32[]{:S(2)}, u32[]{:S(2)}) %all-to-all-start.2) | async-done | bytes 786464 | tf_op jit(solution)/shard_map/all_to_all | solution.py:288
  117.8 3.5 %all-to-all-start.6 = ((bf16[4,16,2304]{2,1,0:T(8,128)(2,1)}), bf16[4,16,2304]{2,1,0:T(8,128)(2,1)S(1)}, u32[]{:S(2)}, u32[]{:S(2)}) async-start(bf16[4,16,2304]{2,1,0:T(8,128)(2,1)} %broadcast_in_dim.22), calls=%async_computation.6 | async-start | bytes 589824 | tf_op jit(solution)/shard_map/all_to_all | solution.py:294
  121.8 5.2 %all-to-all-done.6 = bf16[4,16,2304]{2,1,0:T(8,128)(2,1)S(1)} async-done(((bf16[4,16,2304]{2,1,0:T(8,128)(2,1)}), bf16[4,16,2304]{2,1,0:T(8,128)(2,1)S(1)}, u32[]{:S(2)}, u32[]{:S(2)}) %all-to-all-start.6) | async-done | bytes 294944 | tf_op jit(solution)/shard_map/all_to_all | solution.py:294
  127.0 19.4 %all_to_all.40 = bf16[8,16,3200]{2,1,0:T(8,128)(2,1)S(1)} all-to-all(bf16[8,16,3200]{2,1,0:T(8,128)(2,1)S(1)} %broadcast_in_dim.20), channel_id=1, replica_groups=mesh['row'=8,'col_0'=8,'col_1'=4] {'col_0'}, dimensions={0} | all-to-all | bytes 1638400 | tf_op jit(solution)/shard_map/all_to_all | solution.py:294
  148.3 3.7 %all-to-all-start.5 = ((bf16[4,128,3200]{2,1,0:T(8,128)(2,1)}), bf16[4,128,3200]{2,1,0:T(8,128)(2,1)S(1)}, u32[]{:S(2)}, u32[]{:S(2)}) async-start(bf16[4,128,3200]{2,1,0:T(8,128)(2,1)} %broadcast_in_dim.21), calls=%async_computation.5 | async-start | bytes 6553600 | tf_op jit(solution)/shard_map/all_to_all | solution.py:294
  152.3 2.7 %collective-permute-start.8 = (bf16[64,2304]{1,0:T(8,128)(2,1)}, bf16[64,2304]{1,0:T(8,128)(2,1)S(1)}, u32[]{:S(2)}, u32[]{:S(2)}) collective-permute-start(bf16[64,2304]{1,0:T(8,128)(2,1)} %bitcast.35), channel_id=1, source_target_pairs={{0,28},{4,0},{8,4},{12,8},{16,12},{20,16},{24,20},{28,24},{1,29},{... | collective-permute-start | bytes 884744 | tf_op jit(solution)/shard_map/ppermute | solution.py:216
  155.0 4.3 %collective-permute-done.11.rest_8_ = bf16[64,2304]{1,0:T(8,128)(2,1)S(1)} collective-permute-done((bf16[64,2304]{1,0:T(8,128)(2,1)}, bf16[64,2304]{1,0:T(8,128)(2,1)S(1)}, u32[]{:S(2)}, u32[]{:S(2)}) %collective-permute-start.11) | collective-permute-done | bytes 294944 | tf_op jit(solution)/shard_map/ppermute | solution.py:216
  159.3 2.7 %collective-permute-start.9 = (bf16[64,2304]{1,0:T(8,128)(2,1)S(1)}, bf16[64,2304]{1,0:T(8,128)(2,1)S(1)}, u32[]{:S(2)}, u32[]{:S(2)}) collective-permute-start(bf16[64,2304]{1,0:T(8,128)(2,1)S(1)} %collective-permute-done.8.rest_1_), channel_id=1, source_target_pairs={{0,28},{4,0},{8,4},{12,8},{16,12},{20,16},{24,20},{28,24},{1,29},{... | collective-permute-start | bytes 884744 | tf_op jit(solution)/shard_map/ppermute | solution.py:216
  162.0 5.5 %collective-permute-done.12.rest_7_ = bf16[64,2304]{1,0:T(8,128)(2,1)S(1)} collective-permute-done((bf16[64,2304]{1,0:T(8,128)(2,1)S(1)}, bf16[64,2304]{1,0:T(8,128)(2,1)S(1)}, u32[]{:S(2)}, u32[]{:S(2)}) %collective-permute-start.12) | collective-permute-done | bytes 294944 | tf_op jit(solution)/shard_map/ppermute | solution.py:216
  167.5 2.7 %collective-permute-start.10 = (bf16[64,2304]{1,0:T(8,128)(2,1)S(1)}, bf16[64,2304]{1,0:T(8,128)(2,1)S(1)}, u32[]{:S(2)}, u32[]{:S(2)}) collective-permute-start(bf16[64,2304]{1,0:T(8,128)(2,1)S(1)} %collective-permute-done.9.rest_2_), channel_id=1, source_target_pairs={{0,28},{4,0},{8,4},{12,8},{16,12},{20,16},{24,20},{28,24},{1,29},{... | collective-permute-start | bytes 884744 | tf_op jit(solution)/shard_map/ppermute | solution.py:216
  170.2 4.5 %collective-permute-done.13.rest_6_ = bf16[64,2304]{1,0:T(8,128)(2,1)S(1)} collective-permute-done((bf16[64,2304]{1,0:T(8,128)(2,1)S(1)}, bf16[64,2304]{1,0:T(8,128)(2,1)S(1)}, u32[]{:S(2)}, u32[]{:S(2)}) %collective-permute-start.13) | collective-permute-done | bytes 294944 | tf_op jit(solution)/shard_map/ppermute | solution.py:216
  174.8 2.7 %collective-permute-start.15 = (bf16[32,2304]{1,0:T(8,128)(2,1)S(1)}, bf16[32,2304]{1,0:T(8,128)(2,1)}, u32[]{:S(2)}, u32[]{:S(2)}) collective-permute-start(bf16[32,2304]{1,0:T(8,128)(2,1)S(1)} %slice.97), channel_id=1, source_target_pairs={{0,28},{4,0},{8,4},{12,8},{16,12},{20,16},{24,20},{28,24},{1,29},{... | collective-permute-start | bytes 442376 | tf_op jit(solution)/shard_map/ppermute | solution.py:216
  177.5 2.7 %collective-permute-done.14.rest_4_ = bf16[32,2304]{1,0:T(8,128)(2,1)S(1)} collective-permute-done((bf16[32,2304]{1,0:T(8,128)(2,1)S(1)}, bf16[32,2304]{1,0:T(8,128)(2,1)S(1)}, u32[]{:S(2)}, u32[]{:S(2)}) %collective-permute-start.14) | collective-permute-done | bytes 147488 | tf_op jit(solution)/shard_map/ppermute | solution.py:216
  184.1 7.3 %shard_map.138 = (bf16[512,640]{1,0:T(8,128)(2,1)}, f32[64,128]{1,0:T(8,128)}) custom-call(s32[2]{0:T(128)} %pad_add_fusion.pos, bf16[512,512]{1,0:T(8,128)(2,1)} %bitcast.29, bf16[512,3200]{1,0:T(8,128)(2,1)} %bitcast.26, bf16[256,1792]{1,0:T(8,128)(2,1)} %get-tuple-element.19.eff_g, bf16[256,1792]{1,0:T(8,128)(2,1)} %get-tuple-element.20.eff_u, ...), custom_call_target="tpu_custom_call" | custom-call | flops 1409286144 | bytes 9000000 | tf_op jit(solution)/shard_map/pallas_call | solution.py:31
  191.3 13.6 %all-to-all-start.7 = ((bf16[8,64,640]{2,1,0:T(8,128)(2,1)}), bf16[8,64,640]{2,1,0:T(8,128)(2,1)S(1)}, u32[]{:S(2)}, u32[]{:S(2)}) async-start(bf16[8,64,640]{2,1,0:T(8,128)(2,1)} %bitcast.39), calls=%async_computation.7 | async-start | bytes 1310720 | tf_op jit(solution)/shard_map/all_to_all | solution.py:360
  204.9 7.9 %shard_map.140 = (bf16[256,1792]{1,0:T(8,128)(2,1)}, bf16[256,1792]{1,0:T(8,128)(2,1)}, bf16[1792,256]{1,0:T(8,128)(2,1)}) custom-call(s32[2]{0:T(128)} %pad_add_fusion.pos, s32[2,14]{1,0:T(2,128)} %mg.3, s32[2,14]{1,0:T(2,128)} %mu.3, s32[14,2]{1,0:T(8,128)} %copy.24.md, bf16[512,512]{1,0:T(8,128)(2,1)} %bitcast.30, f32[1,256]{1,0:T(1,128)} %bitcast.41, ...), custom_call_target="tpu_custom_call" | custom-call | flops 1409286144 | bytes 9000000 | tf_op jit(solution)/shard_map/pallas_call | solution.py:31
  212.8 3.0 %all-to-all-done.7.got = bf16[8,64,640]{2,1,0:T(8,128)(2,1)S(1)} async-done(((bf16[8,64,640]{2,1,0:T(8,128)(2,1)}), bf16[8,64,640]{2,1,0:T(8,128)(2,1)S(1)}, u32[]{:S(2)}, u32[]{:S(2)}) %all-to-all-start.7) | async-done | bytes 655392 | tf_op jit(solution)/shard_map/all_to_all | solution.py:360
  (72 shorter events, 32.2 us)
Async XLA Ops:
  2.3 16.1 %all-to-all-start = ((bf16[8,64,512]{2,1,0:T(8,128)(2,1)}), bf16[8,64,512]{2,1,0:T(8,128)(2,1)S(1)}, u32[]{:S(2)}, u32[]{:S(2)}) async-start(bf16[8,64,512]{2,1,0:T(8,128)(2,1)} %broadcast_in_dim.18), calls=%async_computation | async-start | bytes 1048576 | tf_op jit(solution)/shard_map/all_to_all | solution.py:294
  26.4 8.5 %collective-permute-start = (bf16[32,2432]{1,0:T(8,128)(2,1)S(1)}, bf16[32,2432]{1,0:T(8,128)(2,1)S(1)}, u32[]{:S(2)}, u32[]{:S(2)}) collective-permute-start(bf16[32,2432]{1,0:T(8,128)(2,1)S(1)} %get-tuple-element.44), channel_id=1, source_target_pairs={{0,4},{4,8},{8,12},{12,16},{16,20},{20,24},{24,28},{28,0},{1,5},{5... | collective-permute-start | bytes 466952 | tf_op jit(solution)/shard_map/ppermute | solution.py:216
  27.4 7.5 %collective-permute-start.4 = (bf16[32,2432]{1,0:T(8,128)(2,1)S(1)}, bf16[32,2432]{1,0:T(8,128)(2,1)S(1)}, u32[]{:S(2)}, u32[]{:S(2)}) collective-permute-start(bf16[32,2432]{1,0:T(8,128)(2,1)S(1)} %get-tuple-element.45), channel_id=1, source_target_pairs={{0,28},{4,0},{8,4},{12,8},{16,12},{20,16},{24,20},{28,24},{1,29},{... | collective-permute-start | bytes 466952 | tf_op jit(solution)/shard_map/ppermute | solution.py:216
  36.0 8.7 %collective-permute-start.1 = (bf16[64,2432]{1,0:T(8,128)(2,1)S(1)}, bf16[64,2432]{1,0:T(8,128)(2,1)S(1)}, u32[]{:S(2)}, u32[]{:S(2)}) collective-permute-start(bf16[64,2432]{1,0:T(8,128)(2,1)S(1)} %pad_maximum_fusion), channel_id=1, source_target_pairs={{0,4},{4,8},{8,12},{12,16},{16,20},{20,24},{24,28},{28,0},{1,5},{5... | collective-permute-start | bytes 933896 | tf_op jit(solution)/shard_map/ppermute | solution.py:216
  36.8 13.7 %collective-permute-start.5 = (bf16[64,2432]{1,0:T(8,128)(2,1)}, bf16[64,2432]{1,0:T(8,128)(2,1)S(1)}, u32[]{:S(2)}, u32[]{:S(2)}) collective-permute-start(bf16[64,2432]{1,0:T(8,128)(2,1)} %pad_maximum_fusion.1), channel_id=1, source_target_pairs={{0,28},{4,0},{8,4},{12,8},{16,12},{20,16},{24,20},{28,24},{1,29},{... | collective-permute-start | bytes 933896 | tf_op jit(solution)/shard_map/ppermute | solution.py:216
  46.5 8.0 %collective-permute-start.2 = (bf16[64,2432]{1,0:T(8,128)(2,1)}, bf16[64,2432]{1,0:T(8,128)(2,1)}, u32[]{:S(2)}, u32[]{:S(2)}) collective-permute-start(bf16[64,2432]{1,0:T(8,128)(2,1)} %add_convert_fusion.4), channel_id=1, source_target_pairs={{0,4},{4,8},{8,12},{12,16},{16,20},{20,24},{24,28},{28,0},{1,5},{5... | collective-permute-start | bytes 933896 | tf_op jit(solution)/shard_map/ppermute | solution.py:216
  46.5 39.0 %all-to-all-start.1 = ((bf16[4,128,3072]{2,1,0:T(8,128)(2,1)}), bf16[4,128,3072]{2,1,0:T(8,128)(2,1)S(1)}, u32[]{:S(2)}, u32[]{:S(2)}) async-start(bf16[4,128,3072]{2,1,0:T(8,128)(2,1)} %bitcast.32), calls=%async_computation.1 | async-start | bytes 6291456 | tf_op jit(solution)/shard_map/all_to_all | solution.py:288
  55.8 6.1 %collective-permute-start.6 = (bf16[64,2432]{1,0:T(8,128)(2,1)S(1)}, bf16[64,2432]{1,0:T(8,128)(2,1)S(1)}, u32[]{:S(2)}, u32[]{:S(2)}) collective-permute-start(bf16[64,2432]{1,0:T(8,128)(2,1)S(1)} %get-tuple-element.41), channel_id=1, source_target_pairs={{0,28},{4,0},{8,4},{12,8},{16,12},{20,16},{24,20},{28,24},{1,29},{... | collective-permute-start | bytes 933896 | tf_op jit(solution)/shard_map/ppermute | solution.py:216
  55.8 8.4 %collective-permute-start.3 = (bf16[64,2432]{1,0:T(8,128)(2,1)S(1)}, bf16[64,2432]{1,0:T(8,128)(2,1)S(1)}, u32[]{:S(2)}, u32[]{:S(2)}) collective-permute-start(bf16[64,2432]{1,0:T(8,128)(2,1)S(1)} %get-tuple-element.40), channel_id=1, source_target_pairs={{0,4},{4,8},{8,12},{12,16},{16,20},{20,24},{24,28},{28,0},{1,5},{5... | collective-permute-start | bytes 933896 | tf_op jit(solution)/shard_map/ppermute | solution.py:216
  62.9 6.1 %collective-permute-start.7 = (bf16[64,2432]{1,0:T(8,128)(2,1)S(1)}, bf16[64,2432]{1,0:T(8,128)(2,1)S(1)}, u32[]{:S(2)}, u32[]{:S(2)}) collective-permute-start(bf16[64,2432]{1,0:T(8,128)(2,1)S(1)} %add_convert_fusion.1), channel_id=1, source_target_pairs={{0,28},{4,0},{8,4},{12,8},{16,12},{20,16},{24,20},{28,24},{1,29},{... | collective-permute-start | bytes 933896 | tf_op jit(solution)/shard_map/ppermute | solution.py:216
  85.4 9.2 %all-to-all-start.3 = ((bf16[4,16,2432]{2,1,0:T(8,128)(2,1)}), bf16[4,16,2432]{2,1,0:T(8,128)(2,1)S(1)}, u32[]{:S(2)}, u32[]{:S(2)}) async-start(bf16[4,16,2432]{2,1,0:T(8,128)(2,1)} %bitcast.38), calls=%async_computation.3 | async-start | bytes 622592 | tf_op jit(solution)/shard_map/all_to_all | solution.py:288
  94.7 22.4 %all-to-all-start.2 = ((bf16[8,16,3072]{2,1,0:T(8,128)(2,1)}), bf16[8,16,3072]{2,1,0:T(8,128)(2,1)S(1)}, u32[]{:S(2)}, u32[]{:S(2)}) async-start(bf16[8,16,3072]{2,1,0:T(8,128)(2,1)} %bitcast.33), calls=%async_computation.2 | async-start | bytes 1572864 | tf_op jit(solution)/shard_map/all_to_all | solution.py:288
  117.8 9.1 %all-to-all-start.6 = ((bf16[4,16,2304]{2,1,0:T(8,128)(2,1)}), bf16[4,16,2304]{2,1,0:T(8,128)(2,1)S(1)}, u32[]{:S(2)}, u32[]{:S(2)}) async-start(bf16[4,16,2304]{2,1,0:T(8,128)(2,1)} %broadcast_in_dim.22), calls=%async_computation.6 | async-start | bytes 589824 | tf_op jit(solution)/shard_map/all_to_all | solution.py:294
  127.0 21.4 %copy-start.2 = (bf16[4,16,2304]{2,1,0:T(8,128)(2,1)}, bf16[4,16,2304]{2,1,0:T(8,128)(2,1)S(1)}, u32[]{:S(2)}) copy-start(bf16[4,16,2304]{2,1,0:T(8,128)(2,1)S(1)} %all-to-all-done.6) | copy-start | bytes 884740
  148.3 34.0 %all-to-all-start.5 = ((bf16[4,128,3200]{2,1,0:T(8,128)(2,1)}), bf16[4,128,3200]{2,1,0:T(8,128)(2,1)S(1)}, u32[]{:S(2)}, u32[]{:S(2)}) async-start(bf16[4,128,3200]{2,1,0:T(8,128)(2,1)} %broadcast_in_dim.21), calls=%async_computation.5 | async-start | bytes 6553600 | tf_op jit(solution)/shard_map/all_to_all | solution.py:294
  152.1 7.3 %collective-permute-start.11 = (bf16[64,2304]{1,0:T(8,128)(2,1)}, bf16[64,2304]{1,0:T(8,128)(2,1)S(1)}, u32[]{:S(2)}, u32[]{:S(2)}) collective-permute-start(bf16[64,2304]{1,0:T(8,128)(2,1)} %bitcast.34), channel_id=1, source_target_pairs={{0,4},{4,8},{8,12},{12,16},{16,20},{20,24},{24,28},{28,0},{1,5},{5... | collective-permute-start | bytes 884744 | tf_op jit(solution)/shard_map/ppermute | solution.py:216
  152.3 7.0 %collective-permute-start.8 = (bf16[64,2304]{1,0:T(8,128)(2,1)}, bf16[64,2304]{1,0:T(8,128)(2,1)S(1)}, u32[]{:S(2)}, u32[]{:S(2)}) collective-permute-start(bf16[64,2304]{1,0:T(8,128)(2,1)} %bitcast.35), channel_id=1, source_target_pairs={{0,28},{4,0},{8,4},{12,8},{16,12},{20,16},{24,20},{28,24},{1,29},{... | collective-permute-start | bytes 884744 | tf_op jit(solution)/shard_map/ppermute | solution.py:216
  159.3 8.2 %copy-start.6 = (bf16[64,2304]{1,0:T(8,128)(2,1)}, bf16[64,2304]{1,0:T(8,128)(2,1)S(1)}, u32[]{:S(2)}) copy-start(bf16[64,2304]{1,0:T(8,128)(2,1)S(1)} %collective-permute-done.11.rest_8_) | copy-start | bytes 884740
  159.3 8.1 %collective-permute-start.12 = (bf16[64,2304]{1,0:T(8,128)(2,1)S(1)}, bf16[64,2304]{1,0:T(8,128)(2,1)S(1)}, u32[]{:S(2)}, u32[]{:S(2)}) collective-permute-start(bf16[64,2304]{1,0:T(8,128)(2,1)S(1)} %collective-permute-done.11.rest_8_), channel_id=1, source_target_pairs={{0,4},{4,8},{8,12},{12,16},{16,20},{20,24},{24,28},{28,0},{1,5},{5... | collective-permute-start | bytes 884744 | tf_op jit(solution)/shard_map/ppermute | solution.py:216
  159.3 10.9 %copy-start.7 = (bf16[64,2304]{1,0:T(8,128)(2,1)}, bf16[64,2304]{1,0:T(8,128)(2,1)S(1)}, u32[]{:S(2)}) copy-start(bf16[64,2304]{1,0:T(8,128)(2,1)S(1)} %collective-permute-done.8.rest_1_) | copy-start | bytes 884740
  159.3 8.1 %collective-permute-start.9 = (bf16[64,2304]{1,0:T(8,128)(2,1)S(1)}, bf16[64,2304]{1,0:T(8,128)(2,1)S(1)}, u32[]{:S(2)}, u32[]{:S(2)}) collective-permute-start(bf16[64,2304]{1,0:T(8,128)(2,1)S(1)} %collective-permute-done.8.rest_1_), channel_id=1, source_target_pairs={{0,28},{4,0},{8,4},{12,8},{16,12},{20,16},{24,20},{28,24},{1,29},{... | collective-permute-start | bytes 884744 | tf_op jit(solution)/shard_map/ppermute | solution.py:216
  167.5 2.8 %copy-start.8 = (bf16[64,2304]{1,0:T(8,128)(2,1)}, bf16[64,2304]{1,0:T(8,128)(2,1)S(1)}, u32[]{:S(2)}) copy-start(bf16[64,2304]{1,0:T(8,128)(2,1)S(1)} %collective-permute-done.12.rest_7_) | copy-start | bytes 884740
  167.5 7.2 %collective-permute-start.13 = (bf16[64,2304]{1,0:T(8,128)(2,1)S(1)}, bf16[64,2304]{1,0:T(8,128)(2,1)S(1)}, u32[]{:S(2)}, u32[]{:S(2)}) collective-permute-start(bf16[64,2304]{1,0:T(8,128)(2,1)S(1)} %collective-permute-done.12.rest_7_), channel_id=1, source_target_pairs={{0,4},{4,8},{8,12},{12,16},{16,20},{20,24},{24,28},{28,0},{1,5},{5... | collective-permute-start | bytes 884744 | tf_op jit(solution)/shard_map/ppermute | solution.py:216
  167.5 12.8 %copy-start.9 = (bf16[64,2304]{1,0:T(8,128)(2,1)}, bf16[64,2304]{1,0:T(8,128)(2,1)S(1)}, u32[]{:S(2)}) copy-start(bf16[64,2304]{1,0:T(8,128)(2,1)S(1)} %collective-permute-done.9.rest_2_) | copy-start | bytes 884740
  167.5 7.3 %collective-permute-start.10 = (bf16[64,2304]{1,0:T(8,128)(2,1)S(1)}, bf16[64,2304]{1,0:T(8,128)(2,1)S(1)}, u32[]{:S(2)}, u32[]{:S(2)}) collective-permute-start(bf16[64,2304]{1,0:T(8,128)(2,1)S(1)} %collective-permute-done.9.rest_2_), channel_id=1, source_target_pairs={{0,28},{4,0},{8,4},{12,8},{16,12},{20,16},{24,20},{28,24},{1,29},{... | collective-permute-start | bytes 884744 | tf_op jit(solution)/shard_map/ppermute | solution.py:216
  174.7 5.6 %copy-start.4 = (bf16[64,2304]{1,0:T(8,128)(2,1)}, bf16[64,2304]{1,0:T(8,128)(2,1)S(1)}, u32[]{:S(2)}) copy-start(bf16[64,2304]{1,0:T(8,128)(2,1)S(1)} %collective-permute-done.13.rest_6_) | copy-start | bytes 884740
  174.7 5.6 %collective-permute-start.14 = (bf16[32,2304]{1,0:T(8,128)(2,1)S(1)}, bf16[32,2304]{1,0:T(8,128)(2,1)S(1)}, u32[]{:S(2)}, u32[]{:S(2)}) collective-permute-start(bf16[32,2304]{1,0:T(8,128)(2,1)S(1)} %slice.96), channel_id=1, source_target_pairs={{0,4},{4,8},{8,12},{12,16},{16,20},{20,24},{24,28},{28,0},{1,5},{5... | collective-permute-start | bytes 442376 | tf_op jit(solution)/shard_map/ppermute | solution.py:216
  174.8 5.5 %copy-start.5 = (bf16[64,2304]{1,0:T(8,128)(2,1)}, bf16[64,2304]{1,0:T(8,128)(2,1)S(1)}, u32[]{:S(2)}) copy-start(bf16[64,2304]{1,0:T(8,128)(2,1)S(1)} %collective-permute-done.10.rest_3_) | copy-start | bytes 884740
  174.8 5.5 %collective-permute-start.15 = (bf16[32,2304]{1,0:T(8,128)(2,1)S(1)}, bf16[32,2304]{1,0:T(8,128)(2,1)}, u32[]{:S(2)}, u32[]{:S(2)}) collective-permute-start(bf16[32,2304]{1,0:T(8,128)(2,1)S(1)} %slice.97), channel_id=1, source_target_pairs={{0,28},{4,0},{8,4},{12,8},{16,12},{20,16},{24,20},{28,24},{1,29},{... | collective-permute-start | bytes 442376 | tf_op jit(solution)/shard_map/ppermute | solution.py:216
  180.3 2.1 copy-start.10
  182.4 1.7 copy-start
  191.3 24.5 %all-to-all-start.7 = ((bf16[8,64,640]{2,1,0:T(8,128)(2,1)}), bf16[8,64,640]{2,1,0:T(8,128)(2,1)S(1)}, u32[]{:S(2)}, u32[]{:S(2)}) async-start(bf16[8,64,640]{2,1,0:T(8,128)(2,1)} %bitcast.39), calls=%async_computation.7 | async-start | bytes 1310720 | tf_op jit(solution)/shard_map/all_to_all | solution.py:360
  (2 other events, 1.7 us)

commit v3 on v2

v3 whole, which is shorter than its diff:
```python
import jax
import jax.numpy as jnp
from jax import lax
from jax.experimental import pallas as pl
from jax.experimental.pallas import tpu as pltpu
from jax.sharding import Mesh
from jax.sharding import PartitionSpec as P

D = 8192
BLK = 128
NZ, NX = 8, 4
HA, HB = 768, 1024
COL = ("col_0", "col_1")
ALL = ("row", "col_0", "col_1")
norm_eps = 1e-05

f32 = jnp.float32
bf16 = jnp.bfloat16


def vmem():
    return pl.BlockSpec(memory_space=pltpu.VMEM)


def smem():
    return pl.BlockSpec(memory_space=pltpu.SMEM)


def call(kernel, outs, in_specs, scratch, flops, nbytes, args, mib=40, grid=()):
    whole = [pl.BlockSpec(o.shape, lambda *_, n=len(o.shape): (0,) * n) for o in outs]
    return pl.pallas_call(
        kernel,
        out_shape=outs,
        grid=grid,
        in_specs=in_specs,
        out_specs=tuple(whole if grid else [vmem() for _ in outs]),
        scratch_shapes=scratch,
        compiler_params=pltpu.CompilerParams(vmem_limit_bytes=mib * 1024 * 1024),
        cost_estimate=pl.CostEstimate(flops=flops, bytes_accessed=nbytes, transcendentals=0),
    )(*args)


def nn(a, b):
    return jnp.dot(a, b, preferred_element_type=f32)


def nt(a, b):
    return lax.dot_general(a, b, (((1,), (1,)), ((), ())), preferred_element_type=f32)


def tn(a, b):
    return lax.dot_general(a, b, (((0,), (0,)), ((), ())), preferred_element_type=f32)


def parts3(v):
    hi = v.astype(bf16)
    rest = v - hi.astype(f32)
    mid = rest.astype(bf16)
    return hi, mid, (rest - mid.astype(f32)).astype(bf16)


def lane_sum(block, at):
    return sum(block[:, i : i + 1].astype(f32) for i in range(at, at + 3))


def pieces_of_tokens(pos):
    for tz in range(NZ):
        k = lax.rem(tz - pos[1] + NZ, NZ)
        for tx in range(NX):
            j = lax.rem(tx - pos[2] + NX, NX)
            nat = slice(tz * 64 + tx * 16, tz * 64 + tx * 16 + 16)
            in_a = slice((tx * NZ + tz) * 16, (tx * NZ + tz) * 16 + 16)
            in_b = pl.ds(pl.multiple_of(k * 64 + j * 16, 16), 16)
            yield nat, in_a, in_b


def masks_kernel(mg, mu, md, wg, wu, wd, ag, au, ad, bg, bu, bd):
    for w, m, ea, eb, down in ((wg, mg, ag, bg, 0), (wu, mu, au, bu, 0), (wd, md, ad, bd, 1)):
        for a in range(w.shape[0] // BLK):
            for b in range(w.shape[1] // BLK):
                r, c = slice(a * BLK, (a + 1) * BLK), slice(b * BLK, (b + 1) * BLK)
                v = w[r, c] * m[a, b].astype(f32).astype(bf16)
                at = (a if down else b) * BLK
                to = slice(at % HA, at % HA + BLK) if at < HA else slice(at - HA, at - HA + BLK)
                e = ea if at < HA else eb
                if down:
                    e[to, c] = v
                else:
                    e[r, to] = v


def products(left, tok, eff, part, to, half):
    width = left.shape[1] // 2
    x, g = left[tok, :width], left[tok, width:]
    part[to, :half] = nn(x, eff[0][...]).astype(bf16)
    part[to, half : 2 * half] = nn(x, eff[1][...]).astype(bf16)
    part[to, 2 * half : 3 * half] = nt(g, eff[2][...]).astype(bf16)


def scaled(rows, nat, gain):
    width = gain.shape[1]
    return (rows[nat, :width].astype(f32) * gain[...]).astype(bf16)


def square_sums(rows, nat, width):
    sq = jnp.square(rows[nat, :width].astype(f32))
    return (sq[:, :BLK] + sq[:, BLK:]).astype(bf16)


def far_kernel(pos, rows, gain, eg, eu, ed, far_r, far_l, left):
    width = gain.shape[1]
    tz = lax.rem(pos[1] + NZ // 2, NZ)
    for j in range(NX):
        nat = pl.ds(pl.multiple_of(tz * 64 + lax.rem(pos[2] + j, NX) * 16, 16), 16)
        to = slice(j * 16, j * 16 + 16)
        left[to, :width] = scaled(rows, nat, gain)
        left[to, width:] = rows[nat, width:]
        far, at = (far_r, j * 16) if j < 2 else (far_l, j * 16 - 32)
        far[at : at + 16, 3 * HB :] = square_sums(rows, nat, width)
    x, g = left[:, :width], left[:, width:]
    for p, at in ((nn(x, eg[...]), 0), (nn(x, eu[...]), HB), (nt(g, ed[...]), 2 * HB)):
        far_r[:, at : at + HB] = p[:32].astype(bf16)
        far_l[:, at : at + HB] = p[32:].astype(bf16)


def part_a_kernel(rows, gain, eg, eu, ed, part, left):
    width = gain.shape[1]
    for tz in range(NZ):
        for tx in range(NX):
            nat = slice(tz * 64 + tx * 16, tz * 64 + tx * 16 + 16)
            to = slice((tx * NZ + tz) * 16, (tx * NZ + tz) * 16 + 16)
            left[to, :width] = scaled(rows, nat, gain)
            left[to, width:] = rows[nat, width:]
    for t in range(0, left.shape[0], 128):
        products(left, slice(t, t + 128), (eg, eu, ed), part, slice(t, t + 128), HA)


def part_b_kernel(pos, rows, gain, eg, eu, ed, part, left):
    width = gain.shape[1]
    for nat, _, to in pieces_of_tokens(pos):
        left[to, :width] = scaled(rows, nat, gain)
        left[to, width:] = rows[nat, width:]
        part[to, 3 * HB :] = square_sums(rows, nat, width)
    for t, n in ((192, 64), (320, 64), (64, 128), (384, 128), (0, 64)):
        products(left, slice(t, t + n), (eg, eu, ed), part, slice(t, t + n), HB)


def ring_first_kernel(right, left, piece_r, piece_l, out_r, out_l):
    h = right.shape[0]
    out_r[:h] = (piece_r[:h].astype(f32) + right[...].astype(f32)).astype(bf16)
    out_r[h:] = piece_r[h:]
    out_l[:h] = piece_l[:h]
    out_l[h:] = (piece_l[h:].astype(f32) + left[...].astype(f32)).astype(bf16)


def ring_kernel(right, left, piece_r, piece_l, *rest):
    out_r, out_l = rest[-2:]
    out_r[...] = (piece_r[...].astype(f32) + right[...].astype(f32)).astype(bf16)
    out_l[...] = (piece_l[...].astype(f32) + left[...].astype(f32)).astype(bf16)


def ring_last_kernel(right, left, piece, own, *others):
    for j, out in enumerate((own, *others)):
        at = slice(j * 16, j * 16 + 16)
        v = piece[at].astype(f32) + right[at].astype(f32) + left[at].astype(f32)
        out[...] = v.astype(out.dtype)


def hidden_grads(sums, half, scale, to_act, to_gate, to_up):
    dots = jnp.zeros((16, BLK), f32)
    for c in range(0, half, BLK):
        gate = sums(c) * scale
        up = sums(half + c) * scale
        act_grad = sums(2 * half + c)
        sig = jax.nn.sigmoid(gate)
        act = (gate * sig * up).astype(bf16)
        gate_grad = (act_grad * up * sig * (1.0 + gate * (1.0 - sig))).astype(bf16)
        up_grad = (act_grad * gate * sig).astype(bf16)
        to_act(c, act)
        to_gate(c, gate_grad)
        to_up(c, up_grad)
        dots += gate_grad.astype(f32) * gate + up_grad.astype(f32) * up
    return dots


def grads_b_kernel(own, j1, j2, j3, send, scale, dots):
    def sums(c):
        at = slice(c, c + BLK)
        v = own[:, at]
        for j in (j1, j2, j3):
            v = v + j[:, at].astype(f32)
        return v

    def store(at):
        def put(c, v):
            send[:, at + c : at + c + BLK] = v

        return put

    squares = jnp.sum(sums(3 * HB), axis=1, keepdims=True)
    sc = lax.rsqrt(squares / D + norm_eps)
    scale[...] = jnp.broadcast_to(sc, scale.shape)
    dots[...] = hidden_grads(sums, HB, sc, store(0), store(HB), store(2 * HB))


def grads_a_kernel(got, scale, dots_b, copies):
    def sums(c):
        return jnp.sum(got[:, :, c : c + BLK].astype(f32), axis=0)

    def store(at):
        def put(c, v):
            for n in range(NZ):
                copies[n, :, at + c : at + c + BLK] = v

        return put

    sc = scale[:, :1]
    dots = dots_b[...] + hidden_grads(sums, HA, sc, store(0), store(HA), store(2 * HA))
    lane = lax.broadcasted_iota(jnp.int32, (16, BLK), 1)
    extra = jnp.zeros((16, BLK), f32)
    for i, v in enumerate(parts3(sc) + parts3(jnp.sum(dots, axis=1, keepdims=True))):
        extra = jnp.where(lane == i, v.astype(f32), extra)
    store(3 * HA)(0, extra.astype(bf16))


def fetch_pieces(pieces, gb, sems):
    copies, at = [], 0
    for i, p in enumerate(pieces):
        copies.append(pltpu.make_async_copy(p, gb.at[pl.ds(at, p.shape[0])], sems.at[i]))
        copies[-1].start()
        at += p.shape[0]
    return copies


def features_kernel(pos, rows, ga, ag, au, ad, bg, bu, bd, *rest):
    pieces, (both, own_scale, gb, da, na, db, nb, sems) = rest[:-8], rest[-8:]
    copies = fetch_pieces(pieces, gb, sems)
    width = ag.shape[0]
    for hid, d, n, (eg, eu, ed), half in (
        (ga, da, na, (ag, au, ad), HA),
        (gb, db, nb, (bg, bu, bd), HB),
    ):
        if hid is gb:
            for c in copies:
                c.wait()
        for t in range(0, hid.shape[0], 128):
            tok = slice(t, t + 128)
            d[tok, :] = nn(hid[tok, :half], ed[...])
            n[tok, :] = nt(hid[tok, half : 2 * half], eg[...]) + nt(
                hid[tok, 2 * half : 3 * half], eu[...]
            )
    total = jnp.zeros((16, width), f32)
    for nat, in_a, in_b in pieces_of_tokens(pos):
        extra = ga[in_a, 3 * HA :]
        both[nat, :width] = (da[in_a, :] + db[in_b, :]).astype(bf16)
        grad = na[in_a, :] + nb[in_b, :]
        both[nat, width : 2 * width] = grad.astype(bf16)
        total += grad * rows[nat, :width].astype(f32) * lane_sum(extra, 0)
    gain_row = jnp.sum(total, axis=0, keepdims=True)
    lane = lax.broadcasted_iota(jnp.int32, (64, BLK), 1)
    line = lax.broadcasted_iota(jnp.int32, (64, BLK), 0)
    shared = jnp.zeros((64, BLK), f32)
    for c in range(width // 64):
        half_row = gain_row[:, (c // 2) * BLK : (c // 2 + 1) * BLK]
        picked = jnp.where(lane == line + 64 * (c % 2), half_row, 0.0)
        for i, v in enumerate(parts3(jnp.sum(picked, axis=1, keepdims=True))):
            shared = jnp.where(lane == 3 + 3 * c + i, v.astype(f32), shared)
    shared = shared.astype(bf16)
    lane16 = lax.broadcasted_iota(jnp.int32, (16, BLK), 1)
    for tz in range(NZ):
        for tx in range(NX):
            nat = slice(tz * 64 + tx * 16, tz * 64 + tx * 16 + 16)
            extra = ga[(tx * NZ + tz) * 16 : (tx * NZ + tz) * 16 + 16, 3 * HA :].astype(f32)
            moved = jnp.where(lane16 < 3, pltpu.roll(extra, BLK - 3, 1), 0.0)
            both[nat, 2 * width :] = shared[tx * 16 : tx * 16 + 16, :] + moved.astype(bf16)
    for tx in range(NX):
        at = pl.ds(pl.multiple_of(tx * 128 + pos[0] * 16, 16), 16)
        s = lane_sum(ga[at, 3 * HA :], 0)
        own_scale[tx * 16 : tx * 16 + 16, :] = jnp.broadcast_to(s, (16, BLK))


def weights_kernel(pos, mg, mu, md, rows, gain, ga, *rest):
    pieces, (out_g, out_u, out_d, gb, la, lb, sems) = rest[:-7], rest[-7:]
    copies = fetch_pieces(pieces, gb, sems)
    width = gain.shape[1]
    for nat, in_a, in_b in pieces_of_tokens(pos):
        scale = lane_sum(ga[in_a, 3 * HA :], 0)
        x = (rows[nat, :width].astype(f32) * scale * gain[...]).astype(bf16)
        g = rows[nat, width:]
        la[in_a, :width] = x
        lb[in_b, :width] = x
        la[in_a, width:] = g
        lb[in_b, width:] = g
    for hid, left, at, half in ((ga, la, 0, HA), (gb, lb, HA, HB)):
        if at:
            for c in copies:
                c.wait()
        normed, grad = left[:, :width], left[:, width:]
        for c in range(0, half, BLK):
            b = (at + c) // BLK
            gw = tn(normed, hid[:, half + c : half + c + BLK])
            uw = tn(normed, hid[:, 2 * half + c : 2 * half + c + BLK])
            dw = tn(hid[:, c : c + BLK], grad)
            to = slice(at + c, at + c + BLK)
            for a in range(width // BLK):
                r = slice(a * BLK, (a + 1) * BLK)
                out_g[r, to] = (gw[r, :] * mg[a, b].astype(f32)).astype(bf16)
                out_u[r, to] = (uw[r, :] * mu[a, b].astype(f32)).astype(bf16)
                out_d[to, r] = (dw[:, r] * md[b, a].astype(f32)).astype(bf16)


def final_kernel(got, x, grad, gain, scale, layer_out, input_grad, gain_grad):
    width = gain.shape[1]
    s = got[0].astype(f32)
    for r in range(1, got.shape[0]):
        s = s + got[r].astype(f32)
    xf = x[...].astype(f32)
    layer_out[...] = (xf + s[:, :width]).astype(bf16)
    extra = s[:, 2 * width :]
    dots = lane_sum(extra, 0)
    sc = scale[:, :1]
    input_grad[...] = (
        grad[...].astype(f32)
        + sc * gain[...] * s[:, width : 2 * width]
        - xf * sc * sc * (dots / D)
    ).astype(bf16)
    lane = lax.broadcasted_iota(jnp.int32, (64, BLK), 1)
    line = lax.broadcasted_iota(jnp.int32, (64, BLK), 0)
    for h in range(width // BLK):
        spread = jnp.where(
            lane < 64,
            jnp.where(lane == line, lane_sum(extra, 3 + 6 * h), 0.0),
            jnp.where(lane == line + 64, lane_sum(extra, 6 + 6 * h), 0.0),
        )
        gain_grad[:, h * BLK : (h + 1) * BLK] = jnp.sum(spread, axis=0, keepdims=True)


def send(v, axis, step):
    n = lax.axis_size(axis)
    return lax.ppermute(v, axis, [(i, (i + step) % n) for i in range(n)])


def ring_sum(far, part, gate_on):
    wide = part.shape[1]

    def piece(k):
        return pl.BlockSpec((64, wide), lambda i: (k, 0))

    block = jax.ShapeDtypeStruct((64, wide), bf16)
    right, left = (send(v, "col_0", s) for v, s in zip(far, (1, -1)))
    for away in range(NZ // 2 - 1, 0, -1):
        first, last = away == NZ // 2 - 1, away == 1
        got = pl.BlockSpec(right.shape, lambda i: (0, 0))
        right, left = call(
            ring_first_kernel if first else ring_kernel,
            (block, block),
            [got, got, piece(away), piece(NZ - away)]
            + ([pl.BlockSpec(memory_space=pl.ANY)] if last else []),
            [],
            0,
            2_500_000,
            (right, left, part, part) + ((gate_on,) if last else ()),
            mib=16,
            grid=(1,),
        )
        right, left = send(right, "col_0", 1), send(left, "col_0", -1)
    got = pl.BlockSpec(right.shape, lambda i: (0, 0))
    return call(
        ring_last_kernel,
        (
            jax.ShapeDtypeStruct((16, wide), f32),
            *[jax.ShapeDtypeStruct((16, wide), bf16)] * (NX - 1),
        ),
        [got, got, piece(0)],
        [],
        0,
        2_000_000,
        (right, left, part),
        mib=16,
        grid=(1,),
    )


def ring_gather(shard, axis):
    n = lax.axis_size(axis)
    h = shard.shape[0] // 2
    from_right, from_left = [], []
    right = left = shard
    for _ in range(1, n // 2):
        right, left = send(right, axis, 1), send(left, axis, -1)
        from_left.insert(0, right)
        from_right.append(left)
    far = [send(right[:h], axis, 1), send(left[h:], axis, -1)]
    return [shard, *from_right, *far, *from_left]


def from_everyone(shard, axis):
    copies = jnp.broadcast_to(shard, (lax.axis_size(axis), *shard.shape))
    got = lax.all_to_all(copies, axis, split_axis=0, concat_axis=0, tiled=True)
    return got.reshape(-1, shard.shape[-1])


def shape(v):
    return jax.ShapeDtypeStruct(v.shape, v.dtype)


def shards(layer_input, norm_gain, w_gate, w_up, w_down, mask_gate, mask_up, mask_down, out_grad):
    pos = jnp.stack([lax.axis_index(a) for a in ALL]).astype(jnp.int32)
    gain = norm_gain[None, :]
    mine, width = layer_input.shape
    rows = from_everyone(jnp.concatenate([layer_input, out_grad], axis=1), "row")
    tokens = rows.shape[0]
    flops = 2 * tokens * width * 3
    a_cols, b_cols = 3 * HA, 3 * HB + BLK

    def out(*dims, dtype=bf16):
        return jax.ShapeDtypeStruct(dims, dtype)

    eff = call(
        masks_kernel,
        (*[out(width, HA)] * 2, out(HA, width), *[out(width, HB)] * 2, out(HB, width)),
        [smem()] * 3 + [vmem()] * 3,
        [],
        0,
        6_000_000,
        (mask_gate, mask_up, mask_down, w_gate, w_up, w_down),
    )
    eff_a, eff_b = eff[:3], eff[3:]
    far = call(
        far_kernel,
        (out(32, b_cols), out(32, b_cols)),
        [smem()] + [vmem()] * 5,
        [pltpu.VMEM((64, 2 * width), bf16)],
        flops * HB // 8,
        2_000_000,
        (pos, rows, gain, *eff_b),
    )
    left = pltpu.VMEM((tokens, 2 * width), bf16)
    (part_a,) = call(
        part_a_kernel,
        (out(tokens, a_cols),),
        [vmem()] * 5,
        [left],
        flops * HA,
        4_000_000,
        (rows, gain, *eff_a),
    )
    (part_b,) = call(
        part_b_kernel,
        (out(tokens, b_cols),),
        [smem()] + [vmem()] * 5,
        [left],
        flops * HB,
        5_000_000,
        (pos, rows, gain, *eff_b),
    )
    got_a = lax.all_to_all(part_a.reshape(NX, -1, a_cols), "col_1", 0, 0, tiled=True)
    own, *others = ring_sum(far, part_b, got_a)
    got_b = [send(v, "col_1", j) for j, v in enumerate(others, 1)]
    sum_a = jnp.sum(got_a.astype(f32), axis=0).astype(bf16).reshape(NZ, -1, a_cols)
    got_a = lax.all_to_all(sum_a, "col_0", 0, 0, tiled=True)
    send_b, scale, dots_b = call(
        grads_b_kernel,
        (out(16, 3 * HB), out(16, BLK, dtype=f32), out(16, BLK, dtype=f32)),
        [vmem()] * 4,
        [],
        0,
        600_000,
        (own, *got_b),
        mib=16,
    )
    (copies_a,) = call(
        grads_a_kernel,
        (out(NZ, 16, a_cols + BLK),),
        [vmem()] * 3,
        [],
        0,
        1_500_000,
        (got_a, scale, dots_b),
        mib=16,
    )
    near = [send_b] + [send(send_b, "col_1", -j) for j in range(1, NX)]
    pieces_b = ring_gather(jnp.concatenate(near), "col_0")
    all_a = lax.all_to_all(copies_a, "col_0", 0, 0, tiled=True).reshape(-1, a_cols + BLK)
    all_a = from_everyone(all_a, "col_1")

    anywhere = [pl.BlockSpec(memory_space=pl.ANY)] * len(pieces_b)
    gb = pltpu.VMEM((tokens, 3 * HB), bf16)
    sems = pltpu.SemaphoreType.DMA((len(pieces_b),))
    both, own_scale = call(
        features_kernel,
        (out(tokens, 2 * width + BLK), out(mine, BLK, dtype=f32)),
        [smem()] + [vmem()] * 8 + anywhere,
        [gb, *[pltpu.VMEM((tokens, width), f32)] * 4, sems],
        flops * (HA + HB),
        9_000_000,
        (pos, rows, all_a, *eff_a, *eff_b, *pieces_b),
    )
    got = lax.all_to_all(both.reshape(-1, mine, both.shape[1]), "row", 0, 0, tiled=True)
    gate_wgrad, up_wgrad, down_wgrad = call(
        weights_kernel,
        (shape(w_gate), shape(w_up), shape(w_down)),
        [smem()] * 4 + [vmem()] * 3 + anywhere,
        [gb, left, left, sems],
        flops * (HA + HB),
        9_000_000,
        (pos, mask_gate, mask_up, mask_down, rows, gain, all_a, *pieces_b),
    )
    layer_out, input_grad, gain_grad = call(
        final_kernel,
        (shape(layer_input), shape(out_grad), shape(gain)),
        [vmem()] * 5,
        [],
        0,
        1_000_000,
        (got, layer_input, out_grad, gain, own_scale),
        mib=16,
    )
    return (layer_out, input_grad, gain_grad[0], gate_wgrad, up_wgrad, down_wgrad)


def solution(mesh):
    torus = Mesh(mesh.devices.reshape(mesh.shape["row"], NZ, NX), ALL)
    placed = (
        P("row", COL),
        P(COL),
        P(COL, "row"),
        P(COL, "row"),
        P("row", COL),
        P(COL, "row"),
        P(COL, "row"),
        P("row", COL),
        P("row", COL),
    )
    return jax.shard_map(
        shards,
        mesh=torus,
        in_specs=placed,
        out_specs=(
            P("row", COL),
            P("row", COL),
            P(COL),
            P(COL, "row"),
            P(COL, "row"),
            P("row", COL),
        ),
        check_vma=False,
    )
```

time: 220 us -> 228 us (1.036)
  local copies, waits for them, and re-layouts: 9.61 us -> 45.6 us
  blocking collectives: 19.4 us -> 0 us
  waiting for transfers between devices: 89.3 us -> 77.4 us
  starting transfers between devices: 61 us -> 69.6 us
  other arithmetic: 11.6 us -> 3.85 us
    unnamed x24 -> x114, local copies, waits for them, and re-layouts: 4.83 us -> 41.6 us
    all_to_all x1 -> x0, blocking collectives: 19.4 us -> none  [from_everyone(): got = lax.all_to_all(copies, axis, split_axis=0, concat_axis=0, tiled=True)]
    all_to_all x3, waiting for transfers between devices: 36.4 us -> 24.1 us  [the longest x1 12.2 us: shards(): lax.all_to_all(copies_a, 'col_0', 0, 0, tiled=True)]
    ppermute x16 -> x22, waiting for transfers between devices: 38.9 us -> 50.8 us  [send(): return lax.ppermute(v, axis, [(i, (i + step) % n) for i in range(n)])]
    ppermute x16 -> x22, starting transfers between devices: 21.8 us -> 30.5 us  [send(): return lax.ppermute(v, axis, [(i, (i + step) % n) for i in range(n)])]
    all_to_all x3 -> x2, waiting for transfers between devices: 11 us -> 2.46 us  [from_everyone(): got = lax.all_to_all(copies, axis, split_axis=0, concat_axis=0, tiled=True)]
    convert_element_type x5 -> x0, other arithmetic: 7.04 us -> none  [the longest x3 4.13 us: plus(): return (up32(piece) + up32(got)).astype(bf16)]
    all_to_all x3, starting transfers between devices: 11.8 us -> 17.2 us  [the longest x1 7.5 us: shards(): got_a = lax.all_to_all(sum_a, 'col_0', 0, 0, tiled=True)]
  transfers between devices with their start and end apart: 23 -> 28, of which waited for: 16 -> 13; matrix products, arithmetic and copies ran while one was open for 5% -> 5% of each run, Pallas kernels for 5% -> 7%
where the time goes in v3:
time: 228 us; the launch traced here: 225 us
  waiting for transfers between devices  77.4 us (34%)
  starting transfers between devices  69.6 us (31%)
  local copies, waits for them, and re-layouts  45.6 us (20%)
  Pallas kernels  27.4 us (12%)
  other arithmetic  3.85 us (2%)
    ppermute x22, waiting for transfers between devices, send(): return lax.ppermute(v, axis, [(i, (i + step) % n) for i in range(n)])  50.8 us
    unnamed x114, local copies, waits for them, and re-layouts  41.6 us
    ppermute x22, starting transfers between devices, send(): return lax.ppermute(v, axis, [(i, (i + step) % n) for i in range(n)])  30.5 us
    pallas_call x13, Pallas kernels, call(): pl.pallas_call(kernel, out_shape=outs, grid=grid, in_specs=in_specs, out_...  27.4 us
    all_to_all x1, waiting for transfers between devices, shards(): lax.all_to_all(copies_a, 'col_0', 0, 0, tiled=True)  12.2 us
    all_to_all x1, waiting for transfers between devices, shards(): lax.all_to_all(part_a.reshape(NX, -1, a_cols), 'col_1', 0, 0, tiled=True)  11.9 us
    all_to_all x1, starting transfers between devices, shards(): lax.all_to_all(both.reshape(-1, mine, both.shape[1]), 'row', 0, 0, tiled=...  11.5 us
    all_to_all x2, starting transfers between devices, from_everyone(): got = lax.all_to_all(copies, axis, split_axis=0, concat_axis=0, tiled=True)  10.4 us
  transfers between devices with their start and end apart: 28, of which 13 were waited for; matrix products, arithmetic and copies ran while one was open for 5% of the time, Pallas kernels for 7%

profile of v3, /device:TPU:1, one launch (start us, length us, event | category | flops | bytes accessed | tf_op | source)
XLA Modules:
  0.0 224.9 jit_solution(17559585125005887162)
XLA Ops:
  2.3 6.6 %all-to-all-start = ((bf16[8,64,512]{2,1,0:T(8,128)(2,1)}), bf16[8,64,512]{2,1,0:T(8,128)(2,1)S(1)}, u32[]{:S(2)}, u32[]{:S(2)}) async-start(bf16[8,64,512]{2,1,0:T(8,128)(2,1)} %broadcast_in_dim.9), calls=%async_computation | async-start | bytes 1048576 | tf_op jit(solution)/shard_map/all_to_all | solution.py:399
  15.9 2.5 %all-to-all-done = bf16[8,64,512]{2,1,0:T(8,128)(2,1)S(1)} async-done(((bf16[8,64,512]{2,1,0:T(8,128)(2,1)}), bf16[8,64,512]{2,1,0:T(8,128)(2,1)S(1)}, u32[]{:S(2)}, u32[]{:S(2)}) %all-to-all-start) | async-done | bytes 524320 | tf_op jit(solution)/shard_map/all_to_all | solution.py:399
  18.4 2.5 %shard_map.137 = bf16[512,2304]{1,0:T(8,128)(2,1)} custom-call(bf16[512,512]{1,0:T(8,128)(2,1)S(1)} %bitcast.13, f32[1,256]{1,0:T(1,128)S(1)} %bitcast.19, bf16[256,768]{1,0:T(8,128)(2,1)S(1)} %get-tuple-element.35.eg.ag, bf16[256,768]{1,0:T(8,128)(2,1)S(1)} %get-tuple-element.36.eu.au, bf16[768,256]{1,0:T(8,128)(2,1)S(1)} %get-tuple-element.37.ed.ad), custom_call_target="tpu_custom_call" | custom-call | flops 603979776 | bytes 4000000 | tf_op jit(solution)/shard_map/pallas_call | solution.py:31
  20.9 4.5 %all-to-all-start.1 = ((bf16[4,128,2304]{2,1,0:T(8,128)(2,1)}), bf16[4,128,2304]{2,1,0:T(8,128)(2,1)}, u32[]{:S(2)}, u32[]{:S(2)}) async-start(bf16[4,128,2304]{2,1,0:T(8,128)(2,1)} %bitcast.5), calls=%async_computation.1 | async-start | bytes 4718592 | tf_op jit(solution)/shard_map/all_to_all | solution.py:457
  27.6 4.0 %collective-permute-start.1 = (bf16[32,3200]{1,0:T(8,128)(2,1)S(1)}, bf16[32,3200]{1,0:T(8,128)(2,1)S(1)}, u32[]{:S(2)}, u32[]{:S(2)}) collective-permute-start(bf16[32,3200]{1,0:T(8,128)(2,1)S(1)} %get-tuple-element.42), channel_id=1, source_target_pairs={{0,28},{4,0},{8,4},{12,8},{16,12},{20,16},{24,20},{28,24},{1,29},{... | collective-permute-start | bytes 614408 | tf_op jit(solution)/shard_map/ppermute | solution.py:340
  35.8 2.4 %shard_map.139.piece_r.piece_l.piece = bf16[512,3200]{1,0:T(8,128)(2,1)S(1)} custom-call(s32[3]{0:T(128)S(1)} %pad_add_fusion.pos, bf16[512,512]{1,0:T(8,128)(2,1)S(1)} %bitcast.15, f32[1,256]{1,0:T(1,128)S(1)} %bitcast.21, bf16[256,1024]{1,0:T(8,128)(2,1)S(1)} %copy-done.4, bf16[256,1024]{1,0:T(8,128)(2,1)S(1)} %copy-done.7, bf16[1024,256]{1,0:T(8,128)(2,1)S(1)} %copy-done.10), custom_call_target="tpu_custom_call" | custom-call | flops 805306368 | bytes 5000000 | tf_op jit(solution)/shard_map/pallas_call | solution.py:31
  39.2 2.7 %collective-permute-start.3 = (bf16[64,3200]{1,0:T(8,128)(2,1)}, bf16[64,3200]{1,0:T(8,128)(2,1)}, u32[]{:S(2)}, u32[]{:S(2)}) collective-permute-start(bf16[64,3200]{1,0:T(8,128)(2,1)} %get-tuple-element.44), channel_id=1, source_target_pairs={{0,28},{4,0},{8,4},{12,8},{16,12},{20,16},{24,20},{28,24},{1,29},{... | collective-permute-start | bytes 1228808 | tf_op jit(solution)/shard_map/ppermute | solution.py:340
  41.9 11.9 %all-to-all-done.1.rest_0_ = bf16[4,128,2304]{2,1,0:T(8,128)(2,1)} async-done(((bf16[4,128,2304]{2,1,0:T(8,128)(2,1)}), bf16[4,128,2304]{2,1,0:T(8,128)(2,1)}, u32[]{:S(2)}, u32[]{:S(2)}) %all-to-all-start.1) | async-done | bytes 2359328 | tf_op jit(solution)/shard_map/all_to_all | solution.py:457
  53.8 3.0 %reduce_sum.12 = bf16[128,2304]{1,0:T(8,128)(2,1)} reduce(bf16[4,128,2304]{2,1,0:T(8,128)(2,1)} %all-to-all-done.1.rest_0_, bf16[]{:T(256)} %constant.15.clone.1), dimensions={0}, to_apply=%region_0.0 | reduce | flops 884736 | bytes 2949122 | tf_op jit(solution)/shard_map/reduce_sum | solution.py:460
  56.8 7.5 %all-to-all-start.2 = ((bf16[8,16,2304]{2,1,0:T(8,128)(2,1)}), bf16[8,16,2304]{2,1,0:T(8,128)(2,1)}, u32[]{:S(2)}, u32[]{:S(2)}) async-start(bf16[8,16,2304]{2,1,0:T(8,128)(2,1)} %bitcast.25), calls=%async_computation.2 | async-start | bytes 1179648 | tf_op jit(solution)/shard_map/all_to_all | solution.py:461
  68.5 20.3 %collective-permute-done.4.right = bf16[64,3200]{1,0:T(8,128)(2,1)S(1)} collective-permute-done((bf16[64,3200]{1,0:T(8,128)(2,1)S(1)}, bf16[64,3200]{1,0:T(8,128)(2,1)S(1)}, u32[]{:S(2)}, u32[]{:S(2)}) %collective-permute-start.4) | collective-permute-done | bytes 409632 | tf_op jit(solution)/shard_map/ppermute | solution.py:340
  89.1 2.7 %collective-permute-start.7 = (bf16[64,3200]{1,0:T(8,128)(2,1)S(1)}, bf16[64,3200]{1,0:T(8,128)(2,1)S(1)}, u32[]{:S(2)}, u32[]{:S(2)}) collective-permute-start(bf16[64,3200]{1,0:T(8,128)(2,1)S(1)} %get-tuple-element.48), channel_id=1, source_target_pairs={{0,28},{4,0},{8,4},{12,8},{16,12},{20,16},{24,20},{28,24},{1,29},{... | collective-permute-start | bytes 1228808 | tf_op jit(solution)/shard_map/ppermute | solution.py:340
  91.7 8.0 %collective-permute-done.6.right = bf16[64,3200]{1,0:T(8,128)(2,1)S(1)} collective-permute-done((bf16[64,3200]{1,0:T(8,128)(2,1)S(1)}, bf16[64,3200]{1,0:T(8,128)(2,1)S(1)}, u32[]{:S(2)}, u32[]{:S(2)}) %collective-permute-start.6) | collective-permute-done | bytes 409632 | tf_op jit(solution)/shard_map/ppermute | solution.py:340
  100.3 1.8 collective-permute-start.9
  103.0 2.9 %collective-permute-done.8.j1 = bf16[16,3200]{1,0:T(8,128)(2,1)S(1)} collective-permute-done((bf16[16,3200]{1,0:T(8,128)(2,1)S(1)}, bf16[16,3200]{1,0:T(8,128)(2,1)S(1)}, u32[]{:S(2)}, u32[]{:S(2)}) %collective-permute-start.8) | collective-permute-done | bytes 102432 | tf_op jit(solution)/shard_map/ppermute | solution.py:340
  107.2 2.1 shard_map.145
  109.4 5.2 %all-to-all-start.3 = ((bf16[8,16,2432]{2,1,0:T(8,128)(2,1)}), bf16[8,16,2432]{2,1,0:T(8,128)(2,1)S(1)}, u32[]{:S(2)}, u32[]{:S(2)}) async-start(bf16[8,16,2432]{2,1,0:T(8,128)(2,1)} %shard_map.145), calls=%async_computation.3 | async-start | bytes 1245184 | tf_op jit(solution)/shard_map/all_to_all | solution.py:484
  114.5 2.0 collective-permute-start.11
  119.4 12.2 %all-to-all-done.3 = bf16[8,16,2432]{2,1,0:T(8,128)(2,1)S(1)} async-done(((bf16[8,16,2432]{2,1,0:T(8,128)(2,1)}), bf16[8,16,2432]{2,1,0:T(8,128)(2,1)S(1)}, u32[]{:S(2)}, u32[]{:S(2)}) %all-to-all-start.3) | async-done | bytes 622624 | tf_op jit(solution)/shard_map/all_to_all | solution.py:484
  133.2 3.8 %all-to-all-start.4 = ((bf16[4,128,2432]{2,1,0:T(8,128)(2,1)}), bf16[4,128,2432]{2,1,0:T(8,128)(2,1)S(1)}, u32[]{:S(2)}, u32[]{:S(2)}) async-start(bf16[4,128,2432]{2,1,0:T(8,128)(2,1)} %broadcast_in_dim.11), calls=%async_computation.4 | async-start | bytes 4980736 | tf_op jit(solution)/shard_map/all_to_all | solution.py:399
  140.1 2.7 %collective-permute-start.14 = (bf16[64,3072]{1,0:T(8,128)(2,1)}, bf16[64,3072]{1,0:T(8,128)(2,1)S(1)}, u32[]{:S(2)}, u32[]{:S(2)}) collective-permute-start(bf16[64,3072]{1,0:T(8,128)(2,1)} %constant_dynamic-update-slice_fusion.rest_0_), channel_id=1, source_target_pairs={{0,28},{4,0},{8,4},{12,8},{16,12},{20,16},{24,20},{28,24},{1,29},{... | collective-permute-start | bytes 1179656 | tf_op jit(solution)/shard_map/ppermute | solution.py:340
  142.8 5.8 %collective-permute-done.17.rest_8_ = bf16[64,3072]{1,0:T(8,128)(2,1)S(1)} collective-permute-done((bf16[64,3072]{1,0:T(8,128)(2,1)}, bf16[64,3072]{1,0:T(8,128)(2,1)S(1)}, u32[]{:S(2)}, u32[]{:S(2)}) %collective-permute-start.17) | collective-permute-done | bytes 393248 | tf_op jit(solution)/shard_map/ppermute | solution.py:340
  149.4 2.7 %collective-permute-start.15 = (bf16[64,3072]{1,0:T(8,128)(2,1)S(1)}, bf16[64,3072]{1,0:T(8,128)(2,1)S(1)}, u32[]{:S(2)}, u32[]{:S(2)}) collective-permute-start(bf16[64,3072]{1,0:T(8,128)(2,1)S(1)} %collective-permute-done.14.rest_1_), channel_id=1, source_target_pairs={{0,28},{4,0},{8,4},{12,8},{16,12},{20,16},{24,20},{28,24},{1,29},{... | collective-permute-start | bytes 1179656 | tf_op jit(solution)/shard_map/ppermute | solution.py:340
  152.8 4.1 %collective-permute-done.18.rest_7_ = bf16[64,3072]{1,0:T(8,128)(2,1)S(1)} collective-permute-done((bf16[64,3072]{1,0:T(8,128)(2,1)S(1)}, bf16[64,3072]{1,0:T(8,128)(2,1)S(1)}, u32[]{:S(2)}, u32[]{:S(2)}) %collective-permute-start.18) | collective-permute-done | bytes 393248 | tf_op jit(solution)/shard_map/ppermute | solution.py:340
  157.6 2.7 %collective-permute-start.16 = (bf16[64,3072]{1,0:T(8,128)(2,1)S(1)}, bf16[64,3072]{1,0:T(8,128)(2,1)S(1)}, u32[]{:S(2)}, u32[]{:S(2)}) collective-permute-start(bf16[64,3072]{1,0:T(8,128)(2,1)S(1)} %collective-permute-done.15.rest_2_), channel_id=1, source_target_pairs={{0,28},{4,0},{8,4},{12,8},{16,12},{20,16},{24,20},{28,24},{1,29},{... | collective-permute-start | bytes 1179656 | tf_op jit(solution)/shard_map/ppermute | solution.py:340
  161.0 4.9 %collective-permute-done.19.rest_6_ = bf16[64,3072]{1,0:T(8,128)(2,1)S(1)} collective-permute-done((bf16[64,3072]{1,0:T(8,128)(2,1)S(1)}, bf16[64,3072]{1,0:T(8,128)(2,1)S(1)}, u32[]{:S(2)}, u32[]{:S(2)}) %collective-permute-start.19) | collective-permute-done | bytes 393248 | tf_op jit(solution)/shard_map/ppermute | solution.py:340
  166.3 3.4 %collective-permute-start.21 = (bf16[32,3072]{1,0:T(8,128)(2,1)S(1)}, bf16[32,3072]{1,0:T(8,128)(2,1)S(1)}, u32[]{:S(2)}, u32[]{:S(2)}) collective-permute-start(bf16[32,3072]{1,0:T(8,128)(2,1)S(1)} %slice.9), channel_id=1, source_target_pairs={{0,28},{4,0},{8,4},{12,8},{16,12},{20,16},{24,20},{28,24},{1,29},{... | collective-permute-start | bytes 589832 | tf_op jit(solution)/shard_map/ppermute | solution.py:340
  169.7 3.7 %collective-permute-done.20.rest_4_ = bf16[32,3072]{1,0:T(8,128)(2,1)S(1)} collective-permute-done((bf16[32,3072]{1,0:T(8,128)(2,1)S(1)}, bf16[32,3072]{1,0:T(8,128)(2,1)S(1)}, u32[]{:S(2)}, u32[]{:S(2)}) %collective-permute-start.20) | collective-permute-done | bytes 196640 | tf_op jit(solution)/shard_map/ppermute | solution.py:340
  188.0 5.7 %shard_map.146 = (bf16[512,640]{1,0:T(8,128)(2,1)S(1)}, f32[64,128]{1,0:T(8,128)S(1)}) custom-call(s32[3]{0:T(128)S(1)} %pad_add_fusion.pos, bf16[512,512]{1,0:T(8,128)(2,1)S(1)} %bitcast.16, bf16[512,2432]{1,0:T(8,128)(2,1)S(1)} %bitcast.11, bf16[256,768]{1,0:T(8,128)(2,1)S(1)} %copy-done.19, bf16[256,768]{1,0:T(8,128)(2,1)S(1)} %copy-done.21, ...), custom_call_target="tpu_custom_call" | custom-call | flops 1409286144 | bytes 9000000 | tf_op jit(solution)/shard_map/pallas_call | solution.py:31
  195.2 11.5 %all-to-all-start.5 = ((bf16[8,64,640]{2,1,0:T(8,128)(2,1)}), bf16[8,64,640]{2,1,0:T(8,128)(2,1)}, u32[]{:S(2)}, u32[]{:S(2)}) async-start(bf16[8,64,640]{2,1,0:T(8,128)(2,1)} %bitcast.18), calls=%async_computation.5 | async-start | bytes 1310720 | tf_op jit(solution)/shard_map/all_to_all | solution.py:499
  215.9 7.0 %shard_map.148 = (bf16[256,1792]{1,0:T(8,128)(2,1)}, bf16[256,1792]{1,0:T(8,128)(2,1)}, bf16[1792,256]{1,0:T(8,128)(2,1)}) custom-call(s32[3]{0:T(128)S(1)} %pad_add_fusion.pos, s32[2,14]{1,0:T(2,128)S(1)} %copy-done.52, s32[2,14]{1,0:T(2,128)S(1)} %copy-done.54, s32[14,2]{1,0:T(8,128)S(1)} %copy.15.md, bf16[512,512]{1,0:T(8,128)(2,1)S(1)} %bitcast.17, ...), custom_call_target="tpu_custom_call" | custom-call | flops 1409286144 | bytes 9000000 | tf_op jit(solution)/shard_map/pallas_call | solution.py:31
  222.9 1.9 shard_map.147
  (159 shorter events, 59.3 us)
Async XLA Ops:
  0.6 17.8 %copy-start.50 = (f32[256]{0:T(256)S(1)}, f32[256]{0:T(256)}, u32[]{:S(2)}) copy-start(f32[256]{0:T(256)} %param.10) | copy-start | bytes 3076
  2.3 16.1 %all-to-all-start = ((bf16[8,64,512]{2,1,0:T(8,128)(2,1)}), bf16[8,64,512]{2,1,0:T(8,128)(2,1)S(1)}, u32[]{:S(2)}, u32[]{:S(2)}) async-start(bf16[8,64,512]{2,1,0:T(8,128)(2,1)} %broadcast_in_dim.9), calls=%async_computation | async-start | bytes 1048576 | tf_op jit(solution)/shard_map/all_to_all | solution.py:399
  15.9 9.6 %copy-start.3 = (bf16[256,1024]{1,0:T(8,128)(2,1)}, bf16[256,1024]{1,0:T(8,128)(2,1)S(1)}, u32[]{:S(2)}) copy-start(bf16[256,1024]{1,0:T(8,128)(2,1)S(1)} %get-tuple-element.38.eg.bg) | copy-start | bytes 1572868
  20.9 32.9 %all-to-all-start.1 = ((bf16[4,128,2304]{2,1,0:T(8,128)(2,1)}), bf16[4,128,2304]{2,1,0:T(8,128)(2,1)}, u32[]{:S(2)}, u32[]{:S(2)}) async-start(bf16[4,128,2304]{2,1,0:T(8,128)(2,1)} %bitcast.5), calls=%async_computation.1 | async-start | bytes 4718592 | tf_op jit(solution)/shard_map/all_to_all | solution.py:457
  26.6 11.7 %collective-permute-start = (bf16[32,3200]{1,0:T(8,128)(2,1)S(1)}, bf16[32,3200]{1,0:T(8,128)(2,1)S(1)}, u32[]{:S(2)}, u32[]{:S(2)}) collective-permute-start(bf16[32,3200]{1,0:T(8,128)(2,1)S(1)} %get-tuple-element.41), channel_id=1, source_target_pairs={{0,4},{4,8},{8,12},{12,16},{16,20},{20,24},{24,28},{28,0},{1,5},{5... | collective-permute-start | bytes 614408 | tf_op jit(solution)/shard_map/ppermute | solution.py:340
  27.6 10.6 %collective-permute-start.1 = (bf16[32,3200]{1,0:T(8,128)(2,1)S(1)}, bf16[32,3200]{1,0:T(8,128)(2,1)S(1)}, u32[]{:S(2)}, u32[]{:S(2)}) collective-permute-start(bf16[32,3200]{1,0:T(8,128)(2,1)S(1)} %get-tuple-element.42), channel_id=1, source_target_pairs={{0,28},{4,0},{8,4},{12,8},{16,12},{20,16},{24,20},{28,24},{1,29},{... | collective-permute-start | bytes 614408 | tf_op jit(solution)/shard_map/ppermute | solution.py:340
  39.2 25.1 %collective-permute-start.2 = (bf16[64,3200]{1,0:T(8,128)(2,1)}, bf16[64,3200]{1,0:T(8,128)(2,1)}, u32[]{:S(2)}, u32[]{:S(2)}) collective-permute-start(bf16[64,3200]{1,0:T(8,128)(2,1)} %get-tuple-element.43), channel_id=1, source_target_pairs={{0,4},{4,8},{8,12},{12,16},{16,20},{20,24},{24,28},{28,0},{1,5},{5... | collective-permute-start | bytes 1228808 | tf_op jit(solution)/shard_map/ppermute | solution.py:340
  39.2 25.1 %collective-permute-start.3 = (bf16[64,3200]{1,0:T(8,128)(2,1)}, bf16[64,3200]{1,0:T(8,128)(2,1)}, u32[]{:S(2)}, u32[]{:S(2)}) collective-permute-start(bf16[64,3200]{1,0:T(8,128)(2,1)} %get-tuple-element.44), channel_id=1, source_target_pairs={{0,28},{4,0},{8,4},{12,8},{16,12},{20,16},{24,20},{28,24},{1,29},{... | collective-permute-start | bytes 1228808 | tf_op jit(solution)/shard_map/ppermute | solution.py:340
  56.8 50.4 %all-to-all-start.2 = ((bf16[8,16,2304]{2,1,0:T(8,128)(2,1)}), bf16[8,16,2304]{2,1,0:T(8,128)(2,1)}, u32[]{:S(2)}, u32[]{:S(2)}) async-start(bf16[8,16,2304]{2,1,0:T(8,128)(2,1)} %bitcast.25), calls=%async_computation.2 | async-start | bytes 1179648 | tf_op jit(solution)/shard_map/all_to_all | solution.py:461
  65.7 23.1 %collective-permute-start.4 = (bf16[64,3200]{1,0:T(8,128)(2,1)S(1)}, bf16[64,3200]{1,0:T(8,128)(2,1)S(1)}, u32[]{:S(2)}, u32[]{:S(2)}) collective-permute-start(bf16[64,3200]{1,0:T(8,128)(2,1)S(1)} %get-tuple-element.45), channel_id=1, source_target_pairs={{0,4},{4,8},{8,12},{12,16},{16,20},{20,24},{24,28},{28,0},{1,5},{5... | collective-permute-start | bytes 1228808 | tf_op jit(solution)/shard_map/ppermute | solution.py:340
  67.2 21.6 %collective-permute-start.5 = (bf16[64,3200]{1,0:T(8,128)(2,1)S(1)}, bf16[64,3200]{1,0:T(8,128)(2,1)S(1)}, u32[]{:S(2)}, u32[]{:S(2)}) collective-permute-start(bf16[64,3200]{1,0:T(8,128)(2,1)S(1)} %get-tuple-element.46), channel_id=1, source_target_pairs={{0,28},{4,0},{8,4},{12,8},{16,12},{20,16},{24,20},{28,24},{1,29},{... | collective-permute-start | bytes 1228808 | tf_op jit(solution)/shard_map/ppermute | solution.py:340
  89.0 10.8 %collective-permute-start.6 = (bf16[64,3200]{1,0:T(8,128)(2,1)S(1)}, bf16[64,3200]{1,0:T(8,128)(2,1)S(1)}, u32[]{:S(2)}, u32[]{:S(2)}) collective-permute-start(bf16[64,3200]{1,0:T(8,128)(2,1)S(1)} %get-tuple-element.47), channel_id=1, source_target_pairs={{0,4},{4,8},{8,12},{12,16},{16,20},{20,24},{24,28},{28,0},{1,5},{5... | collective-permute-start | bytes 1228808 | tf_op jit(solution)/shard_map/ppermute | solution.py:340
  89.1 10.7 %collective-permute-start.7 = (bf16[64,3200]{1,0:T(8,128)(2,1)S(1)}, bf16[64,3200]{1,0:T(8,128)(2,1)S(1)}, u32[]{:S(2)}, u32[]{:S(2)}) collective-permute-start(bf16[64,3200]{1,0:T(8,128)(2,1)S(1)} %get-tuple-element.48), channel_id=1, source_target_pairs={{0,28},{4,0},{8,4},{12,8},{16,12},{20,16},{24,20},{28,24},{1,29},{... | collective-permute-start | bytes 1228808 | tf_op jit(solution)/shard_map/ppermute | solution.py:340
  99.9 5.9 %collective-permute-start.8 = (bf16[16,3200]{1,0:T(8,128)(2,1)S(1)}, bf16[16,3200]{1,0:T(8,128)(2,1)S(1)}, u32[]{:S(2)}, u32[]{:S(2)}) collective-permute-start(bf16[16,3200]{1,0:T(8,128)(2,1)S(1)} %get-tuple-element.50), channel_id=1, source_target_pairs={{0,1},{1,2},{2,3},{3,0},{4,5},{5,6},{6,7},{7,4},{8,9},{9,10},{10,1... | collective-permute-start | bytes 307208 | tf_op jit(solution)/shard_map/ppermute | solution.py:340
  100.3 5.5 %collective-permute-start.9 = (bf16[16,3200]{1,0:T(8,128)(2,1)S(1)}, bf16[16,3200]{1,0:T(8,128)(2,1)S(1)}, u32[]{:S(2)}, u32[]{:S(2)}) collective-permute-start(bf16[16,3200]{1,0:T(8,128)(2,1)S(1)} %get-tuple-element.51), channel_id=1, source_target_pairs={{0,2},{1,3},{2,0},{3,1},{4,6},{5,7},{6,4},{7,5},{8,10},{9,11},{10,... | collective-permute-start | bytes 307208 | tf_op jit(solution)/shard_map/ppermute | solution.py:340
  102.1 4.4 %collective-permute-start.10 = (bf16[16,3200]{1,0:T(8,128)(2,1)S(1)}, bf16[16,3200]{1,0:T(8,128)(2,1)S(1)}, u32[]{:S(2)}, u32[]{:S(2)}) collective-permute-start(bf16[16,3200]{1,0:T(8,128)(2,1)S(1)} %get-tuple-element.52), channel_id=1, source_target_pairs={{0,3},{1,0},{2,1},{3,2},{4,7},{5,4},{6,5},{7,6},{8,11},{9,8},{10,9... | collective-permute-start | bytes 307208 | tf_op jit(solution)/shard_map/ppermute | solution.py:340
  109.4 22.2 %all-to-all-start.3 = ((bf16[8,16,2432]{2,1,0:T(8,128)(2,1)}), bf16[8,16,2432]{2,1,0:T(8,128)(2,1)S(1)}, u32[]{:S(2)}, u32[]{:S(2)}) async-start(bf16[8,16,2432]{2,1,0:T(8,128)(2,1)} %shard_map.145), calls=%async_computation.3 | async-start | bytes 1245184 | tf_op jit(solution)/shard_map/all_to_all | solution.py:484
  114.5 4.2 %collective-permute-start.11 = (bf16[16,3072]{1,0:T(8,128)(2,1)}, bf16[16,3072]{1,0:T(8,128)(2,1)S(1)}, u32[]{:S(2)}, u32[]{:S(2)}) collective-permute-start(bf16[16,3072]{1,0:T(8,128)(2,1)} %get-tuple-element.55), channel_id=1, source_target_pairs={{0,3},{1,0},{2,1},{3,2},{4,7},{5,4},{6,5},{7,6},{8,11},{9,8},{10,9... | collective-permute-start | bytes 294920 | tf_op jit(solution)/shard_map/ppermute | solution.py:340
  118.2 18.8 %collective-permute-start.12 = (bf16[16,3072]{1,0:T(8,128)(2,1)}, bf16[16,3072]{1,0:T(8,128)(2,1)}, u32[]{:S(2)}, u32[]{:S(2)}) collective-permute-start(bf16[16,3072]{1,0:T(8,128)(2,1)} %get-tuple-element.55), channel_id=1, source_target_pairs={{0,2},{1,3},{2,0},{3,1},{4,6},{5,7},{6,4},{7,5},{8,10},{9,11},{10,... | collective-permute-start | bytes 294920 | tf_op jit(solution)/shard_map/ppermute | solution.py:340
  118.2 20.4 %collective-permute-start.13 = (bf16[16,3072]{1,0:T(8,128)(2,1)}, bf16[16,3072]{1,0:T(8,128)(2,1)}, u32[]{:S(2)}, u32[]{:S(2)}) collective-permute-start(bf16[16,3072]{1,0:T(8,128)(2,1)} %get-tuple-element.55), channel_id=1, source_target_pairs={{0,1},{1,2},{2,3},{3,0},{4,5},{5,6},{6,7},{7,4},{8,9},{9,10},{10,1... | collective-permute-start | bytes 294920 | tf_op jit(solution)/shard_map/ppermute | solution.py:340
  133.2 41.9 %copy-start.2 = (bf16[8,64,512]{2,1,0:T(8,128)(2,1)S(1)}, bf16[8,64,512]{2,1,0:T(8,128)(2,1)}, u32[]{:S(2)}) copy-start(bf16[8,64,512]{2,1,0:T(8,128)(2,1)} %copy-done) | copy-start | bytes 1572868
  133.2 41.9 %copy-start.5 = (bf16[256,1024]{1,0:T(8,128)(2,1)S(1)}, bf16[256,1024]{1,0:T(8,128)(2,1)}, u32[]{:S(2)}) copy-start(bf16[256,1024]{1,0:T(8,128)(2,1)} %copy-done.3) | copy-start | bytes 1572868
  133.2 41.9 %all-to-all-start.4 = ((bf16[4,128,2432]{2,1,0:T(8,128)(2,1)}), bf16[4,128,2432]{2,1,0:T(8,128)(2,1)S(1)}, u32[]{:S(2)}, u32[]{:S(2)}) async-start(bf16[4,128,2432]{2,1,0:T(8,128)(2,1)} %broadcast_in_dim.11), calls=%async_computation.4 | async-start | bytes 4980736 | tf_op jit(solution)/shard_map/all_to_all | solution.py:399
  140.1 8.5 %collective-permute-start.17 = (bf16[64,3072]{1,0:T(8,128)(2,1)}, bf16[64,3072]{1,0:T(8,128)(2,1)S(1)}, u32[]{:S(2)}, u32[]{:S(2)}) collective-permute-start(bf16[64,3072]{1,0:T(8,128)(2,1)} %constant_dynamic-update-slice_fusion.rest_0_), channel_id=1, source_target_pairs={{0,4},{4,8},{8,12},{12,16},{16,20},{20,24},{24,28},{28,0},{1,5},{5... | collective-permute-start | bytes 1179656 | tf_op jit(solution)/shard_map/ppermute | solution.py:340
  140.1 9.3 %collective-permute-start.14 = (bf16[64,3072]{1,0:T(8,128)(2,1)}, bf16[64,3072]{1,0:T(8,128)(2,1)S(1)}, u32[]{:S(2)}, u32[]{:S(2)}) collective-permute-start(bf16[64,3072]{1,0:T(8,128)(2,1)} %constant_dynamic-update-slice_fusion.rest_0_), channel_id=1, source_target_pairs={{0,28},{4,0},{8,4},{12,8},{16,12},{20,16},{24,20},{28,24},{1,29},{... | collective-permute-start | bytes 1179656 | tf_op jit(solution)/shard_map/ppermute | solution.py:340
  148.6 8.3 %collective-permute-start.18 = (bf16[64,3072]{1,0:T(8,128)(2,1)S(1)}, bf16[64,3072]{1,0:T(8,128)(2,1)S(1)}, u32[]{:S(2)}, u32[]{:S(2)}) collective-permute-start(bf16[64,3072]{1,0:T(8,128)(2,1)S(1)} %collective-permute-done.17.rest_8_), channel_id=1, source_target_pairs={{0,4},{4,8},{8,12},{12,16},{16,20},{20,24},{24,28},{28,0},{1,5},{5... | collective-permute-start | bytes 1179656 | tf_op jit(solution)/shard_map/ppermute | solution.py:340
  149.4 8.2 %collective-permute-start.15 = (bf16[64,3072]{1,0:T(8,128)(2,1)S(1)}, bf16[64,3072]{1,0:T(8,128)(2,1)S(1)}, u32[]{:S(2)}, u32[]{:S(2)}) collective-permute-start(bf16[64,3072]{1,0:T(8,128)(2,1)S(1)} %collective-permute-done.14.rest_1_), channel_id=1, source_target_pairs={{0,28},{4,0},{8,4},{12,8},{16,12},{20,16},{24,20},{28,24},{1,29},{... | collective-permute-start | bytes 1179656 | tf_op jit(solution)/shard_map/ppermute | solution.py:340
  156.9 9.1 %collective-permute-start.19 = (bf16[64,3072]{1,0:T(8,128)(2,1)S(1)}, bf16[64,3072]{1,0:T(8,128)(2,1)S(1)}, u32[]{:S(2)}, u32[]{:S(2)}) collective-permute-start(bf16[64,3072]{1,0:T(8,128)(2,1)S(1)} %collective-permute-done.18.rest_7_), channel_id=1, source_target_pairs={{0,4},{4,8},{8,12},{12,16},{16,20},{20,24},{24,28},{28,0},{1,5},{5... | collective-permute-start | bytes 1179656 | tf_op jit(solution)/shard_map/ppermute | solution.py:340
  157.6 8.7 %collective-permute-start.16 = (bf16[64,3072]{1,0:T(8,128)(2,1)S(1)}, bf16[64,3072]{1,0:T(8,128)(2,1)S(1)}, u32[]{:S(2)}, u32[]{:S(2)}) collective-permute-start(bf16[64,3072]{1,0:T(8,128)(2,1)S(1)} %collective-permute-done.15.rest_2_), channel_id=1, source_target_pairs={{0,28},{4,0},{8,4},{12,8},{16,12},{20,16},{24,20},{28,24},{1,29},{... | collective-permute-start | bytes 1179656 | tf_op jit(solution)/shard_map/ppermute | solution.py:340
  165.9 7.4 %collective-permute-start.20 = (bf16[32,3072]{1,0:T(8,128)(2,1)S(1)}, bf16[32,3072]{1,0:T(8,128)(2,1)S(1)}, u32[]{:S(2)}, u32[]{:S(2)}) collective-permute-start(bf16[32,3072]{1,0:T(8,128)(2,1)S(1)} %slice.8), channel_id=1, source_target_pairs={{0,4},{4,8},{8,12},{12,16},{16,20},{20,24},{24,28},{28,0},{1,5},{5... | collective-permute-start | bytes 589832 | tf_op jit(solution)/shard_map/ppermute | solution.py:340
  166.3 8.1 %collective-permute-start.21 = (bf16[32,3072]{1,0:T(8,128)(2,1)S(1)}, bf16[32,3072]{1,0:T(8,128)(2,1)S(1)}, u32[]{:S(2)}, u32[]{:S(2)}) collective-permute-start(bf16[32,3072]{1,0:T(8,128)(2,1)S(1)} %slice.9), channel_id=1, source_target_pairs={{0,28},{4,0},{8,4},{12,8},{16,12},{20,16},{24,20},{28,24},{1,29},{... | collective-permute-start | bytes 589832 | tf_op jit(solution)/shard_map/ppermute | solution.py:340
  195.2 27.7 %all-to-all-start.5 = ((bf16[8,64,640]{2,1,0:T(8,128)(2,1)}), bf16[8,64,640]{2,1,0:T(8,128)(2,1)}, u32[]{:S(2)}, u32[]{:S(2)}) async-start(bf16[8,64,640]{2,1,0:T(8,128)(2,1)} %bitcast.18), calls=%async_computation.5 | async-start | bytes 1310720 | tf_op jit(solution)/shard_map/all_to_all | solution.py:499
  (51 other events, 114.3 us)

commit v4 on v3

--- a/solution.py
+++ b/solution.py
@@ -9,7 +9,7 @@
 D = 8192
 BLK = 128
 NZ, NX = 8, 4
-HA, HB = 768, 1024
+HA, HB = 1024, 768
 COL = ("col_0", "col_1")
 ALL = ("row", "col_0", "col_1")
 norm_eps = 1e-05
@@ -26,7 +26,7 @@
     return pl.BlockSpec(memory_space=pltpu.SMEM)
 
 
-def call(kernel, outs, in_specs, scratch, flops, nbytes, args, mib=40, grid=()):
+def call(kernel, outs, in_specs, scratch, flops, nbytes, args, mib=56, grid=()):
     whole = [pl.BlockSpec(o.shape, lambda *_, n=len(o.shape): (0,) * n) for o in outs]
     return pl.pallas_call(
         kernel,
@@ -65,12 +65,11 @@
 
 def pieces_of_tokens(pos):
     for tz in range(NZ):
-        k = lax.rem(tz - pos[1] + NZ, NZ)
         for tx in range(NX):
             j = lax.rem(tx - pos[2] + NX, NX)
             nat = slice(tz * 64 + tx * 16, tz * 64 + tx * 16 + 16)
             in_a = slice((tx * NZ + tz) * 16, (tx * NZ + tz) * 16 + 16)
-            in_b = pl.ds(pl.multiple_of(k * 64 + j * 16, 16), 16)
+            in_b = pl.ds(pl.multiple_of(tz * 64 + j * 16, 16), 16)
             yield nat, in_a, in_b
 
 
@@ -107,22 +106,6 @@
     return (sq[:, :BLK] + sq[:, BLK:]).astype(bf16)
 
 
-def far_kernel(pos, rows, gain, eg, eu, ed, far_r, far_l, left):
-    width = gain.shape[1]
-    tz = lax.rem(pos[1] + NZ // 2, NZ)
-    for j in range(NX):
-        nat = pl.ds(pl.multiple_of(tz * 64 + lax.rem(pos[2] + j, NX) * 16, 16), 16)
-        to = slice(j * 16, j * 16 + 16)
-        left[to, :width] = scaled(rows, nat, gain)
-        left[to, width:] = rows[nat, width:]
-        far, at = (far_r, j * 16) if j < 2 else (far_l, j * 16 - 32)
-        far[at : at + 16, 3 * HB :] = square_sums(rows, nat, width)
-    x, g = left[:, :width], left[:, width:]
-    for p, at in ((nn(x, eg[...]), 0), (nn(x, eu[...]), HB), (nt(g, ed[...]), 2 * HB)):
-        far_r[:, at : at + HB] = p[:32].astype(bf16)
-        far_l[:, at : at + HB] = p[32:].astype(bf16)
-
-
 def part_a_kernel(rows, gain, eg, eu, ed, part, left):
     width = gain.shape[1]
     for tz in range(NZ):
@@ -141,29 +124,8 @@
         left[to, :width] = scaled(rows, nat, gain)
         left[to, width:] = rows[nat, width:]
         part[to, 3 * HB :] = square_sums(rows, nat, width)
-    for t, n in ((192, 64), (320, 64), (64, 128), (384, 128), (0, 64)):
-        products(left, slice(t, t + n), (eg, eu, ed), part, slice(t, t + n), HB)
-
-
-def ring_first_kernel(right, left, piece_r, piece_l, out_r, out_l):
-    h = right.shape[0]
-    out_r[:h] = (piece_r[:h].astype(f32) + right[...].astype(f32)).astype(bf16)
-    out_r[h:] = piece_r[h:]
-    out_l[:h] = piece_l[:h]
-    out_l[h:] = (piece_l[h:].astype(f32) + left[...].astype(f32)).astype(bf16)
-
-
-def ring_kernel(right, left, piece_r, piece_l, *rest):
-    out_r, out_l = rest[-2:]
-    out_r[...] = (piece_r[...].astype(f32) + right[...].astype(f32)).astype(bf16)
-    out_l[...] = (piece_l[...].astype(f32) + left[...].astype(f32)).astype(bf16)
-
-
-def ring_last_kernel(right, left, piece, own, *others):
-    for j, out in enumerate((own, *others)):
-        at = slice(j * 16, j * 16 + 16)
-        v = piece[at].astype(f32) + right[at].astype(f32) + left[at].astype(f32)
-        out[...] = v.astype(out.dtype)
+    for t in range(0, left.shape[0], 128):
+        products(left, slice(t, t + 128), (eg, eu, ed), part, slice(t, t + 128), HB)
 
 
 def hidden_grads(sums, half, scale, to_act, to_gate, to_up):
@@ -183,10 +145,10 @@
     return dots
 
 
-def grads_b_kernel(own, j1, j2, j3, send, scale, dots):
+def grads_b_kernel(part, j1, j2, j3, send, scale, dots):
     def sums(c):
         at = slice(c, c + BLK)
-        v = own[:, at]
+        v = part[:16, at].astype(f32)
         for j in (j1, j2, j3):
             v = v + j[:, at].astype(f32)
         return v
@@ -223,26 +185,27 @@
     store(3 * HA)(0, extra.astype(bf16))
 
 
-def fetch_pieces(pieces, gb, sems):
-    copies, at = [], 0
-    for i, p in enumerate(pieces):
-        copies.append(pltpu.make_async_copy(p, gb.at[pl.ds(at, p.shape[0])], sems.at[i]))
+def fetch(sources, targets, sems):
+    copies = []
+    for i, (a, b) in enumerate(zip(sources, targets)):
+        copies.append(pltpu.make_async_copy(a, b, sems.at[i]))
         copies[-1].start()
-        at += p.shape[0]
     return copies
 
 
-def features_kernel(pos, rows, ga, ag, au, ad, bg, bu, bd, *rest):
-    pieces, (both, own_scale, gb, da, na, db, nb, sems) = rest[:-8], rest[-8:]
-    copies = fetch_pieces(pieces, gb, sems)
+def features_kernel(pos, *rest):
+    n = 9
+    both, own_scale, da, na, db, nb = rest[n : n + 6]
+    held, sems = rest[n + 6 : -1], rest[-1]
+    copies = fetch(rest[:n], held, sems)
+    gb, bg, bu, bd, ga, ag, au, ad, rows = held
     width = ag.shape[0]
-    for hid, d, n, (eg, eu, ed), half in (
-        (ga, da, na, (ag, au, ad), HA),
-        (gb, db, nb, (bg, bu, bd), HB),
+    for hid, d, n, (eg, eu, ed), half, waits in (
+        (gb, db, nb, (bg, bu, bd), HB, copies[:4]),
+        (ga, da, na, (ag, au, ad), HA, copies[4:]),
     ):
-        if hid is gb:
-            for c in copies:
-                c.wait()
+        for c in waits:
+            c.wait()
         for t in range(0, hid.shape[0], 128):
             tok = slice(t, t + 128)
             d[tok, :] = nn(hid[tok, :half], ed[...])
@@ -279,9 +242,11 @@
         own_scale[tx * 16 : tx * 16 + 16, :] = jnp.broadcast_to(s, (16, BLK))
 
 
-def weights_kernel(pos, mg, mu, md, rows, gain, ga, *rest):
-    pieces, (out_g, out_u, out_d, gb, la, lb, sems) = rest[:-7], rest[-7:]
-    copies = fetch_pieces(pieces, gb, sems)
+def weights_kernel(pos, mg, mu, md, gain, *rest):
+    sources, (out_g, out_u, out_d, la, lb, rows, ga, gb, sems) = rest[:3], rest[3:]
+    copies = fetch(sources, (rows, ga, gb), sems)
+    copies[0].wait()
+    copies[1].wait()
     width = gain.shape[1]
     for nat, in_a, in_b in pieces_of_tokens(pos):
         scale = lane_sum(ga[in_a, 3 * HA :], 0)
@@ -293,8 +258,7 @@
         lb[in_b, width:] = g
     for hid, left, at, half in ((ga, la, 0, HA), (gb, lb, HA, HB)):
         if at:
-            for c in copies:
-                c.wait()
+            copies[2].wait()
         normed, grad = left[:, :width], left[:, width:]
         for c in range(0, half, BLK):
             b = (at + c) // BLK
@@ -340,60 +304,6 @@
     return lax.ppermute(v, axis, [(i, (i + step) % n) for i in range(n)])
 
 
-def ring_sum(far, part, gate_on):
-    wide = part.shape[1]
-
-    def piece(k):
-        return pl.BlockSpec((64, wide), lambda i: (k, 0))
-
-    block = jax.ShapeDtypeStruct((64, wide), bf16)
-    right, left = (send(v, "col_0", s) for v, s in zip(far, (1, -1)))
-    for away in range(NZ // 2 - 1, 0, -1):
-        first, last = away == NZ // 2 - 1, away == 1
-        got = pl.BlockSpec(right.shape, lambda i: (0, 0))
-        right, left = call(
-            ring_first_kernel if first else ring_kernel,
-            (block, block),
-            [got, got, piece(away), piece(NZ - away)]
-            + ([pl.BlockSpec(memory_space=pl.ANY)] if last else []),
-            [],
-            0,
-            2_500_000,
-            (right, left, part, part) + ((gate_on,) if last else ()),
-            mib=16,
-            grid=(1,),
-        )
-        right, left = send(right, "col_0", 1), send(left, "col_0", -1)
-    got = pl.BlockSpec(right.shape, lambda i: (0, 0))
-    return call(
-        ring_last_kernel,
-        (
-            jax.ShapeDtypeStruct((16, wide), f32),
-            *[jax.ShapeDtypeStruct((16, wide), bf16)] * (NX - 1),
-        ),
-        [got, got, piece(0)],
-        [],
-        0,
-        2_000_000,
-        (right, left, part),
-        mib=16,
-        grid=(1,),
-    )
-
-
-def ring_gather(shard, axis):
-    n = lax.axis_size(axis)
-    h = shard.shape[0] // 2
-    from_right, from_left = [], []
-    right = left = shard
-    for _ in range(1, n // 2):
-        right, left = send(right, axis, 1), send(left, axis, -1)
-        from_left.insert(0, right)
-        from_right.append(left)
-    far = [send(right[:h], axis, 1), send(left[h:], axis, -1)]
-    return [shard, *from_right, *far, *from_left]
-
-
 def from_everyone(shard, axis):
     copies = jnp.broadcast_to(shard, (lax.axis_size(axis), *shard.shape))
     got = lax.all_to_all(copies, axis, split_axis=0, concat_axis=0, tiled=True)
@@ -426,15 +336,6 @@
         (mask_gate, mask_up, mask_down, w_gate, w_up, w_down),
     )
     eff_a, eff_b = eff[:3], eff[3:]
-    far = call(
-        far_kernel,
-        (out(32, b_cols), out(32, b_cols)),
-        [smem()] + [vmem()] * 5,
-        [pltpu.VMEM((64, 2 * width), bf16)],
-        flops * HB // 8,
-        2_000_000,
-        (pos, rows, gain, *eff_b),
-    )
     left = pltpu.VMEM((tokens, 2 * width), bf16)
     (part_a,) = call(
         part_a_kernel,
@@ -455,8 +356,8 @@
         (pos, rows, gain, *eff_b),
     )
     got_a = lax.all_to_all(part_a.reshape(NX, -1, a_cols), "col_1", 0, 0, tiled=True)
-    own, *others = ring_sum(far, part_b, got_a)
-    got_b = [send(v, "col_1", j) for j, v in enumerate(others, 1)]
+    mine_b = lax.psum_scatter(part_b, "col_0", scatter_dimension=0, tiled=True)
+    got_b = [send(mine_b[j * 16 : j * 16 + 16], "col_1", j) for j in range(1, NX)]
     sum_a = jnp.sum(got_a.astype(f32), axis=0).astype(bf16).reshape(NZ, -1, a_cols)
     got_a = lax.all_to_all(sum_a, "col_0", 0, 0, tiled=True)
     send_b, scale, dots_b = call(
@@ -466,8 +367,7 @@
         [],
         0,
         600_000,
-        (own, *got_b),
-        mib=16,
+        (mine_b, *got_b),
     )
     (copies_a,) = call(
         grads_a_kernel,
@@ -477,34 +377,36 @@
         0,
         1_500_000,
         (got_a, scale, dots_b),
-        mib=16,
     )
     near = [send_b] + [send(send_b, "col_1", -j) for j in range(1, NX)]
-    pieces_b = ring_gather(jnp.concatenate(near), "col_0")
+    all_b = lax.all_gather(jnp.concatenate(near), "col_0", axis=0, tiled=True)
     all_a = lax.all_to_all(copies_a, "col_0", 0, 0, tiled=True).reshape(-1, a_cols + BLK)
     all_a = from_everyone(all_a, "col_1")
 
-    anywhere = [pl.BlockSpec(memory_space=pl.ANY)] * len(pieces_b)
-    gb = pltpu.VMEM((tokens, 3 * HB), bf16)
-    sems = pltpu.SemaphoreType.DMA((len(pieces_b),))
+    anywhere = pl.BlockSpec(memory_space=pl.ANY)
+    sources = (all_b, *eff_b, all_a, *eff_a, rows)
     both, own_scale = call(
         features_kernel,
         (out(tokens, 2 * width + BLK), out(mine, BLK, dtype=f32)),
-        [smem()] + [vmem()] * 8 + anywhere,
-        [gb, *[pltpu.VMEM((tokens, width), f32)] * 4, sems],
+        [smem()] + [anywhere] * len(sources),
+        [pltpu.VMEM((tokens, width), f32)] * 4
+        + [pltpu.VMEM(v.shape, bf16) for v in sources]
+        + [pltpu.SemaphoreType.DMA((len(sources),))],
         flops * (HA + HB),
         9_000_000,
-        (pos, rows, all_a, *eff_a, *eff_b, *pieces_b),
+        (pos, *sources),
     )
     got = lax.all_to_all(both.reshape(-1, mine, both.shape[1]), "row", 0, 0, tiled=True)
     gate_wgrad, up_wgrad, down_wgrad = call(
         weights_kernel,
         (shape(w_gate), shape(w_up), shape(w_down)),
-        [smem()] * 4 + [vmem()] * 3 + anywhere,
-        [gb, left, left, sems],
+        [smem()] * 4 + [vmem()] + [anywhere] * 3,
+        [left, left]
+        + [pltpu.VMEM(v.shape, bf16) for v in (rows, all_a, all_b)]
+        + [pltpu.SemaphoreType.DMA((3,))],
         flops * (HA + HB),
         9_000_000,
-        (pos, mask_gate, mask_up, mask_down, rows, gain, all_a, *pieces_b),
+        (pos, mask_gate, mask_up, mask_down, gain, rows, all_a, all_b),
     )
     layer_out, input_grad, gain_grad = call(
         final_kernel,
@@ -514,7 +416,6 @@
         0,
         1_000_000,
         (got, layer_input, out_grad, gain, own_scale),
-        mib=16,
     )
     return (layer_out, input_grad, gain_grad[0], gate_wgrad, up_wgrad, down_wgrad)
 

time: 228 us -> 211 us (0.925); the launches traced: 225 us -> 210 us
  blocking collectives: 0 us -> 98.9 us
  waiting for transfers between devices: 77.4 us -> 17.6 us
  local copies, waits for them, and re-layouts: 45.6 us -> 6.58 us
  starting transfers between devices: 69.6 us -> 35.3 us
  between operations: 0.96 us -> 14.1 us
  Pallas kernels: 27.4 us -> 33.1 us
    all_to_all x0 -> x3, blocking collectives: none -> 98.9 us  [the longest x1 40.3 us: shards(): lax.all_to_all(part_a.reshape(NX, -1, a_cols), 'col_1', 0, 0, tiled=True)]
    ppermute x22 -> x6, waiting for transfers between devices: 50.8 us -> 7.24 us  [send(): return lax.ppermute(v, axis, [(i, (i + step) % n) for i in range(n)])]
    unnamed x114 -> x13, local copies, waits for them, and re-layouts: 41.6 us -> 4.55 us
    ppermute x22 -> x6, starting transfers between devices: 30.5 us -> 5.64 us  [send(): return lax.ppermute(v, axis, [(i, (i + step) % n) for i in range(n)])]
    all_to_all x2 -> x0, waiting for transfers between devices: 24.1 us -> none  [the longest x1 12.2 us: shards(): lax.all_to_all(copies_a, 'col_0', 0, 0, tiled=True)]
    all_to_all x2 -> x0, starting transfers between devices: 9.67 us -> none  [the longest x1 5.18 us: shards(): lax.all_to_all(copies_a, 'col_0', 0, 0, tiled=True)]
    pallas_call x13 -> x8, Pallas kernels: 27.4 us -> 33.1 us  [call(): pl.pallas_call(kernel, out_shape=outs, grid=grid, in_specs=in_specs, out_...]
    all_to_all x1, starting transfers between devices: 11.5 us -> 15.4 us  [shards(): lax.all_to_all(both.reshape(-1, mine, both.shape[1]), 'row', 0, 0, tiled=...]
  transfers between devices with their start and end apart: 28 -> 11, of which waited for: 13 -> 8; matrix products, arithmetic and copies ran while one was open for 5% -> 3% of each run, Pallas kernels for 7% -> 10%
where the time goes in v4:
time: 211 us; the launch traced here: 210 us
  blocking collectives  98.9 us (47%)
  starting transfers between devices  35.3 us (17%)
  Pallas kernels  33.1 us (16%)
  waiting for transfers between devices  17.6 us (8%)
  between operations  14.1 us (7%)
  local copies, waits for them, and re-layouts  6.58 us (3%)
  other arithmetic  4.7 us (2%)
    all_to_all x1, blocking collectives, shards(): lax.all_to_all(part_a.reshape(NX, -1, a_cols), 'col_1', 0, 0, tiled=True)  40.3 us
    pallas_call x8, Pallas kernels, call(): pl.pallas_call(kernel, out_shape=outs, grid=grid, in_specs=in_specs, out_...  33.1 us
    all_to_all x1, blocking collectives, from_everyone(): got = lax.all_to_all(copies, axis, split_axis=0, concat_axis=0, tiled=True)  31.4 us
    all_to_all x1, blocking collectives, shards(): lax.all_to_all(copies_a, 'col_0', 0, 0, tiled=True)  27.2 us
    all_to_all x1, starting transfers between devices, shards(): lax.all_to_all(both.reshape(-1, mine, both.shape[1]), 'row', 0, 0, tiled=...  15.4 us
    all_to_all x1, starting transfers between devices, shards(): got_a = lax.all_to_all(sum_a, 'col_0', 0, 0, tiled=True)  7.6 us
    ppermute x6, waiting for transfers between devices, send(): return lax.ppermute(v, axis, [(i, (i + step) % n) for i in range(n)])  7.24 us
    all_to_all x1, starting transfers between devices, from_everyone(): got = lax.all_to_all(copies, axis, split_axis=0, concat_axis=0, tiled=True)  6.64 us
  transfers between devices with their start and end apart: 11, of which 8 were waited for; matrix products, arithmetic and copies ran while one was open for 3% of the time, Pallas kernels for 10%

profile of v4, /device:TPU:1, one launch (start us, length us, event | category | flops | bytes accessed | tf_op | source)
XLA Modules:
  0.0 210.2 jit_solution(11704848717822144236)
XLA Ops:
  8.8 6.6 %all-to-all-start = ((bf16[8,64,512]{2,1,0:T(8,128)(2,1)}), bf16[8,64,512]{2,1,0:T(8,128)(2,1)S(1)}, u32[]{:S(2)}, u32[]{:S(2)}) async-start(bf16[8,64,512]{2,1,0:T(8,128)(2,1)} %broadcast_in_dim.9), calls=%async_computation | async-start | bytes 1048576 | tf_op jit(solution)/shard_map/all_to_all | solution.py:309
  15.4 1.4 copy.15.md
  16.8 3.9 %shard_map.136 = (bf16[256,1024]{1,0:T(8,128)(2,1)}, bf16[256,1024]{1,0:T(8,128)(2,1)}, bf16[1024,256]{1,0:T(8,128)(2,1)}, bf16[256,768]{1,0:T(8,128)(2,1)}, bf1...) custom-call(s32[2,14]{1,0:T(2,128)} %mg.3, s32[2,14]{1,0:T(2,128)} %mu.3, s32[14,2]{1,0:T(8,128)} %copy.15.md, ...), custom_call_target="tpu_custom_call" | custom-call | bytes 6000000 | tf_op jit(solution)/shard_map/pallas_call | solution.py:31
  21.4 3.6 %all-to-all-done = bf16[8,64,512]{2,1,0:T(8,128)(2,1)S(1)} async-done(((bf16[8,64,512]{2,1,0:T(8,128)(2,1)}), bf16[8,64,512]{2,1,0:T(8,128)(2,1)S(1)}, u32[]{:S(2)}, u32[]{:S(2)}) %all-to-all-start) | async-done | bytes 524320 | tf_op jit(solution)/shard_map/all_to_all | solution.py:309
  25.7 4.0 %shard_map.137 = bf16[512,2432]{1,0:T(8,128)(2,1)} custom-call(s32[3]{0:T(128)} %pad_add_fusion.pos, bf16[512,512]{1,0:T(8,128)(2,1)} %bitcast.13, f32[1,256]{1,0:T(1,128)} %bitcast.21, bf16[256,768]{1,0:T(8,128)(2,1)} %get-tuple-element.23.eg.rest_1_, bf16[256,768]{1,0:T(8,128)(2,1)} %get-tuple-element.24.eu.rest_2_, ...), custom_call_target="tpu_custom_call" | custom-call | flops 603979776 | bytes 5000000 | tf_op jit(solution)/shard_map/pallas_call | solution.py:31
  29.8 4.6 %shard_map.139 = bf16[512,3072]{1,0:T(8,128)(2,1)} custom-call(bf16[512,512]{1,0:T(8,128)(2,1)} %bitcast.14, f32[1,256]{1,0:T(1,128)} %bitcast.22, bf16[256,1024]{1,0:T(8,128)(2,1)} %get-tuple-element.27.eg.rest_5_, bf16[256,1024]{1,0:T(8,128)(2,1)} %get-tuple-element.28.eu.rest_6_, bf16[1024,256]{1,0:T(8,128)(2,1)} %get-tuple-element.29.ed.rest_7_), custom_call_target="tpu_custom_call" | custom-call | flops 805306368 | bytes 4000000 | tf_op jit(solution)/shard_map/pallas_call | solution.py:31
  34.4 40.3 %all_to_all.30 = bf16[4,128,3072]{2,1,0:T(8,128)(2,1)S(1)} all-to-all(bf16[4,128,3072]{2,1,0:T(8,128)(2,1)} %bitcast.17), channel_id=1, replica_groups=mesh['row'=8,'col_0'=8,'col_1'=4] {'col_1'}, dimensions={0} | all-to-all | bytes 6291456 | tf_op jit(solution)/shard_map/all_to_all | solution.py:358
  74.7 1.6 reduce_sum.12
  76.4 7.6 %all-to-all-start.2 = ((bf16[8,16,3072]{2,1,0:T(8,128)(2,1)}), bf16[8,16,3072]{2,1,0:T(8,128)(2,1)S(1)}, u32[]{:S(2)}, u32[]{:S(2)}) async-start(bf16[8,16,3072]{2,1,0:T(8,128)(2,1)} %bitcast.19), calls=%async_computation.3 | async-start | bytes 1572864 | tf_op jit(solution)/shard_map/all_to_all | solution.py:362
  84.0 1.0 fusion
  85.0 1.0 collective-permute-start.2
  86.0 1.2 collective-permute-start.1
  87.2 1.2 collective-permute-done.2.j3
  88.3 2.4 %collective-permute-done.1.j2 = bf16[16,2432]{1,0:T(8,128)(2,1)S(1)} collective-permute-done((bf16[16,2432]{1,0:T(8,128)(2,1)S(1)}, bf16[16,2432]{1,0:T(8,128)(2,1)S(1)}, u32[]{:S(2)}, u32[]{:S(2)}) %collective-permute-start.1) | collective-permute-done | bytes 77856 | tf_op jit(solution)/shard_map/ppermute | solution.py:304
  90.7 0.9 collective-permute-done.j1
  92.3 1.8 shard_map.138
  94.1 1.0 collective-permute-start.5
  95.1 1.0 collective-permute-start.4
  96.1 1.4 collective-permute-start.3
  97.6 1.4 collective-permute-done.5
  99.0 1.3 collective-permute-done.4
  100.4 1.6 pad_maximum_fusion
  102.0 3.2 %all-to-all-done.2.got = bf16[8,16,3072]{2,1,0:T(8,128)(2,1)S(1)} async-done(((bf16[8,16,3072]{2,1,0:T(8,128)(2,1)}), bf16[8,16,3072]{2,1,0:T(8,128)(2,1)S(1)}, u32[]{:S(2)}, u32[]{:S(2)}) %all-to-all-start.2) | async-done | bytes 786464 | tf_op jit(solution)/shard_map/all_to_all | solution.py:362
  105.3 0.9 copy-done.1
  106.1 2.3 %shard_map.140 = bf16[8,16,3200]{2,1,0:T(8,128)(2,1)} custom-call(bf16[8,16,3072]{2,1,0:T(8,128)(2,1)} %copy-done.1, f32[16,128]{1,0:T(8,128)} %get-tuple-element.30.scale, f32[16,128]{1,0:T(8,128)} %get-tuple-element.31.dots_b), custom_call_target="tpu_custom_call" | custom-call | bytes 1500000 | tf_op jit(solution)/shard_map/pallas_call | solution.py:31
  108.5 27.2 %all_to_all.31 = bf16[8,16,3200]{2,1,0:T(8,128)(2,1)S(1)} all-to-all(bf16[8,16,3200]{2,1,0:T(8,128)(2,1)} %shard_map.140), channel_id=1, replica_groups=mesh['row'=8,'col_0'=8,'col_1'=4] {'col_0'}, dimensions={0} | all-to-all | bytes 1638400 | tf_op jit(solution)/shard_map/all_to_all | solution.py:383
  135.9 31.4 %all_to_all.32 = bf16[4,128,3200]{2,1,0:T(8,128)(2,1)} all-to-all(bf16[4,128,3200]{2,1,0:T(8,128)(2,1)S(1)} %broadcast_in_dim.11), channel_id=1, replica_groups=mesh['row'=8,'col_0'=8,'col_1'=4] {'col_1'}, dimensions={0} | all-to-all | bytes 6553600 | tf_op jit(solution)/shard_map/all_to_all | solution.py:309
  167.2 7.1 %shard_map.141 = (bf16[512,640]{1,0:T(8,128)(2,1)}, f32[64,128]{1,0:T(8,128)}) custom-call(s32[3]{0:T(128)} %pad_add_fusion.pos, bf16[512,2304]{1,0:T(8,128)(2,1)} %all-gather.2.cloned.1.call-done.rest_0_.rest_2_, bf16[256,768]{1,0:T(8,128)(2,1)} %get-tuple-element.23.eg.rest_1_, bf16[256,768]{1,0:T(8,128)(2,1)} %get-tuple-element.24.eu.rest_2_, ...), custom_call_target="tpu_custom_call" | custom-call | flops 1409286144 | bytes 9000000 | tf_op jit(solution)/shard_map/pallas_call | solution.py:31
  174.3 15.4 %all-to-all-start.5 = ((bf16[8,64,640]{2,1,0:T(8,128)(2,1)}), bf16[8,64,640]{2,1,0:T(8,128)(2,1)S(1)}, u32[]{:S(2)}, u32[]{:S(2)}) async-start(bf16[8,64,640]{2,1,0:T(8,128)(2,1)} %bitcast.20), calls=%async_computation.6 | async-start | bytes 1310720 | tf_op jit(solution)/shard_map/all_to_all | solution.py:399
  189.6 7.4 %shard_map.143 = (bf16[256,1792]{1,0:T(8,128)(2,1)}, bf16[256,1792]{1,0:T(8,128)(2,1)}, bf16[1792,256]{1,0:T(8,128)(2,1)}) custom-call(s32[3]{0:T(128)} %pad_add_fusion.pos, s32[2,14]{1,0:T(2,128)} %mg.3, s32[2,14]{1,0:T(2,128)} %mu.3, s32[14,2]{1,0:T(8,128)} %copy.15.md, f32[1,256]{1,0:T(1,128)} %bitcast.23, bf16[512,512]{1,0:T(8,128)(2,1)} %bitcast.16, ...), custom_call_target="tpu_custom_call" | custom-call | flops 1409286144 | bytes 9000000 | tf_op jit(solution)/shard_map/pallas_call | solution.py:31
  197.0 3.5 %all-to-all-done.5.got = bf16[8,64,640]{2,1,0:T(8,128)(2,1)S(1)} async-done(((bf16[8,64,640]{2,1,0:T(8,128)(2,1)}), bf16[8,64,640]{2,1,0:T(8,128)(2,1)S(1)}, u32[]{:S(2)}, u32[]{:S(2)}) %all-to-all-start.5) | async-done | bytes 655392 | tf_op jit(solution)/shard_map/all_to_all | solution.py:399
  201.4 2.0 shard_map.142
  (23 shorter events, 4.9 us)
Async XLA Ops:
  8.8 16.1 %all-to-all-start = ((bf16[8,64,512]{2,1,0:T(8,128)(2,1)}), bf16[8,64,512]{2,1,0:T(8,128)(2,1)S(1)}, u32[]{:S(2)}, u32[]{:S(2)}) async-start(bf16[8,64,512]{2,1,0:T(8,128)(2,1)} %broadcast_in_dim.9), calls=%async_computation | async-start | bytes 1048576 | tf_op jit(solution)/shard_map/all_to_all | solution.py:309
  15.4 68.6 %reduce-scatter.2.cloned.1.call-start = ((), (), s32[]{:S(2)}) async-start(), calls=%async_computation.7 | async-start | bytes 2801664 | tf_op jit(solution)/shard_map/reduce_scatter | solution.py:359
  24.9 0.8 copy-start
  76.4 28.9 %all-to-all-start.2 = ((bf16[8,16,3072]{2,1,0:T(8,128)(2,1)}), bf16[8,16,3072]{2,1,0:T(8,128)(2,1)S(1)}, u32[]{:S(2)}, u32[]{:S(2)}) async-start(bf16[8,16,3072]{2,1,0:T(8,128)(2,1)} %bitcast.19), calls=%async_computation.3 | async-start | bytes 1572864 | tf_op jit(solution)/shard_map/all_to_all | solution.py:362
  84.0 83.3 %all-gather.2.cloned.1.call-start = ((), (), s32[]{:S(2)}) async-start(), calls=%async_computation.8 | async-start | bytes 2654208 | tf_op jit(solution)/shard_map/all_gather | solution.py:382
  85.0 3.3 %collective-permute-start.2 = (bf16[16,2432]{1,0:T(8,128)(2,1)S(1)}, bf16[16,2432]{1,0:T(8,128)(2,1)S(1)}, u32[]{:S(2)}, u32[]{:S(2)}) collective-permute-start(bf16[16,2432]{1,0:T(8,128)(2,1)S(1)} %get-tuple-element.40), channel_id=1, source_target_pairs={{0,3},{1,0},{2,1},{3,2},{4,7},{5,4},{6,5},{7,6},{8,11},{9,8},{10,9... | collective-permute-start | bytes 233480 | tf_op jit(solution)/shard_map/ppermute | solution.py:304
  86.0 4.8 %collective-permute-start.1 = (bf16[16,2432]{1,0:T(8,128)(2,1)S(1)}, bf16[16,2432]{1,0:T(8,128)(2,1)S(1)}, u32[]{:S(2)}, u32[]{:S(2)}) collective-permute-start(bf16[16,2432]{1,0:T(8,128)(2,1)S(1)} %get-tuple-element.41), channel_id=1, source_target_pairs={{0,2},{1,3},{2,0},{3,1},{4,6},{5,7},{6,4},{7,5},{8,10},{9,11},{10,... | collective-permute-start | bytes 233480 | tf_op jit(solution)/shard_map/ppermute | solution.py:304
  87.2 4.5 %collective-permute-start = (bf16[16,2432]{1,0:T(8,128)(2,1)S(1)}, bf16[16,2432]{1,0:T(8,128)(2,1)S(1)}, u32[]{:S(2)}, u32[]{:S(2)}) collective-permute-start(bf16[16,2432]{1,0:T(8,128)(2,1)S(1)} %get-tuple-element.42), channel_id=1, source_target_pairs={{0,1},{1,2},{2,3},{3,0},{4,5},{5,6},{6,7},{7,4},{8,9},{9,10},{10,1... | collective-permute-start | bytes 233480 | tf_op jit(solution)/shard_map/ppermute | solution.py:304
  88.3 3.3 %copy-start.3 = (bf16[16,2432]{1,0:T(8,128)(2,1)}, bf16[16,2432]{1,0:T(8,128)(2,1)S(1)}, u32[]{:S(2)}) copy-start(bf16[16,2432]{1,0:T(8,128)(2,1)S(1)} %collective-permute-done.2.j3) | copy-start | bytes 233476
  90.7 0.9 copy-start.4
  91.6 0.6 copy-start.5
  94.1 4.9 %collective-permute-start.5 = (bf16[16,2304]{1,0:T(8,128)(2,1)}, bf16[16,2304]{1,0:T(8,128)(2,1)S(1)}, u32[]{:S(2)}, u32[]{:S(2)}) collective-permute-start(bf16[16,2304]{1,0:T(8,128)(2,1)} %get-tuple-element.26), channel_id=1, source_target_pairs={{0,1},{1,2},{2,3},{3,0},{4,5},{5,6},{6,7},{7,4},{8,9},{9,10},{10,1... | collective-permute-start | bytes 221192 | tf_op jit(solution)/shard_map/ppermute | solution.py:304
  95.1 5.2 %collective-permute-start.4 = (bf16[16,2304]{1,0:T(8,128)(2,1)}, bf16[16,2304]{1,0:T(8,128)(2,1)S(1)}, u32[]{:S(2)}, u32[]{:S(2)}) collective-permute-start(bf16[16,2304]{1,0:T(8,128)(2,1)} %get-tuple-element.26), channel_id=1, source_target_pairs={{0,2},{1,3},{2,0},{3,1},{4,6},{5,7},{6,4},{7,5},{8,10},{9,11},{10,... | collective-permute-start | bytes 221192 | tf_op jit(solution)/shard_map/ppermute | solution.py:304
  96.1 4.2 %collective-permute-start.3 = (bf16[16,2304]{1,0:T(8,128)(2,1)}, bf16[16,2304]{1,0:T(8,128)(2,1)S(1)}, u32[]{:S(2)}, u32[]{:S(2)}) collective-permute-start(bf16[16,2304]{1,0:T(8,128)(2,1)} %get-tuple-element.26), channel_id=1, source_target_pairs={{0,3},{1,0},{2,1},{3,2},{4,7},{5,4},{6,5},{7,6},{8,11},{9,8},{10,9... | collective-permute-start | bytes 221192 | tf_op jit(solution)/shard_map/ppermute | solution.py:304
  105.3 0.9 copy-start.1
  174.3 26.3 %all-to-all-start.5 = ((bf16[8,64,640]{2,1,0:T(8,128)(2,1)}), bf16[8,64,640]{2,1,0:T(8,128)(2,1)S(1)}, u32[]{:S(2)}, u32[]{:S(2)}) async-start(bf16[8,64,640]{2,1,0:T(8,128)(2,1)} %bitcast.20), calls=%async_computation.6 | async-start | bytes 1310720 | tf_op jit(solution)/shard_map/all_to_all | solution.py:399
  200.6 0.9 copy-start.2
Sparse Core Ops, SparseCore 0:
  29.9 39.9 reduce-scatter.1
  102.1 54.7 all-gather.1

commit v5 on v4

--- a/solution.py
+++ b/solution.py
@@ -1,3 +1,5 @@
+import functools
+
 import jax
 import jax.numpy as jnp
 from jax import lax
@@ -9,7 +11,7 @@
 D = 8192
 BLK = 128
 NZ, NX = 8, 4
-HA, HB = 1024, 768
+HA, HB = 768, 1024
 COL = ("col_0", "col_1")
 ALL = ("row", "col_0", "col_1")
 norm_eps = 1e-05
@@ -114,8 +116,8 @@
             to = slice((tx * NZ + tz) * 16, (tx * NZ + tz) * 16 + 16)
             left[to, :width] = scaled(rows, nat, gain)
             left[to, width:] = rows[nat, width:]
-    for t in range(0, left.shape[0], 128):
-        products(left, slice(t, t + 128), (eg, eu, ed), part, slice(t, t + 128), HA)
+    for t in range(0, left.shape[0], 512):
+        products(left, slice(t, t + 512), (eg, eu, ed), part, slice(t, t + 512), HA)
 
 
 def part_b_kernel(pos, rows, gain, eg, eu, ed, part, left):
@@ -124,8 +126,19 @@
         left[to, :width] = scaled(rows, nat, gain)
         left[to, width:] = rows[nat, width:]
         part[to, 3 * HB :] = square_sums(rows, nat, width)
-    for t in range(0, left.shape[0], 128):
-        products(left, slice(t, t + 128), (eg, eu, ed), part, slice(t, t + 128), HB)
+    for t in range(0, left.shape[0], 512):
+        products(left, slice(t, t + 512), (eg, eu, ed), part, slice(t, t + 512), HB)
+
+
+def split_kernel(mine, after, *outs):
+    for j, out in enumerate(outs, 1):
+        out[...] = mine[j * 16 : j * 16 + 16, :]
+
+
+def join_kernel(*refs):
+    *pieces, _, out = refs
+    for j, v in enumerate(pieces):
+        out[j * 16 : j * 16 + 16, :] = v[...]
 
 
 def hidden_grads(sums, half, scale, to_act, to_gate, to_up):
@@ -193,32 +206,55 @@
     return copies
 
 
-def features_kernel(pos, *rest):
-    n = 9
-    both, own_scale, da, na, db, nb = rest[n : n + 6]
+def copies_kernel(x, grad, out):
+    width = x.shape[1]
+    for r in range(out.shape[0]):
+        out[r, :, :width] = x[...]
+        out[r, :, width:] = grad[...]
+
+
+def features(hid, half, eg, eu, ed, down, norm):
+    down[...] = nn(hid[:, :half], ed[...])
+    norm[...] = nt(hid[:, half : 2 * half], eg[...]) + nt(hid[:, 2 * half : 3 * half], eu[...])
+
+
+def features_a_kernel(pos, *rest):
+    n = 4
+    sums, scales, dots, own_scale, da, na = rest[n : n + 6]
     held, sems = rest[n + 6 : -1], rest[-1]
-    copies = fetch(rest[:n], held, sems)
-    gb, bg, bu, bd, ga, ag, au, ad, rows = held
-    width = ag.shape[0]
-    for hid, d, n, (eg, eu, ed), half, waits in (
-        (gb, db, nb, (bg, bu, bd), HB, copies[:4]),
-        (ga, da, na, (ag, au, ad), HA, copies[4:]),
-    ):
-        for c in waits:
-            c.wait()
-        for t in range(0, hid.shape[0], 128):
-            tok = slice(t, t + 128)
-            d[tok, :] = nn(hid[tok, :half], ed[...])
-            n[tok, :] = nt(hid[tok, half : 2 * half], eg[...]) + nt(
-                hid[tok, 2 * half : 3 * half], eu[...]
-            )
+    for c in fetch(rest[:n], held, sems):
+        c.wait()
+    ga, eg, eu, ed = held
+    width = eg.shape[0]
+    features(ga, HA, eg, eu, ed, da, na)
+    lane = lax.broadcasted_iota(jnp.int32, (16, BLK), 1)
+    for nat, in_a, _ in pieces_of_tokens(pos):
+        sums[nat, :width] = da[in_a, :]
+        sums[nat, width:] = na[in_a, :]
+        extra = ga[in_a, 3 * HA :].astype(f32)
+        scales[nat, :] = jnp.broadcast_to(lane_sum(extra, 0), (16, BLK))
+        dots[nat, :] = jnp.where(lane < 3, pltpu.roll(extra, BLK - 3, 1), 0.0).astype(bf16)
+    for tx in range(NX):
+        at = pl.ds(pl.multiple_of(tx * 128 + pos[0] * 16, 16), 16)
+        s = lane_sum(ga[at, 3 * HA :], 0)
+        own_scale[tx * 16 : tx * 16 + 16, :] = jnp.broadcast_to(s, (16, BLK))
+
+
+def features_b_kernel(pos, *rest):
+    n = 8
+    both, db, nb = rest[n : n + 3]
+    held, sems = rest[n + 3 : -1], rest[-1]
+    for c in fetch(rest[:n], held, sems):
+        c.wait()
+    gb, eg, eu, ed, sums, scales, dots, rows = held
+    width = eg.shape[0]
+    features(gb, HB, eg, eu, ed, db, nb)
     total = jnp.zeros((16, width), f32)
-    for nat, in_a, in_b in pieces_of_tokens(pos):
-        extra = ga[in_a, 3 * HA :]
-        both[nat, :width] = (da[in_a, :] + db[in_b, :]).astype(bf16)
-        grad = na[in_a, :] + nb[in_b, :]
+    for nat, _, in_b in pieces_of_tokens(pos):
+        both[nat, :width] = (sums[nat, :width] + db[in_b, :]).astype(bf16)
+        grad = sums[nat, width:] + nb[in_b, :]
         both[nat, width : 2 * width] = grad.astype(bf16)
-        total += grad * rows[nat, :width].astype(f32) * lane_sum(extra, 0)
+        total += grad * rows[nat, :width].astype(f32) * scales[nat, :1]
     gain_row = jnp.sum(total, axis=0, keepdims=True)
     lane = lax.broadcasted_iota(jnp.int32, (64, BLK), 1)
     line = lax.broadcasted_iota(jnp.int32, (64, BLK), 0)
@@ -229,17 +265,9 @@
         for i, v in enumerate(parts3(jnp.sum(picked, axis=1, keepdims=True))):
             shared = jnp.where(lane == 3 + 3 * c + i, v.astype(f32), shared)
     shared = shared.astype(bf16)
-    lane16 = lax.broadcasted_iota(jnp.int32, (16, BLK), 1)
     for tz in range(NZ):
-        for tx in range(NX):
-            nat = slice(tz * 64 + tx * 16, tz * 64 + tx * 16 + 16)
-            extra = ga[(tx * NZ + tz) * 16 : (tx * NZ + tz) * 16 + 16, 3 * HA :].astype(f32)
-            moved = jnp.where(lane16 < 3, pltpu.roll(extra, BLK - 3, 1), 0.0)
-            both[nat, 2 * width :] = shared[tx * 16 : tx * 16 + 16, :] + moved.astype(bf16)
-    for tx in range(NX):
-        at = pl.ds(pl.multiple_of(tx * 128 + pos[0] * 16, 16), 16)
-        s = lane_sum(ga[at, 3 * HA :], 0)
-        own_scale[tx * 16 : tx * 16 + 16, :] = jnp.broadcast_to(s, (16, BLK))
+        nat = slice(tz * 64, tz * 64 + 64)
+        both[nat, 2 * width :] = shared + dots[nat, :]
 
 
 def weights_kernel(pos, mg, mu, md, gain, *rest):
@@ -318,14 +346,25 @@
     pos = jnp.stack([lax.axis_index(a) for a in ALL]).astype(jnp.int32)
     gain = norm_gain[None, :]
     mine, width = layer_input.shape
-    rows = from_everyone(jnp.concatenate([layer_input, out_grad], axis=1), "row")
-    tokens = rows.shape[0]
+    n_rows = lax.axis_size("row")
+    tokens = n_rows * mine
     flops = 2 * tokens * width * 3
     a_cols, b_cols = 3 * HA, 3 * HB + BLK
 
     def out(*dims, dtype=bf16):
         return jax.ShapeDtypeStruct(dims, dtype)
 
+    (first,) = call(
+        copies_kernel,
+        (out(n_rows, mine, 2 * width),),
+        [vmem()] * 2,
+        [],
+        0,
+        600_000,
+        (layer_input, out_grad),
+        mib=16,
+    )
+    rows = lax.all_to_all(first, "row", 0, 0, tiled=True).reshape(tokens, -1)
     eff = call(
         masks_kernel,
         (*[out(width, HA)] * 2, out(HA, width), *[out(width, HB)] * 2, out(HB, width)),
@@ -334,6 +373,7 @@
         0,
         6_000_000,
         (mask_gate, mask_up, mask_down, w_gate, w_up, w_down),
+        mib=56,
     )
     eff_a, eff_b = eff[:3], eff[3:]
     left = pltpu.VMEM((tokens, 2 * width), bf16)
@@ -345,6 +385,7 @@
         flops * HA,
         4_000_000,
         (rows, gain, *eff_a),
+        mib=56,
     )
     (part_b,) = call(
         part_b_kernel,
@@ -354,11 +395,22 @@
         flops * HB,
         5_000_000,
         (pos, rows, gain, *eff_b),
+        mib=56,
     )
     got_a = lax.all_to_all(part_a.reshape(NX, -1, a_cols), "col_1", 0, 0, tiled=True)
     mine_b = lax.psum_scatter(part_b, "col_0", scatter_dimension=0, tiled=True)
-    got_b = [send(mine_b[j * 16 : j * 16 + 16], "col_1", j) for j in range(1, NX)]
     sum_a = jnp.sum(got_a.astype(f32), axis=0).astype(bf16).reshape(NZ, -1, a_cols)
+    others = call(
+        split_kernel,
+        tuple([out(16, b_cols)] * (NX - 1)),
+        [vmem(), pl.BlockSpec(memory_space=pl.ANY)],
+        [],
+        0,
+        600_000,
+        (mine_b, sum_a),
+        mib=16,
+    )
+    got_b = [send(v, "col_1", j) for j, v in enumerate(others, 1)]
     got_a = lax.all_to_all(sum_a, "col_0", 0, 0, tiled=True)
     send_b, scale, dots_b = call(
         grads_b_kernel,
@@ -368,6 +420,7 @@
         0,
         600_000,
         (mine_b, *got_b),
+        mib=16,
     )
     (copies_a,) = call(
         grads_a_kernel,
@@ -377,23 +430,47 @@
         0,
         1_500_000,
         (got_a, scale, dots_b),
+        mib=16,
     )
     near = [send_b] + [send(send_b, "col_1", -j) for j in range(1, NX)]
-    all_b = lax.all_gather(jnp.concatenate(near), "col_0", axis=0, tiled=True)
+    (near,) = call(
+        join_kernel,
+        (out(NX * 16, 3 * HB),),
+        [vmem()] * NX + [pl.BlockSpec(memory_space=pl.ANY)],
+        [],
+        0,
+        600_000,
+        (*near, got_a),
+        mib=16,
+    )
+    all_b = lax.all_gather(near, "col_0", axis=0, tiled=True)
     all_a = lax.all_to_all(copies_a, "col_0", 0, 0, tiled=True).reshape(-1, a_cols + BLK)
     all_a = from_everyone(all_a, "col_1")
 
     anywhere = pl.BlockSpec(memory_space=pl.ANY)
-    sources = (all_b, *eff_b, all_a, *eff_a, rows)
-    both, own_scale = call(
-        features_kernel,
-        (out(tokens, 2 * width + BLK), out(mine, BLK, dtype=f32)),
+    f_shape = functools.partial(out, dtype=f32)
+    sources = (all_a, *eff_a)
+    sums, scales, dots, own_scale = call(
+        features_a_kernel,
+        (f_shape(tokens, 2 * width), f_shape(tokens, BLK), out(tokens, BLK), f_shape(mine, BLK)),
         [smem()] + [anywhere] * len(sources),
-        [pltpu.VMEM((tokens, width), f32)] * 4
-        + [pltpu.VMEM(v.shape, bf16) for v in sources]
+        [pltpu.VMEM((tokens, width), f32)] * 2
+        + [pltpu.VMEM(v.shape, v.dtype) for v in sources]
         + [pltpu.SemaphoreType.DMA((len(sources),))],
-        flops * (HA + HB),
-        9_000_000,
+        flops * HA,
+        6_000_000,
+        (pos, *sources),
+    )
+    sources = (all_b, *eff_b, sums, scales, dots, rows)
+    (both,) = call(
+        features_b_kernel,
+        (out(tokens, 2 * width + BLK),),
+        [smem()] + [anywhere] * len(sources),
+        [pltpu.VMEM((tokens, width), f32)] * 2
+        + [pltpu.VMEM(v.shape, v.dtype) for v in sources]
+        + [pltpu.SemaphoreType.DMA((len(sources),))],
+        flops * HB,
+        8_000_000,
         (pos, *sources),
     )
     got = lax.all_to_all(both.reshape(-1, mine, both.shape[1]), "row", 0, 0, tiled=True)
@@ -416,6 +493,7 @@
         0,
         1_000_000,
         (got, layer_input, out_grad, gain, own_scale),
+        mib=16,
     )
     return (layer_out, input_grad, gain_grad[0], gate_wgrad, up_wgrad, down_wgrad)
 

time: 211 us -> 186 us (0.88)
  blocking collectives: 98.9 us -> 73.5 us
  waiting for transfers between devices: 17.6 us -> 25.2 us
  other arithmetic: 4.7 us -> 1.9 us
  starting transfers between devices: 35.3 us -> 32.6 us
    all_gather x1, waiting for transfers between devices: 0.01 us -> 10.6 us  [shards(): all_b = lax.all_gather(near, 'col_0', axis=0, tiled=True)]
    all_to_all x1, blocking collectives: 27.2 us -> 18.1 us  [shards(): lax.all_to_all(copies_a, 'col_0', 0, 0, tiled=True)]
    all_to_all x1, blocking collectives: 40.3 us -> 31.9 us  [shards(): lax.all_to_all(part_a.reshape(NX, -1, a_cols), 'col_1', 0, 0, tiled=True)]
    all_to_all x1, blocking collectives: 31.4 us -> 23.5 us  [from_everyone(): got = lax.all_to_all(copies, axis, split_axis=0, concat_axis=0, tiled=True)]
    all_to_all x1, starting transfers between devices: 15.4 us -> 9.26 us  [shards(): lax.all_to_all(both.reshape(-1, mine, both.shape[1]), 'row', 0, 0, tiled=...]
    ppermute x6, waiting for transfers between devices: 7.24 us -> 3.66 us  [send(): return lax.ppermute(v, axis, [(i, (i + step) % n) for i in range(n)])]
    ppermute x6, starting transfers between devices: 5.64 us -> 9.02 us  [send(): return lax.ppermute(v, axis, [(i, (i + step) % n) for i in range(n)])]
    concatenate x2 -> x0, other arithmetic: 2.41 us -> none  [the longest x1 1.63 us: shards(): all_b = lax.all_gather(jnp.concatenate(near), 'col_0', axis=0, tiled=True)]
  transfers between devices with their start and end apart: 11 -> 11, of which waited for: 8 -> 10; matrix products, arithmetic and copies ran while one was open for 3% -> 2% of each run, Pallas kernels for 10% -> 11%
where the time goes in v5:
time: 186 us; the launch traced here: 185 us
  blocking collectives  73.5 us (40%)
  Pallas kernels  32.6 us (18%)
  starting transfers between devices  32.6 us (18%)
  waiting for transfers between devices  25.2 us (14%)
  between operations  14.1 us (8%)
  local copies, waits for them, and re-layouts  4.87 us (3%)
  other arithmetic  1.9 us (1%)
    pallas_call x12, Pallas kernels, call(): pl.pallas_call(kernel, out_shape=outs, grid=grid, in_specs=in_specs, out_...  32.6 us
    all_to_all x1, blocking collectives, shards(): lax.all_to_all(part_a.reshape(NX, -1, a_cols), 'col_1', 0, 0, tiled=True)  31.9 us
    all_to_all x1, blocking collectives, from_everyone(): got = lax.all_to_all(copies, axis, split_axis=0, concat_axis=0, tiled=True)  23.5 us
    all_to_all x1, blocking collectives, shards(): lax.all_to_all(copies_a, 'col_0', 0, 0, tiled=True)  18.1 us
    all_gather x1, waiting for transfers between devices, shards(): all_b = lax.all_gather(near, 'col_0', axis=0, tiled=True)  10.6 us
    all_to_all x1, starting transfers between devices, shards(): lax.all_to_all(both.reshape(-1, mine, both.shape[1]), 'row', 0, 0, tiled=...  9.26 us
    ppermute x6, starting transfers between devices, send(): return lax.ppermute(v, axis, [(i, (i + step) % n) for i in range(n)])  9.02 us
    all_to_all x1, starting transfers between devices, shards(): got_a = lax.all_to_all(sum_a, 'col_0', 0, 0, tiled=True)  7.65 us
  transfers between devices with their start and end apart: 11, of which 10 were waited for; matrix products, arithmetic and copies ran while one was open for 2% of the time, Pallas kernels for 11%

profile of v5, /device:TPU:1, one launch (start us, length us, event | category | flops | bytes accessed | tf_op | source)
XLA Modules:
  0.0 184.9 jit_solution(9150314653176361531)
XLA Ops:
  7.9 0.8 copy-done.3
  8.7 0.8 shard_map.136
  9.5 6.6 %all-to-all-start = ((bf16[8,64,512]{2,1,0:T(8,128)(2,1)}), bf16[8,64,512]{2,1,0:T(8,128)(2,1)S(1)}, u32[]{:S(2)}, u32[]{:S(2)}) async-start(bf16[8,64,512]{2,1,0:T(8,128)(2,1)} %shard_map.136), calls=%async_computation | async-start | bytes 1048576 | tf_op jit(solution)/shard_map/all_to_all | solution.py:367
  16.2 1.4 copy.15.md
  17.5 3.9 %shard_map.137 = (bf16[256,768]{1,0:T(8,128)(2,1)}, bf16[256,768]{1,0:T(8,128)(2,1)}, bf16[768,256]{1,0:T(8,128)(2,1)}, bf16[256,1024]{1,0:T(8,128)(2,1)}, bf16[...) custom-call(s32[2,14]{1,0:T(2,128)} %mg.3, s32[2,14]{1,0:T(2,128)} %mu.3, s32[14,2]{1,0:T(8,128)} %copy.15.md, ...), custom_call_target="tpu_custom_call" | custom-call | bytes 6000000 | tf_op jit(solution)/shard_map/pallas_call | solution.py:33
  22.0 3.7 %all-to-all-done = bf16[8,64,512]{2,1,0:T(8,128)(2,1)S(1)} async-done(((bf16[8,64,512]{2,1,0:T(8,128)(2,1)}), bf16[8,64,512]{2,1,0:T(8,128)(2,1)S(1)}, u32[]{:S(2)}, u32[]{:S(2)}) %all-to-all-start) | async-done | bytes 524320 | tf_op jit(solution)/shard_map/all_to_all | solution.py:367
  25.7 0.8 copy-done.7
  26.5 4.3 %shard_map.138 = bf16[512,3200]{1,0:T(8,128)(2,1)} custom-call(s32[3]{0:T(128)} %pad_add_fusion.pos, bf16[512,512]{1,0:T(8,128)(2,1)} %bitcast.17, f32[1,256]{1,0:T(1,128)} %bitcast.11, bf16[256,1024]{1,0:T(8,128)(2,1)} %get-tuple-element.28.eg.rest_1_, bf16[256,1024]{1,0:T(8,128)(2,1)} %get-tuple-element.29.eu.rest_2_, ...), custom_call_target="tpu_custom_call" | custom-call | flops 805306368 | bytes 5000000 | tf_op jit(solution)/shard_map/pallas_call | solution.py:33
  30.8 3.6 %shard_map.139 = bf16[512,2304]{1,0:T(8,128)(2,1)} custom-call(bf16[512,512]{1,0:T(8,128)(2,1)} %bitcast.18, f32[1,256]{1,0:T(1,128)} %bitcast.12, bf16[256,768]{1,0:T(8,128)(2,1)} %get-tuple-element.31.eg.rest_1_, bf16[256,768]{1,0:T(8,128)(2,1)} %get-tuple-element.32.eu.rest_2_, bf16[768,256]{1,0:T(8,128)(2,1)} %get-tuple-element.33.ed.rest_3_), custom_call_target="tpu_custom_call" | custom-call | flops 603979776 | bytes 4000000 | tf_op jit(solution)/shard_map/pallas_call | solution.py:33
  34.4 31.9 %all_to_all.30 = bf16[4,128,2304]{2,1,0:T(8,128)(2,1)S(1)} all-to-all(bf16[4,128,2304]{2,1,0:T(8,128)(2,1)} %bitcast.21), channel_id=1, replica_groups=mesh['row'=8,'col_0'=8,'col_1'=4] {'col_1'}, dimensions={0} | all-to-all | bytes 4718592 | tf_op jit(solution)/shard_map/all_to_all | solution.py:400
  66.3 1.3 reduce_sum.12
  67.6 7.6 %all-to-all-start.2 = ((bf16[8,16,2304]{2,1,0:T(8,128)(2,1)}), bf16[8,16,2304]{2,1,0:T(8,128)(2,1)S(1)}, u32[]{:S(2)}, u32[]{:S(2)}) async-start(bf16[8,16,2304]{2,1,0:T(8,128)(2,1)} %bitcast.6.after), calls=%async_computation.3 | async-start | bytes 1179648 | tf_op jit(solution)/shard_map/all_to_all | solution.py:414
  75.3 1.9 %reduce-scatter.2.cloned.1.call-done.mine.part = bf16[64,3200]{1,0:T(8,128)(2,1)} async-done(((bf16[512,3200]{1,0:T(8,128)(2,1)}), bf16[64,3200]{1,0:T(8,128)(2,1)}) %reduce-scatter.2.cloned.1.call-update) | async-done | bytes 409616 | tf_op jit(solution)/shard_map/reduce_scatter | solution.py:401
  77.2 1.0 copy-done
  78.2 1.2 collective-permute-start
  79.4 2.4 %collective-permute-start.1 = (bf16[16,3200]{1,0:T(8,128)(2,1)S(1)}, bf16[16,3200]{1,0:T(8,128)(2,1)S(1)}, u32[]{:S(2)}, u32[]{:S(2)}) collective-permute-start(bf16[16,3200]{1,0:T(8,128)(2,1)S(1)} %get-tuple-element.35), channel_id=1, source_target_pairs={{0,2},{1,3},{2,0},{3,1},{4,6},{5,7},{6,4},{7,5},{8,10},{9,11},{10,... | collective-permute-start | bytes 307208 | tf_op jit(solution)/shard_map/ppermute | solution.py:332
  81.8 1.0 collective-permute-start.2
  83.0 2.0 %collective-permute-done.1.j2 = bf16[16,3200]{1,0:T(8,128)(2,1)S(1)} collective-permute-done((bf16[16,3200]{1,0:T(8,128)(2,1)S(1)}, bf16[16,3200]{1,0:T(8,128)(2,1)S(1)}, u32[]{:S(2)}, u32[]{:S(2)}) %collective-permute-start.1) | collective-permute-done | bytes 102432 | tf_op jit(solution)/shard_map/ppermute | solution.py:332
  85.8 0.9 collective-permute-start.5
  86.7 2.6 %collective-permute-start.4 = (bf16[16,3072]{1,0:T(8,128)(2,1)S(1)}, bf16[16,3072]{1,0:T(8,128)(2,1)S(1)}, u32[]{:S(2)}, u32[]{:S(2)}) collective-permute-start(bf16[16,3072]{1,0:T(8,128)(2,1)S(1)} %get-tuple-element.37.refs_0_), channel_id=1, source_target_pairs={{0,2},{1,3},{2,0},{3,1},{4,6},{5,7},{6,4},{7,5},{8,10},{9,11},{10,... | collective-permute-start | bytes 294920 | tf_op jit(solution)/shard_map/ppermute | solution.py:332
  89.3 0.9 collective-permute-start.3
  90.2 2.0 %all-to-all-done.2.refs_4_.got = bf16[8,16,2304]{2,1,0:T(8,128)(2,1)S(1)} async-done(((bf16[8,16,2304]{2,1,0:T(8,128)(2,1)}), bf16[8,16,2304]{2,1,0:T(8,128)(2,1)S(1)}, u32[]{:S(2)}, u32[]{:S(2)}) %all-to-all-start.2) | async-done | bytes 589856 | tf_op jit(solution)/shard_map/all_to_all | solution.py:414
  93.0 0.8 shard_map.142
  94.0 18.1 %all_to_all.31 = bf16[8,16,2432]{2,1,0:T(8,128)(2,1)S(1)} all-to-all(bf16[8,16,2432]{2,1,0:T(8,128)(2,1)S(1)} %shard_map.143), channel_id=1, replica_groups=mesh['row'=8,'col_0'=8,'col_1'=4] {'col_0'}, dimensions={0} | all-to-all | bytes 1245184 | tf_op jit(solution)/shard_map/all_to_all | solution.py:447
  112.4 23.5 %all_to_all.32 = bf16[4,128,2432]{2,1,0:T(8,128)(2,1)} all-to-all(bf16[4,128,2432]{2,1,0:T(8,128)(2,1)S(1)} %broadcast_in_dim.7), channel_id=1, replica_groups=mesh['row'=8,'col_0'=8,'col_1'=4] {'col_1'}, dimensions={0} | all-to-all | bytes 4980736 | tf_op jit(solution)/shard_map/all_to_all | solution.py:337
  135.9 4.8 %shard_map.144 = (f32[512,512]{1,0:T(8,128)}, f32[512,128]{1,0:T(8,128)}, bf16[512,128]{1,0:T(8,128)(2,1)}, f32[64,128]{1,0:T(8,128)}) custom-call(s32[3]{0:T(128)} %pad_add_fusion.pos, bf16[512,2432]{1,0:T(8,128)(2,1)} %bitcast.15, bf16[256,768]{1,0:T(8,128)(2,1)} %get-tuple-element.31.eg.rest_1_, bf16[256,768]{1,0:T(8,128)(2,1)} %get-tuple-element.32.eu.rest_2_, ...), custom_call_target="tpu_custom_call" | custom-call | flops 603979776 | bytes 6000000 | tf_op jit(solution)/shard_map/pallas_call | solution.py:33
  140.7 10.6 %all-gather.2.cloned.1.call-done.rest_0_.rest_2_ = bf16[512,3072]{1,0:T(8,128)(2,1)} async-done(((bf16[64,3072]{1,0:T(8,128)(2,1)}), bf16[512,3072]{1,0:T(8,128)(2,1)}) %all-gather.2.cloned.1.call-update) | async-done | bytes 3145744 | tf_op jit(solution)/shard_map/all_gather | solution.py:446
  151.3 5.8 %shard_map.145 = bf16[512,640]{1,0:T(8,128)(2,1)} custom-call(s32[3]{0:T(128)} %pad_add_fusion.pos, bf16[512,3072]{1,0:T(8,128)(2,1)} %all-gather.2.cloned.1.call-done.rest_0_.rest_2_, bf16[256,1024]{1,0:T(8,128)(2,1)} %get-tuple-element.28.eg.rest_1_, bf16[256,1024]{1,0:T(8,128)(2,1)} %get-tuple-element.29.eu.rest_2_, ...), custom_call_target="tpu_custom_call" | custom-call | flops 805306368 | bytes 8000000 | tf_op jit(solution)/shard_map/pallas_call | solution.py:33
  157.1 9.3 %all-to-all-start.5 = ((bf16[8,64,640]{2,1,0:T(8,128)(2,1)}), bf16[8,64,640]{2,1,0:T(8,128)(2,1)S(1)}, u32[]{:S(2)}, u32[]{:S(2)}) async-start(bf16[8,64,640]{2,1,0:T(8,128)(2,1)} %bitcast.22), calls=%async_computation.6 | async-start | bytes 1310720 | tf_op jit(solution)/shard_map/all_to_all | solution.py:476
  166.3 7.5 %shard_map.147 = (bf16[256,1792]{1,0:T(8,128)(2,1)}, bf16[256,1792]{1,0:T(8,128)(2,1)}, bf16[1792,256]{1,0:T(8,128)(2,1)}) custom-call(s32[3]{0:T(128)} %pad_add_fusion.pos, s32[2,14]{1,0:T(2,128)} %mg.3, s32[2,14]{1,0:T(2,128)} %mu.3, s32[14,2]{1,0:T(8,128)} %copy.15.md, f32[1,256]{1,0:T(1,128)} %bitcast.13, bf16[512,512]{1,0:T(8,128)(2,1)} %bitcast.20, ...), custom_call_target="tpu_custom_call" | custom-call | flops 1409286144 | bytes 9000000 | tf_op jit(solution)/shard_map/pallas_call | solution.py:33
  173.8 3.4 %all-to-all-done.5.got = bf16[8,64,640]{2,1,0:T(8,128)(2,1)S(1)} async-done(((bf16[8,64,640]{2,1,0:T(8,128)(2,1)}), bf16[8,64,640]{2,1,0:T(8,128)(2,1)S(1)}, u32[]{:S(2)}, u32[]{:S(2)}) %all-to-all-start.5) | async-done | bytes 655392 | tf_op jit(solution)/shard_map/all_to_all | solution.py:476
  177.2 0.8 shard_map.146
  (27 shorter events, 3.7 us)
Async XLA Ops:
  7.2 0.8 copy-start.1
  7.9 0.8 copy-start.3
  9.5 16.1 %all-to-all-start = ((bf16[8,64,512]{2,1,0:T(8,128)(2,1)}), bf16[8,64,512]{2,1,0:T(8,128)(2,1)S(1)}, u32[]{:S(2)}, u32[]{:S(2)}) async-start(bf16[8,64,512]{2,1,0:T(8,128)(2,1)} %shard_map.136), calls=%async_computation | async-start | bytes 1048576 | tf_op jit(solution)/shard_map/all_to_all | solution.py:367
  16.2 61.1 %reduce-scatter.2.cloned.1.call-start = ((), (), s32[]{:S(2)}) async-start(), calls=%async_computation.7 | async-start | bytes 3686400 | tf_op jit(solution)/shard_map/reduce_scatter | solution.py:401
  25.7 0.8 copy-start.7
  67.6 24.5 %all-to-all-start.2 = ((bf16[8,16,2304]{2,1,0:T(8,128)(2,1)}), bf16[8,16,2304]{2,1,0:T(8,128)(2,1)S(1)}, u32[]{:S(2)}, u32[]{:S(2)}) async-start(bf16[8,16,2304]{2,1,0:T(8,128)(2,1)} %bitcast.6.after), calls=%async_computation.3 | async-start | bytes 1179648 | tf_op jit(solution)/shard_map/all_to_all | solution.py:414
  75.3 76.0 %all-gather.2.cloned.1.call-start = ((), (), s32[]{:S(2)}) async-start(), calls=%async_computation.8 | async-start | bytes 3538944 | tf_op jit(solution)/shard_map/all_gather | solution.py:446
  77.2 1.0 copy-start
  78.2 4.8 %collective-permute-start = (bf16[16,3200]{1,0:T(8,128)(2,1)S(1)}, bf16[16,3200]{1,0:T(8,128)(2,1)S(1)}, u32[]{:S(2)}, u32[]{:S(2)}) collective-permute-start(bf16[16,3200]{1,0:T(8,128)(2,1)S(1)} %get-tuple-element.34), channel_id=1, source_target_pairs={{0,1},{1,2},{2,3},{3,0},{4,5},{5,6},{6,7},{7,4},{8,9},{9,10},{10,1... | collective-permute-start | bytes 307208 | tf_op jit(solution)/shard_map/ppermute | solution.py:332
  79.4 5.6 %collective-permute-start.1 = (bf16[16,3200]{1,0:T(8,128)(2,1)S(1)}, bf16[16,3200]{1,0:T(8,128)(2,1)S(1)}, u32[]{:S(2)}, u32[]{:S(2)}) collective-permute-start(bf16[16,3200]{1,0:T(8,128)(2,1)S(1)} %get-tuple-element.35), channel_id=1, source_target_pairs={{0,2},{1,3},{2,0},{3,1},{4,6},{5,7},{6,4},{7,5},{8,10},{9,11},{10,... | collective-permute-start | bytes 307208 | tf_op jit(solution)/shard_map/ppermute | solution.py:332
  81.8 3.8 %collective-permute-start.2 = (bf16[16,3200]{1,0:T(8,128)(2,1)S(1)}, bf16[16,3200]{1,0:T(8,128)(2,1)S(1)}, u32[]{:S(2)}, u32[]{:S(2)}) collective-permute-start(bf16[16,3200]{1,0:T(8,128)(2,1)S(1)} %get-tuple-element.36), channel_id=1, source_target_pairs={{0,3},{1,0},{2,1},{3,2},{4,7},{5,4},{6,5},{7,6},{8,11},{9,8},{10,9... | collective-permute-start | bytes 307208 | tf_op jit(solution)/shard_map/ppermute | solution.py:332
  85.8 6.4 %collective-permute-start.5 = (bf16[16,3072]{1,0:T(8,128)(2,1)S(1)}, bf16[16,3072]{1,0:T(8,128)(2,1)S(1)}, u32[]{:S(2)}, u32[]{:S(2)}) collective-permute-start(bf16[16,3072]{1,0:T(8,128)(2,1)S(1)} %get-tuple-element.37.refs_0_), channel_id=1, source_target_pairs={{0,1},{1,2},{2,3},{3,0},{4,5},{5,6},{6,7},{7,4},{8,9},{9,10},{10,1... | collective-permute-start | bytes 294920 | tf_op jit(solution)/shard_map/ppermute | solution.py:332
  86.7 5.6 %collective-permute-start.4 = (bf16[16,3072]{1,0:T(8,128)(2,1)S(1)}, bf16[16,3072]{1,0:T(8,128)(2,1)S(1)}, u32[]{:S(2)}, u32[]{:S(2)}) collective-permute-start(bf16[16,3072]{1,0:T(8,128)(2,1)S(1)} %get-tuple-element.37.refs_0_), channel_id=1, source_target_pairs={{0,2},{1,3},{2,0},{3,1},{4,6},{5,7},{6,4},{7,5},{8,10},{9,11},{10,... | collective-permute-start | bytes 294920 | tf_op jit(solution)/shard_map/ppermute | solution.py:332
  89.3 3.8 %collective-permute-start.3 = (bf16[16,3072]{1,0:T(8,128)(2,1)S(1)}, bf16[16,3072]{1,0:T(8,128)(2,1)S(1)}, u32[]{:S(2)}, u32[]{:S(2)}) collective-permute-start(bf16[16,3072]{1,0:T(8,128)(2,1)S(1)} %get-tuple-element.37.refs_0_), channel_id=1, source_target_pairs={{0,3},{1,0},{2,1},{3,2},{4,7},{5,4},{6,5},{7,6},{8,11},{9,8},{10,9... | collective-permute-start | bytes 294920 | tf_op jit(solution)/shard_map/ppermute | solution.py:332
  157.1 20.1 %all-to-all-start.5 = ((bf16[8,64,640]{2,1,0:T(8,128)(2,1)}), bf16[8,64,640]{2,1,0:T(8,128)(2,1)S(1)}, u32[]{:S(2)}, u32[]{:S(2)}) async-start(bf16[8,64,640]{2,1,0:T(8,128)(2,1)} %bitcast.22), calls=%async_computation.6 | async-start | bytes 1310720 | tf_op jit(solution)/shard_map/all_to_all | solution.py:476
  166.3 10.9 %copy-start.2 = (bf16[64,256]{1,0:T(8,128)(2,1)S(1)}, bf16[64,256]{1,0:T(8,128)(2,1)}, u32[]{:S(2)}) copy-start(bf16[64,256]{1,0:T(8,128)(2,1)} %x.3) | copy-start | bytes 98308
  166.3 10.9 %copy-start.4 = (bf16[64,256]{1,0:T(8,128)(2,1)S(1)}, bf16[64,256]{1,0:T(8,128)(2,1)}, u32[]{:S(2)}) copy-start(bf16[64,256]{1,0:T(8,128)(2,1)} %grad.3) | copy-start | bytes 98308
  166.3 10.9 %copy-start.5 = (f32[64,128]{1,0:T(8,128)S(1)}, f32[64,128]{1,0:T(8,128)}, u32[]{:S(2)}) copy-start(f32[64,128]{1,0:T(8,128)} %get-tuple-element.43.scale) | copy-start | bytes 98308
  166.3 10.9 %copy-start.6 = (f32[256]{0:T(256)S(1)}, f32[256]{0:T(256)}, u32[]{:S(2)}) copy-start(f32[256]{0:T(256)} %param.10) | copy-start | bytes 3076
Sparse Core Ops, SparseCore 0:
  30.9 46.2 reduce-scatter.1
  94.0 57.2 all-gather.1

commit v6 on v5

--- a/solution.py
+++ b/solution.py
@@ -244,11 +244,14 @@
     n = 8
     both, db, nb = rest[n : n + 3]
     held, sems = rest[n + 3 : -1], rest[-1]
-    for c in fetch(rest[:n], held, sems):
+    copies = fetch(rest[:n], held, sems)
+    for c in copies[:4]:
         c.wait()
     gb, eg, eu, ed, sums, scales, dots, rows = held
     width = eg.shape[0]
     features(gb, HB, eg, eu, ed, db, nb)
+    for c in copies[4:]:
+        c.wait()
     total = jnp.zeros((16, width), f32)
     for nat, _, in_b in pieces_of_tokens(pos):
         both[nat, :width] = (sums[nat, :width] + db[in_b, :]).astype(bf16)
@@ -362,7 +365,7 @@
         0,
         600_000,
         (layer_input, out_grad),
-        mib=16,
+        mib=56,
     )
     rows = lax.all_to_all(first, "row", 0, 0, tiled=True).reshape(tokens, -1)
     eff = call(

time: 186 us -> 185 us (level)
    unnamed x17 -> x13, local copies, waits for them, and re-layouts: 4.7 us -> 3.18 us
where the time goes in v6:
time: 185 us; the launch traced here: 184 us
  blocking collectives  73.7 us (40%)
  starting transfers between devices  33 us (18%)
  Pallas kernels  32.8 us (18%)
  waiting for transfers between devices  25.1 us (14%)
  between operations  14.1 us (8%)
  local copies, waits for them, and re-layouts  3.35 us (2%)
  other arithmetic  1.91 us (1%)
    pallas_call x12, Pallas kernels, call(): pl.pallas_call(kernel, out_shape=outs, grid=grid, in_specs=in_specs, out_...  32.8 us
    all_to_all x1, blocking collectives, shards(): lax.all_to_all(part_a.reshape(NX, -1, a_cols), 'col_1', 0, 0, tiled=True)  31.9 us
    all_to_all x1, blocking collectives, from_everyone(): got = lax.all_to_all(copies, axis, split_axis=0, concat_axis=0, tiled=True)  24.2 us
    all_to_all x1, blocking collectives, shards(): lax.all_to_all(copies_a, 'col_0', 0, 0, tiled=True)  17.6 us
    all_gather x1, waiting for transfers between devices, shards(): all_b = lax.all_gather(near, 'col_0', axis=0, tiled=True)  10.6 us
    all_to_all x1, starting transfers between devices, shards(): lax.all_to_all(both.reshape(-1, mine, both.shape[1]), 'row', 0, 0, tiled=...  9.51 us
    ppermute x6, starting transfers between devices, send(): return lax.ppermute(v, axis, [(i, (i + step) % n) for i in range(n)])  9.09 us
    all_to_all x1, starting transfers between devices, shards(): got_a = lax.all_to_all(sum_a, 'col_0', 0, 0, tiled=True)  7.68 us
  transfers between devices with their start and end apart: 11, of which 10 were waited for; matrix products, arithmetic and copies ran while one was open for 2% of the time, Pallas kernels for 11%

profile of v6, /device:TPU:1, one launch (start us, length us, event | category | flops | bytes accessed | tf_op | source)
XLA Modules:
  0.0 183.9 jit_solution(7364553102457664798)
XLA Ops:
  7.2 1.6 shard_map.136
  8.8 6.6 %all-to-all-start = ((bf16[8,64,512]{2,1,0:T(8,128)(2,1)}), bf16[8,64,512]{2,1,0:T(8,128)(2,1)S(1)}, u32[]{:S(2)}, u32[]{:S(2)}) async-start(bf16[8,64,512]{2,1,0:T(8,128)(2,1)} %shard_map.136), calls=%async_computation | async-start | bytes 1048576 | tf_op jit(solution)/shard_map/all_to_all | solution.py:370
  15.4 1.4 copy.15.md
  16.8 3.9 %shard_map.137 = (bf16[256,768]{1,0:T(8,128)(2,1)}, bf16[256,768]{1,0:T(8,128)(2,1)}, bf16[768,256]{1,0:T(8,128)(2,1)}, bf16[256,1024]{1,0:T(8,128)(2,1)}, bf16[...) custom-call(s32[2,14]{1,0:T(2,128)} %mg.3, s32[2,14]{1,0:T(2,128)} %mu.3, s32[14,2]{1,0:T(8,128)} %copy.15.md, ...), custom_call_target="tpu_custom_call" | custom-call | bytes 6000000 | tf_op jit(solution)/shard_map/pallas_call | solution.py:33
  21.3 3.7 %all-to-all-done = bf16[8,64,512]{2,1,0:T(8,128)(2,1)S(1)} async-done(((bf16[8,64,512]{2,1,0:T(8,128)(2,1)}), bf16[8,64,512]{2,1,0:T(8,128)(2,1)S(1)}, u32[]{:S(2)}, u32[]{:S(2)}) %all-to-all-start) | async-done | bytes 524320 | tf_op jit(solution)/shard_map/all_to_all | solution.py:370
  24.9 0.8 copy-done.5
  25.7 4.3 %shard_map.138 = bf16[512,3200]{1,0:T(8,128)(2,1)} custom-call(s32[3]{0:T(128)} %pad_add_fusion.pos, bf16[512,512]{1,0:T(8,128)(2,1)} %bitcast.17, f32[1,256]{1,0:T(1,128)} %bitcast.11, bf16[256,1024]{1,0:T(8,128)(2,1)} %get-tuple-element.28.eg.rest_1_, bf16[256,1024]{1,0:T(8,128)(2,1)} %get-tuple-element.29.eu.rest_2_, ...), custom_call_target="tpu_custom_call" | custom-call | flops 805306368 | bytes 5000000 | tf_op jit(solution)/shard_map/pallas_call | solution.py:33
  30.0 3.6 %shard_map.139 = bf16[512,2304]{1,0:T(8,128)(2,1)} custom-call(bf16[512,512]{1,0:T(8,128)(2,1)} %bitcast.18, f32[1,256]{1,0:T(1,128)} %bitcast.12, bf16[256,768]{1,0:T(8,128)(2,1)} %get-tuple-element.31.eg.rest_1_, bf16[256,768]{1,0:T(8,128)(2,1)} %get-tuple-element.32.eu.rest_2_, bf16[768,256]{1,0:T(8,128)(2,1)} %get-tuple-element.33.ed.rest_3_), custom_call_target="tpu_custom_call" | custom-call | flops 603979776 | bytes 4000000 | tf_op jit(solution)/shard_map/pallas_call | solution.py:33
  33.7 31.9 %all_to_all.30 = bf16[4,128,2304]{2,1,0:T(8,128)(2,1)S(1)} all-to-all(bf16[4,128,2304]{2,1,0:T(8,128)(2,1)} %bitcast.21), channel_id=1, replica_groups=mesh['row'=8,'col_0'=8,'col_1'=4] {'col_1'}, dimensions={0} | all-to-all | bytes 4718592 | tf_op jit(solution)/shard_map/all_to_all | solution.py:403
  65.5 1.3 reduce_sum.12
  66.9 7.7 %all-to-all-start.2 = ((bf16[8,16,2304]{2,1,0:T(8,128)(2,1)}), bf16[8,16,2304]{2,1,0:T(8,128)(2,1)S(1)}, u32[]{:S(2)}, u32[]{:S(2)}) async-start(bf16[8,16,2304]{2,1,0:T(8,128)(2,1)} %bitcast.6.after), calls=%async_computation.3 | async-start | bytes 1179648 | tf_op jit(solution)/shard_map/all_to_all | solution.py:417
  74.6 1.9 %reduce-scatter.2.cloned.1.call-done.mine.part = bf16[64,3200]{1,0:T(8,128)(2,1)} async-done(((bf16[512,3200]{1,0:T(8,128)(2,1)}), bf16[64,3200]{1,0:T(8,128)(2,1)}) %reduce-scatter.2.cloned.1.call-update) | async-done | bytes 409616 | tf_op jit(solution)/shard_map/reduce_scatter | solution.py:404
  76.4 1.0 copy-done
  77.5 1.1 collective-permute-start
  78.6 2.4 %collective-permute-start.1 = (bf16[16,3200]{1,0:T(8,128)(2,1)S(1)}, bf16[16,3200]{1,0:T(8,128)(2,1)S(1)}, u32[]{:S(2)}, u32[]{:S(2)}) collective-permute-start(bf16[16,3200]{1,0:T(8,128)(2,1)S(1)} %get-tuple-element.35), channel_id=1, source_target_pairs={{0,2},{1,3},{2,0},{3,1},{4,6},{5,7},{6,4},{7,5},{8,10},{9,11},{10,... | collective-permute-start | bytes 307208 | tf_op jit(solution)/shard_map/ppermute | solution.py:335
  81.0 1.1 collective-permute-start.2
  82.3 1.9 %collective-permute-done.1.j2 = bf16[16,3200]{1,0:T(8,128)(2,1)S(1)} collective-permute-done((bf16[16,3200]{1,0:T(8,128)(2,1)S(1)}, bf16[16,3200]{1,0:T(8,128)(2,1)S(1)}, u32[]{:S(2)}, u32[]{:S(2)}) %collective-permute-start.1) | collective-permute-done | bytes 102432 | tf_op jit(solution)/shard_map/ppermute | solution.py:335
  84.9 1.0 collective-permute-start.5
  85.9 2.6 %collective-permute-start.4 = (bf16[16,3072]{1,0:T(8,128)(2,1)S(1)}, bf16[16,3072]{1,0:T(8,128)(2,1)S(1)}, u32[]{:S(2)}, u32[]{:S(2)}) collective-permute-start(bf16[16,3072]{1,0:T(8,128)(2,1)S(1)} %get-tuple-element.37.refs_0_), channel_id=1, source_target_pairs={{0,2},{1,3},{2,0},{3,1},{4,6},{5,7},{6,4},{7,5},{8,10},{9,11},{10,... | collective-permute-start | bytes 294920 | tf_op jit(solution)/shard_map/ppermute | solution.py:335
  88.5 0.9 collective-permute-start.3
  89.4 2.0 %all-to-all-done.2.refs_4_.got = bf16[8,16,2304]{2,1,0:T(8,128)(2,1)S(1)} async-done(((bf16[8,16,2304]{2,1,0:T(8,128)(2,1)}), bf16[8,16,2304]{2,1,0:T(8,128)(2,1)S(1)}, u32[]{:S(2)}, u32[]{:S(2)}) %all-to-all-start.2) | async-done | bytes 589856 | tf_op jit(solution)/shard_map/all_to_all | solution.py:417
  91.5 0.7 collective-permute-done.3.refs_1_
  92.2 0.8 shard_map.142
  93.3 17.6 %all_to_all.31 = bf16[8,16,2432]{2,1,0:T(8,128)(2,1)S(1)} all-to-all(bf16[8,16,2432]{2,1,0:T(8,128)(2,1)S(1)} %shard_map.143), channel_id=1, replica_groups=mesh['row'=8,'col_0'=8,'col_1'=4] {'col_0'}, dimensions={0} | all-to-all | bytes 1245184 | tf_op jit(solution)/shard_map/all_to_all | solution.py:450
  111.1 24.2 %all_to_all.32 = bf16[4,128,2432]{2,1,0:T(8,128)(2,1)} all-to-all(bf16[4,128,2432]{2,1,0:T(8,128)(2,1)S(1)} %broadcast_in_dim.7), channel_id=1, replica_groups=mesh['row'=8,'col_0'=8,'col_1'=4] {'col_1'}, dimensions={0} | all-to-all | bytes 4980736 | tf_op jit(solution)/shard_map/all_to_all | solution.py:340
  135.2 4.8 %shard_map.144 = (f32[512,512]{1,0:T(8,128)}, f32[512,128]{1,0:T(8,128)}, bf16[512,128]{1,0:T(8,128)(2,1)}, f32[64,128]{1,0:T(8,128)}) custom-call(s32[3]{0:T(128)} %pad_add_fusion.pos, bf16[512,2432]{1,0:T(8,128)(2,1)} %bitcast.15, bf16[256,768]{1,0:T(8,128)(2,1)} %get-tuple-element.31.eg.rest_1_, bf16[256,768]{1,0:T(8,128)(2,1)} %get-tuple-element.32.eu.rest_2_, ...), custom_call_target="tpu_custom_call" | custom-call | flops 603979776 | bytes 6000000 | tf_op jit(solution)/shard_map/pallas_call | solution.py:33
  140.0 10.6 %all-gather.2.cloned.1.call-done.rest_0_.rest_2_ = bf16[512,3072]{1,0:T(8,128)(2,1)} async-done(((bf16[64,3072]{1,0:T(8,128)(2,1)}), bf16[512,3072]{1,0:T(8,128)(2,1)}) %all-gather.2.cloned.1.call-update) | async-done | bytes 3145744 | tf_op jit(solution)/shard_map/all_gather | solution.py:449
  150.6 5.2 %shard_map.145 = bf16[512,640]{1,0:T(8,128)(2,1)} custom-call(s32[3]{0:T(128)} %pad_add_fusion.pos, bf16[512,3072]{1,0:T(8,128)(2,1)} %all-gather.2.cloned.1.call-done.rest_0_.rest_2_, bf16[256,1024]{1,0:T(8,128)(2,1)} %get-tuple-element.28.eg.rest_1_, bf16[256,1024]{1,0:T(8,128)(2,1)} %get-tuple-element.29.eu.rest_2_, ...), custom_call_target="tpu_custom_call" | custom-call | flops 805306368 | bytes 8000000 | tf_op jit(solution)/shard_map/pallas_call | solution.py:33
  155.8 9.5 %all-to-all-start.5 = ((bf16[8,64,640]{2,1,0:T(8,128)(2,1)}), bf16[8,64,640]{2,1,0:T(8,128)(2,1)S(1)}, u32[]{:S(2)}, u32[]{:S(2)}) async-start(bf16[8,64,640]{2,1,0:T(8,128)(2,1)} %bitcast.22), calls=%async_computation.6 | async-start | bytes 1310720 | tf_op jit(solution)/shard_map/all_to_all | solution.py:479
  165.3 7.5 %shard_map.147 = (bf16[256,1792]{1,0:T(8,128)(2,1)}, bf16[256,1792]{1,0:T(8,128)(2,1)}, bf16[1792,256]{1,0:T(8,128)(2,1)}) custom-call(s32[3]{0:T(128)} %pad_add_fusion.pos, s32[2,14]{1,0:T(2,128)} %mg.3, s32[2,14]{1,0:T(2,128)} %mu.3, s32[14,2]{1,0:T(8,128)} %copy.15.md, f32[1,256]{1,0:T(1,128)} %bitcast.13, bf16[512,512]{1,0:T(8,128)(2,1)} %bitcast.20, ...), custom_call_target="tpu_custom_call" | custom-call | flops 1409286144 | bytes 9000000 | tf_op jit(solution)/shard_map/pallas_call | solution.py:33
  172.8 3.4 %all-to-all-done.5.got = bf16[8,64,640]{2,1,0:T(8,128)(2,1)S(1)} async-done(((bf16[8,64,640]{2,1,0:T(8,128)(2,1)}), bf16[8,64,640]{2,1,0:T(8,128)(2,1)S(1)}, u32[]{:S(2)}, u32[]{:S(2)}) %all-to-all-start.5) | async-done | bytes 655392 | tf_op jit(solution)/shard_map/all_to_all | solution.py:479
  176.2 0.8 shard_map.146
  (23 shorter events, 2.2 us)
Async XLA Ops:
  8.8 16.1 %all-to-all-start = ((bf16[8,64,512]{2,1,0:T(8,128)(2,1)}), bf16[8,64,512]{2,1,0:T(8,128)(2,1)S(1)}, u32[]{:S(2)}, u32[]{:S(2)}) async-start(bf16[8,64,512]{2,1,0:T(8,128)(2,1)} %shard_map.136), calls=%async_computation | async-start | bytes 1048576 | tf_op jit(solution)/shard_map/all_to_all | solution.py:370
  15.4 61.0 %reduce-scatter.2.cloned.1.call-start = ((), (), s32[]{:S(2)}) async-start(), calls=%async_computation.7 | async-start | bytes 3686400 | tf_op jit(solution)/shard_map/reduce_scatter | solution.py:404
  24.9 0.8 copy-start.5
  66.9 24.6 %all-to-all-start.2 = ((bf16[8,16,2304]{2,1,0:T(8,128)(2,1)}), bf16[8,16,2304]{2,1,0:T(8,128)(2,1)S(1)}, u32[]{:S(2)}, u32[]{:S(2)}) async-start(bf16[8,16,2304]{2,1,0:T(8,128)(2,1)} %bitcast.6.after), calls=%async_computation.3 | async-start | bytes 1179648 | tf_op jit(solution)/shard_map/all_to_all | solution.py:417
  74.5 76.1 %all-gather.2.cloned.1.call-start = ((), (), s32[]{:S(2)}) async-start(), calls=%async_computation.8 | async-start | bytes 3538944 | tf_op jit(solution)/shard_map/all_gather | solution.py:449
  76.4 1.0 copy-start
  77.5 4.8 %collective-permute-start = (bf16[16,3200]{1,0:T(8,128)(2,1)S(1)}, bf16[16,3200]{1,0:T(8,128)(2,1)S(1)}, u32[]{:S(2)}, u32[]{:S(2)}) collective-permute-start(bf16[16,3200]{1,0:T(8,128)(2,1)S(1)} %get-tuple-element.34), channel_id=1, source_target_pairs={{0,1},{1,2},{2,3},{3,0},{4,5},{5,6},{6,7},{7,4},{8,9},{9,10},{10,1... | collective-permute-start | bytes 307208 | tf_op jit(solution)/shard_map/ppermute | solution.py:335
  78.6 5.6 %collective-permute-start.1 = (bf16[16,3200]{1,0:T(8,128)(2,1)S(1)}, bf16[16,3200]{1,0:T(8,128)(2,1)S(1)}, u32[]{:S(2)}, u32[]{:S(2)}) collective-permute-start(bf16[16,3200]{1,0:T(8,128)(2,1)S(1)} %get-tuple-element.35), channel_id=1, source_target_pairs={{0,2},{1,3},{2,0},{3,1},{4,6},{5,7},{6,4},{7,5},{8,10},{9,11},{10,... | collective-permute-start | bytes 307208 | tf_op jit(solution)/shard_map/ppermute | solution.py:335
  81.0 3.8 %collective-permute-start.2 = (bf16[16,3200]{1,0:T(8,128)(2,1)S(1)}, bf16[16,3200]{1,0:T(8,128)(2,1)S(1)}, u32[]{:S(2)}, u32[]{:S(2)}) collective-permute-start(bf16[16,3200]{1,0:T(8,128)(2,1)S(1)} %get-tuple-element.36), channel_id=1, source_target_pairs={{0,3},{1,0},{2,1},{3,2},{4,7},{5,4},{6,5},{7,6},{8,11},{9,8},{10,9... | collective-permute-start | bytes 307208 | tf_op jit(solution)/shard_map/ppermute | solution.py:335
  84.9 6.5 %collective-permute-start.5 = (bf16[16,3072]{1,0:T(8,128)(2,1)S(1)}, bf16[16,3072]{1,0:T(8,128)(2,1)S(1)}, u32[]{:S(2)}, u32[]{:S(2)}) collective-permute-start(bf16[16,3072]{1,0:T(8,128)(2,1)S(1)} %get-tuple-element.37.refs_0_), channel_id=1, source_target_pairs={{0,1},{1,2},{2,3},{3,0},{4,5},{5,6},{6,7},{7,4},{8,9},{9,10},{10,1... | collective-permute-start | bytes 294920 | tf_op jit(solution)/shard_map/ppermute | solution.py:335
  85.9 5.6 %collective-permute-start.4 = (bf16[16,3072]{1,0:T(8,128)(2,1)S(1)}, bf16[16,3072]{1,0:T(8,128)(2,1)S(1)}, u32[]{:S(2)}, u32[]{:S(2)}) collective-permute-start(bf16[16,3072]{1,0:T(8,128)(2,1)S(1)} %get-tuple-element.37.refs_0_), channel_id=1, source_target_pairs={{0,2},{1,3},{2,0},{3,1},{4,6},{5,7},{6,4},{7,5},{8,10},{9,11},{10,... | collective-permute-start | bytes 294920 | tf_op jit(solution)/shard_map/ppermute | solution.py:335
  88.5 3.8 %collective-permute-start.3 = (bf16[16,3072]{1,0:T(8,128)(2,1)S(1)}, bf16[16,3072]{1,0:T(8,128)(2,1)S(1)}, u32[]{:S(2)}, u32[]{:S(2)}) collective-permute-start(bf16[16,3072]{1,0:T(8,128)(2,1)S(1)} %get-tuple-element.37.refs_0_), channel_id=1, source_target_pairs={{0,3},{1,0},{2,1},{3,2},{4,7},{5,4},{6,5},{7,6},{8,11},{9,8},{10,9... | collective-permute-start | bytes 294920 | tf_op jit(solution)/shard_map/ppermute | solution.py:335
  155.8 20.4 %all-to-all-start.5 = ((bf16[8,64,640]{2,1,0:T(8,128)(2,1)}), bf16[8,64,640]{2,1,0:T(8,128)(2,1)S(1)}, u32[]{:S(2)}, u32[]{:S(2)}) async-start(bf16[8,64,640]{2,1,0:T(8,128)(2,1)} %bitcast.22), calls=%async_computation.6 | async-start | bytes 1310720 | tf_op jit(solution)/shard_map/all_to_all | solution.py:479
  165.3 10.9 %copy-start.1 = (bf16[64,256]{1,0:T(8,128)(2,1)S(1)}, bf16[64,256]{1,0:T(8,128)(2,1)}, u32[]{:S(2)}) copy-start(bf16[64,256]{1,0:T(8,128)(2,1)} %x.3) | copy-start | bytes 98308
  165.3 10.9 %copy-start.2 = (bf16[64,256]{1,0:T(8,128)(2,1)S(1)}, bf16[64,256]{1,0:T(8,128)(2,1)}, u32[]{:S(2)}) copy-start(bf16[64,256]{1,0:T(8,128)(2,1)} %grad.3) | copy-start | bytes 98308
  165.3 10.9 %copy-start.3 = (f32[64,128]{1,0:T(8,128)S(1)}, f32[64,128]{1,0:T(8,128)}, u32[]{:S(2)}) copy-start(f32[64,128]{1,0:T(8,128)} %get-tuple-element.43.scale) | copy-start | bytes 98308
  165.3 10.9 %copy-start.4 = (f32[256]{0:T(256)S(1)}, f32[256]{0:T(256)}, u32[]{:S(2)}) copy-start(f32[256]{0:T(256)} %param.10) | copy-start | bytes 3076
Sparse Core Ops, SparseCore 0:
  30.2 46.2 reduce-scatter.1
  93.2 57.3 all-gather.1

commit v7 on v6

--- a/solution.py
+++ b/solution.py
@@ -413,7 +413,7 @@
         (mine_b, sum_a),
         mib=16,
     )
-    got_b = [send(v, "col_1", j) for j, v in enumerate(others, 1)]
+    got_b = [send(others[j - 1], "col_1", j) for j in (1, 3, 2)]
     got_a = lax.all_to_all(sum_a, "col_0", 0, 0, tiled=True)
     send_b, scale, dots_b = call(
         grads_b_kernel,
@@ -435,7 +435,8 @@
         (got_a, scale, dots_b),
         mib=16,
     )
-    near = [send_b] + [send(send_b, "col_1", -j) for j in range(1, NX)]
+    near = [send_b] + [send(send_b, "col_1", -j) for j in (1, 3, 2)]
+    near = [near[0], near[1], near[3], near[2]]
     (near,) = call(
         join_kernel,
         (out(NX * 16, 3 * HB),),

time: 185 us -> 183 us (0.989)
    all_gather x1, waiting for transfers between devices: 10.6 us -> 8.42 us  [shards(): all_b = lax.all_gather(near, 'col_0', axis=0, tiled=True)]
where the time goes in v7:
time: 183 us
  blocking collectives  73.9 us (40%)
  Pallas kernels  32.8 us (18%)
  starting transfers between devices  32.6 us (18%)
  waiting for transfers between devices  24 us (13%)
  between operations  14.1 us (8%)
  local copies, waits for them, and re-layouts  3.35 us (2%)
  other arithmetic  1.91 us (1%)
    pallas_call x12, Pallas kernels, call(): pl.pallas_call(kernel, out_shape=outs, grid=grid, in_specs=in_specs, out_...  32.8 us
    all_to_all x1, blocking collectives, shards(): lax.all_to_all(part_a.reshape(NX, -1, a_cols), 'col_1', 0, 0, tiled=True)  31.9 us
    all_to_all x1, blocking collectives, from_everyone(): got = lax.all_to_all(copies, axis, split_axis=0, concat_axis=0, tiled=True)  24.4 us
    all_to_all x1, blocking collectives, shards(): lax.all_to_all(copies_a, 'col_0', 0, 0, tiled=True)  17.6 us
    all_to_all x1, starting transfers between devices, shards(): lax.all_to_all(both.reshape(-1, mine, both.shape[1]), 'row', 0, 0, tiled=...  10.1 us
    all_gather x1, waiting for transfers between devices, shards(): all_b = lax.all_gather(near, 'col_0', axis=0, tiled=True)  8.42 us
    ppermute x6, starting transfers between devices, send(): return lax.ppermute(v, axis, [(i, (i + step) % n) for i in range(n)])  8.18 us
    all_to_all x1, starting transfers between devices, shards(): got_a = lax.all_to_all(sum_a, 'col_0', 0, 0, tiled=True)  7.68 us
  transfers between devices with their start and end apart: 11, of which 10 were waited for; matrix products, arithmetic and copies ran while one was open for 2% of the time, Pallas kernels for 11%

profile of v7, /device:TPU:1, one launch (start us, length us, event | category | flops | bytes accessed | tf_op | source)
XLA Modules:
  0.0 182.7 jit_solution(2944468132261645138)
XLA Ops:
  7.2 1.6 shard_map.136
  8.8 6.6 %all-to-all-start = ((bf16[8,64,512]{2,1,0:T(8,128)(2,1)}), bf16[8,64,512]{2,1,0:T(8,128)(2,1)S(1)}, u32[]{:S(2)}, u32[]{:S(2)}) async-start(bf16[8,64,512]{2,1,0:T(8,128)(2,1)} %shard_map.136), calls=%async_computation | async-start | bytes 1048576 | tf_op jit(solution)/shard_map/all_to_all | solution.py:370
  15.4 1.4 copy.15.md
  16.8 3.9 %shard_map.137 = (bf16[256,768]{1,0:T(8,128)(2,1)}, bf16[256,768]{1,0:T(8,128)(2,1)}, bf16[768,256]{1,0:T(8,128)(2,1)}, bf16[256,1024]{1,0:T(8,128)(2,1)}, bf16[...) custom-call(s32[2,14]{1,0:T(2,128)} %mg.3, s32[2,14]{1,0:T(2,128)} %mu.3, s32[14,2]{1,0:T(8,128)} %copy.15.md, ...), custom_call_target="tpu_custom_call" | custom-call | bytes 6000000 | tf_op jit(solution)/shard_map/pallas_call | solution.py:33
  21.3 3.7 %all-to-all-done = bf16[8,64,512]{2,1,0:T(8,128)(2,1)S(1)} async-done(((bf16[8,64,512]{2,1,0:T(8,128)(2,1)}), bf16[8,64,512]{2,1,0:T(8,128)(2,1)S(1)}, u32[]{:S(2)}, u32[]{:S(2)}) %all-to-all-start) | async-done | bytes 524320 | tf_op jit(solution)/shard_map/all_to_all | solution.py:370
  24.9 0.8 copy-done.5
  25.7 4.3 %shard_map.138 = bf16[512,3200]{1,0:T(8,128)(2,1)} custom-call(s32[3]{0:T(128)} %pad_add_fusion.pos, bf16[512,512]{1,0:T(8,128)(2,1)} %bitcast.17, f32[1,256]{1,0:T(1,128)} %bitcast.11, bf16[256,1024]{1,0:T(8,128)(2,1)} %get-tuple-element.28.eg.rest_1_, bf16[256,1024]{1,0:T(8,128)(2,1)} %get-tuple-element.29.eu.rest_2_, ...), custom_call_target="tpu_custom_call" | custom-call | flops 805306368 | bytes 5000000 | tf_op jit(solution)/shard_map/pallas_call | solution.py:33
  30.0 3.6 %shard_map.139 = bf16[512,2304]{1,0:T(8,128)(2,1)} custom-call(bf16[512,512]{1,0:T(8,128)(2,1)} %bitcast.18, f32[1,256]{1,0:T(1,128)} %bitcast.12, bf16[256,768]{1,0:T(8,128)(2,1)} %get-tuple-element.31.eg.rest_1_, bf16[256,768]{1,0:T(8,128)(2,1)} %get-tuple-element.32.eu.rest_2_, bf16[768,256]{1,0:T(8,128)(2,1)} %get-tuple-element.33.ed.rest_3_), custom_call_target="tpu_custom_call" | custom-call | flops 603979776 | bytes 4000000 | tf_op jit(solution)/shard_map/pallas_call | solution.py:33
  33.7 31.9 %all_to_all.30 = bf16[4,128,2304]{2,1,0:T(8,128)(2,1)S(1)} all-to-all(bf16[4,128,2304]{2,1,0:T(8,128)(2,1)} %bitcast.21), channel_id=1, replica_groups=mesh['row'=8,'col_0'=8,'col_1'=4] {'col_1'}, dimensions={0} | all-to-all | bytes 4718592 | tf_op jit(solution)/shard_map/all_to_all | solution.py:403
  65.5 1.3 reduce_sum.12
  66.9 7.7 %all-to-all-start.2 = ((bf16[8,16,2304]{2,1,0:T(8,128)(2,1)}), bf16[8,16,2304]{2,1,0:T(8,128)(2,1)S(1)}, u32[]{:S(2)}, u32[]{:S(2)}) async-start(bf16[8,16,2304]{2,1,0:T(8,128)(2,1)} %bitcast.6.after), calls=%async_computation.3 | async-start | bytes 1179648 | tf_op jit(solution)/shard_map/all_to_all | solution.py:417
  74.6 1.9 %reduce-scatter.2.cloned.1.call-done.mine.part = bf16[64,3200]{1,0:T(8,128)(2,1)} async-done(((bf16[512,3200]{1,0:T(8,128)(2,1)}), bf16[64,3200]{1,0:T(8,128)(2,1)}) %reduce-scatter.2.cloned.1.call-update) | async-done | bytes 409616 | tf_op jit(solution)/shard_map/reduce_scatter | solution.py:404
  76.4 1.0 copy-done
  77.5 1.1 collective-permute-start
  78.6 1.7 collective-permute-start.1
  80.2 1.2 collective-permute-start.2
  81.5 0.8 collective-permute-done.j1
  82.4 3.2 %collective-permute-done.2.j3 = bf16[16,3200]{1,0:T(8,128)(2,1)S(1)} collective-permute-done((bf16[16,3200]{1,0:T(8,128)(2,1)S(1)}, bf16[16,3200]{1,0:T(8,128)(2,1)S(1)}, u32[]{:S(2)}, u32[]{:S(2)}) %collective-permute-start.2) | collective-permute-done | bytes 102432 | tf_op jit(solution)/shard_map/ppermute | solution.py:335
  85.8 2.2 %collective-permute-start.4 = (bf16[16,3072]{1,0:T(8,128)(2,1)S(1)}, bf16[16,3072]{1,0:T(8,128)(2,1)S(1)}, u32[]{:S(2)}, u32[]{:S(2)}) collective-permute-start(bf16[16,3072]{1,0:T(8,128)(2,1)S(1)} %get-tuple-element.37.refs_0_), channel_id=1, source_target_pairs={{0,2},{1,3},{2,0},{3,1},{4,6},{5,7},{6,4},{7,5},{8,10},{9,11},{10,... | collective-permute-start | bytes 294920 | tf_op jit(solution)/shard_map/ppermute | solution.py:335
  88.0 2.0 %collective-permute-start.3 = (bf16[16,3072]{1,0:T(8,128)(2,1)S(1)}, bf16[16,3072]{1,0:T(8,128)(2,1)S(1)}, u32[]{:S(2)}, u32[]{:S(2)}) collective-permute-start(bf16[16,3072]{1,0:T(8,128)(2,1)S(1)} %get-tuple-element.37.refs_0_), channel_id=1, source_target_pairs={{0,3},{1,0},{2,1},{3,2},{4,7},{5,4},{6,5},{7,6},{8,11},{9,8},{10,9... | collective-permute-start | bytes 294920 | tf_op jit(solution)/shard_map/ppermute | solution.py:335
  89.9 1.5 all-to-all-done.2.refs_4_.got
  91.5 0.9 collective-permute-done.3.refs_1_
  92.4 0.8 shard_map.142
  93.4 17.6 %all_to_all.31 = bf16[8,16,2432]{2,1,0:T(8,128)(2,1)S(1)} all-to-all(bf16[8,16,2432]{2,1,0:T(8,128)(2,1)S(1)} %shard_map.143), channel_id=1, replica_groups=mesh['row'=8,'col_0'=8,'col_1'=4] {'col_0'}, dimensions={0} | all-to-all | bytes 1245184 | tf_op jit(solution)/shard_map/all_to_all | solution.py:451
  111.2 24.4 %all_to_all.32 = bf16[4,128,2432]{2,1,0:T(8,128)(2,1)} all-to-all(bf16[4,128,2432]{2,1,0:T(8,128)(2,1)S(1)} %broadcast_in_dim.7), channel_id=1, replica_groups=mesh['row'=8,'col_0'=8,'col_1'=4] {'col_1'}, dimensions={0} | all-to-all | bytes 4980736 | tf_op jit(solution)/shard_map/all_to_all | solution.py:340
  135.6 4.8 %shard_map.144 = (f32[512,512]{1,0:T(8,128)}, f32[512,128]{1,0:T(8,128)}, bf16[512,128]{1,0:T(8,128)(2,1)}, f32[64,128]{1,0:T(8,128)}) custom-call(s32[3]{0:T(128)} %pad_add_fusion.pos, bf16[512,2432]{1,0:T(8,128)(2,1)} %bitcast.15, bf16[256,768]{1,0:T(8,128)(2,1)} %get-tuple-element.31.eg.rest_1_, bf16[256,768]{1,0:T(8,128)(2,1)} %get-tuple-element.32.eu.rest_2_, ...), custom_call_target="tpu_custom_call" | custom-call | flops 603979776 | bytes 6000000 | tf_op jit(solution)/shard_map/pallas_call | solution.py:33
  140.4 8.4 %all-gather.2.cloned.1.call-done.rest_0_.rest_2_ = bf16[512,3072]{1,0:T(8,128)(2,1)} async-done(((bf16[64,3072]{1,0:T(8,128)(2,1)}), bf16[512,3072]{1,0:T(8,128)(2,1)}) %all-gather.2.cloned.1.call-update) | async-done | bytes 3145744 | tf_op jit(solution)/shard_map/all_gather | solution.py:450
  148.8 5.2 %shard_map.145 = bf16[512,640]{1,0:T(8,128)(2,1)} custom-call(s32[3]{0:T(128)} %pad_add_fusion.pos, bf16[512,3072]{1,0:T(8,128)(2,1)} %all-gather.2.cloned.1.call-done.rest_0_.rest_2_, bf16[256,1024]{1,0:T(8,128)(2,1)} %get-tuple-element.28.eg.rest_1_, bf16[256,1024]{1,0:T(8,128)(2,1)} %get-tuple-element.29.eu.rest_2_, ...), custom_call_target="tpu_custom_call" | custom-call | flops 805306368 | bytes 8000000 | tf_op jit(solution)/shard_map/pallas_call | solution.py:33
  154.0 10.1 %all-to-all-start.5 = ((bf16[8,64,640]{2,1,0:T(8,128)(2,1)}), bf16[8,64,640]{2,1,0:T(8,128)(2,1)S(1)}, u32[]{:S(2)}, u32[]{:S(2)}) async-start(bf16[8,64,640]{2,1,0:T(8,128)(2,1)} %bitcast.22), calls=%async_computation.6 | async-start | bytes 1310720 | tf_op jit(solution)/shard_map/all_to_all | solution.py:480
  164.1 7.5 %shard_map.147 = (bf16[256,1792]{1,0:T(8,128)(2,1)}, bf16[256,1792]{1,0:T(8,128)(2,1)}, bf16[1792,256]{1,0:T(8,128)(2,1)}) custom-call(s32[3]{0:T(128)} %pad_add_fusion.pos, s32[2,14]{1,0:T(2,128)} %mg.3, s32[2,14]{1,0:T(2,128)} %mu.3, s32[14,2]{1,0:T(8,128)} %copy.15.md, f32[1,256]{1,0:T(1,128)} %bitcast.13, bf16[512,512]{1,0:T(8,128)(2,1)} %bitcast.20, ...), custom_call_target="tpu_custom_call" | custom-call | flops 1409286144 | bytes 9000000 | tf_op jit(solution)/shard_map/pallas_call | solution.py:33
  171.6 3.4 %all-to-all-done.5.got = bf16[8,64,640]{2,1,0:T(8,128)(2,1)S(1)} async-done(((bf16[8,64,640]{2,1,0:T(8,128)(2,1)}), bf16[8,64,640]{2,1,0:T(8,128)(2,1)S(1)}, u32[]{:S(2)}, u32[]{:S(2)}) %all-to-all-start.5) | async-done | bytes 655392 | tf_op jit(solution)/shard_map/all_to_all | solution.py:480
  175.0 0.8 shard_map.146
  (23 shorter events, 1.5 us)
Async XLA Ops:
  8.8 16.1 %all-to-all-start = ((bf16[8,64,512]{2,1,0:T(8,128)(2,1)}), bf16[8,64,512]{2,1,0:T(8,128)(2,1)S(1)}, u32[]{:S(2)}, u32[]{:S(2)}) async-start(bf16[8,64,512]{2,1,0:T(8,128)(2,1)} %shard_map.136), calls=%async_computation | async-start | bytes 1048576 | tf_op jit(solution)/shard_map/all_to_all | solution.py:370
  15.4 61.0 %reduce-scatter.2.cloned.1.call-start = ((), (), s32[]{:S(2)}) async-start(), calls=%async_computation.7 | async-start | bytes 3686400 | tf_op jit(solution)/shard_map/reduce_scatter | solution.py:404
  24.9 0.8 copy-start.5
  66.9 24.6 %all-to-all-start.2 = ((bf16[8,16,2304]{2,1,0:T(8,128)(2,1)}), bf16[8,16,2304]{2,1,0:T(8,128)(2,1)S(1)}, u32[]{:S(2)}, u32[]{:S(2)}) async-start(bf16[8,16,2304]{2,1,0:T(8,128)(2,1)} %bitcast.6.after), calls=%async_computation.3 | async-start | bytes 1179648 | tf_op jit(solution)/shard_map/all_to_all | solution.py:417
  74.5 74.3 %all-gather.2.cloned.1.call-start = ((), (), s32[]{:S(2)}) async-start(), calls=%async_computation.8 | async-start | bytes 3538944 | tf_op jit(solution)/shard_map/all_gather | solution.py:450
  76.4 1.0 copy-start
  77.5 4.8 %collective-permute-start = (bf16[16,3200]{1,0:T(8,128)(2,1)S(1)}, bf16[16,3200]{1,0:T(8,128)(2,1)S(1)}, u32[]{:S(2)}, u32[]{:S(2)}) collective-permute-start(bf16[16,3200]{1,0:T(8,128)(2,1)S(1)} %get-tuple-element.34), channel_id=1, source_target_pairs={{0,1},{1,2},{2,3},{3,0},{4,5},{5,6},{6,7},{7,4},{8,9},{9,10},{10,1... | collective-permute-start | bytes 307208 | tf_op jit(solution)/shard_map/ppermute | solution.py:335
  78.6 3.8 %collective-permute-start.1 = (bf16[16,3200]{1,0:T(8,128)(2,1)S(1)}, bf16[16,3200]{1,0:T(8,128)(2,1)S(1)}, u32[]{:S(2)}, u32[]{:S(2)}) collective-permute-start(bf16[16,3200]{1,0:T(8,128)(2,1)S(1)} %get-tuple-element.35), channel_id=1, source_target_pairs={{0,3},{1,0},{2,1},{3,2},{4,7},{5,4},{6,5},{7,6},{8,11},{9,8},{10,9... | collective-permute-start | bytes 307208 | tf_op jit(solution)/shard_map/ppermute | solution.py:335
  80.2 5.4 %collective-permute-start.2 = (bf16[16,3200]{1,0:T(8,128)(2,1)S(1)}, bf16[16,3200]{1,0:T(8,128)(2,1)S(1)}, u32[]{:S(2)}, u32[]{:S(2)}) collective-permute-start(bf16[16,3200]{1,0:T(8,128)(2,1)S(1)} %get-tuple-element.36), channel_id=1, source_target_pairs={{0,2},{1,3},{2,0},{3,1},{4,6},{5,7},{6,4},{7,5},{8,10},{9,11},{10,... | collective-permute-start | bytes 307208 | tf_op jit(solution)/shard_map/ppermute | solution.py:335
  85.7 5.8 %collective-permute-start.5 = (bf16[16,3072]{1,0:T(8,128)(2,1)S(1)}, bf16[16,3072]{1,0:T(8,128)(2,1)S(1)}, u32[]{:S(2)}, u32[]{:S(2)}) collective-permute-start(bf16[16,3072]{1,0:T(8,128)(2,1)S(1)} %get-tuple-element.37.refs_0_), channel_id=1, source_target_pairs={{0,1},{1,2},{2,3},{3,0},{4,5},{5,6},{6,7},{7,4},{8,9},{9,10},{10,1... | collective-permute-start | bytes 294920 | tf_op jit(solution)/shard_map/ppermute | solution.py:335
  85.8 5.7 %collective-permute-start.4 = (bf16[16,3072]{1,0:T(8,128)(2,1)S(1)}, bf16[16,3072]{1,0:T(8,128)(2,1)S(1)}, u32[]{:S(2)}, u32[]{:S(2)}) collective-permute-start(bf16[16,3072]{1,0:T(8,128)(2,1)S(1)} %get-tuple-element.37.refs_0_), channel_id=1, source_target_pairs={{0,2},{1,3},{2,0},{3,1},{4,6},{5,7},{6,4},{7,5},{8,10},{9,11},{10,... | collective-permute-start | bytes 294920 | tf_op jit(solution)/shard_map/ppermute | solution.py:335
  88.0 4.4 %collective-permute-start.3 = (bf16[16,3072]{1,0:T(8,128)(2,1)S(1)}, bf16[16,3072]{1,0:T(8,128)(2,1)S(1)}, u32[]{:S(2)}, u32[]{:S(2)}) collective-permute-start(bf16[16,3072]{1,0:T(8,128)(2,1)S(1)} %get-tuple-element.37.refs_0_), channel_id=1, source_target_pairs={{0,3},{1,0},{2,1},{3,2},{4,7},{5,4},{6,5},{7,6},{8,11},{9,8},{10,9... | collective-permute-start | bytes 294920 | tf_op jit(solution)/shard_map/ppermute | solution.py:335
  154.0 20.9 %all-to-all-start.5 = ((bf16[8,64,640]{2,1,0:T(8,128)(2,1)}), bf16[8,64,640]{2,1,0:T(8,128)(2,1)S(1)}, u32[]{:S(2)}, u32[]{:S(2)}) async-start(bf16[8,64,640]{2,1,0:T(8,128)(2,1)} %bitcast.22), calls=%async_computation.6 | async-start | bytes 1310720 | tf_op jit(solution)/shard_map/all_to_all | solution.py:480
  164.1 10.9 %copy-start.1 = (bf16[64,256]{1,0:T(8,128)(2,1)S(1)}, bf16[64,256]{1,0:T(8,128)(2,1)}, u32[]{:S(2)}) copy-start(bf16[64,256]{1,0:T(8,128)(2,1)} %x.3) | copy-start | bytes 98308
  164.1 10.9 %copy-start.2 = (bf16[64,256]{1,0:T(8,128)(2,1)S(1)}, bf16[64,256]{1,0:T(8,128)(2,1)}, u32[]{:S(2)}) copy-start(bf16[64,256]{1,0:T(8,128)(2,1)} %grad.3) | copy-start | bytes 98308
  164.1 10.9 %copy-start.3 = (f32[64,128]{1,0:T(8,128)S(1)}, f32[64,128]{1,0:T(8,128)}, u32[]{:S(2)}) copy-start(f32[64,128]{1,0:T(8,128)} %get-tuple-element.43.scale) | copy-start | bytes 98308
  164.1 10.9 %copy-start.4 = (f32[256]{0:T(256)S(1)}, f32[256]{0:T(256)}, u32[]{:S(2)}) copy-start(f32[256]{0:T(256)} %param.10) | copy-start | bytes 3076
Sparse Core Ops, SparseCore 0:
  30.2 46.2 reduce-scatter.1
  93.3 55.4 all-gather.1

commit v8 on v7

--- a/solution.py
+++ b/solution.py
@@ -128,6 +128,15 @@
         part[to, 3 * HB :] = square_sums(rows, nat, width)
     for t in range(0, left.shape[0], 512):
         products(left, slice(t, t + 512), (eg, eu, ed), part, slice(t, t + 512), HB)
+
+
+def sum_kernel(got, out):
+    for r in range(NZ):
+        at = slice(r * 16, r * 16 + 16)
+        total = got[0, at, :].astype(f32)
+        for j in range(1, NX):
+            total = total + got[j, at, :].astype(f32)
+        out[r] = total.astype(bf16)
 
 
 def split_kernel(mine, after, *outs):
@@ -402,7 +411,16 @@
     )
     got_a = lax.all_to_all(part_a.reshape(NX, -1, a_cols), "col_1", 0, 0, tiled=True)
     mine_b = lax.psum_scatter(part_b, "col_0", scatter_dimension=0, tiled=True)
-    sum_a = jnp.sum(got_a.astype(f32), axis=0).astype(bf16).reshape(NZ, -1, a_cols)
+    (sum_a,) = call(
+        sum_kernel,
+        (out(NZ, 16, a_cols),),
+        [vmem()],
+        [],
+        0,
+        2_500_000,
+        (got_a,),
+        mib=16,
+    )
     others = call(
         split_kernel,
         tuple([out(16, b_cols)] * (NX - 1)),

time: 183 us -> 185 us (1.011)
    pallas_call x12 -> x13, Pallas kernels: 32.8 us -> 33.9 us  [call(): pl.pallas_call(kernel, out_shape=outs, grid=grid, in_specs=in_specs, out_...]
    unnamed x13 -> x15, local copies, waits for them, and re-layouts: 3.18 us -> 4.19 us
  transfers between devices with their start and end apart: 11 -> 11, of which waited for: 10 -> 10; matrix products, arithmetic and copies ran while one was open for 2% -> 1% of each run, Pallas kernels for 11% -> 12%
where the time goes in v8:
time: 185 us; the launch traced here: 184 us
  blocking collectives  74.2 us (40%)
  Pallas kernels  33.9 us (18%)
  starting transfers between devices  32.8 us (18%)
  waiting for transfers between devices  24.1 us (13%)
  between operations  14.1 us (8%)
  local copies, waits for them, and re-layouts  4.36 us (2%)
    pallas_call x13, Pallas kernels, call(): pl.pallas_call(kernel, out_shape=outs, grid=grid, in_specs=in_specs, out_...  33.9 us
    all_to_all x1, blocking collectives, shards(): lax.all_to_all(part_a.reshape(NX, -1, a_cols), 'col_1', 0, 0, tiled=True)  31.9 us
    all_to_all x1, blocking collectives, from_everyone(): got = lax.all_to_all(copies, axis, split_axis=0, concat_axis=0, tiled=True)  24.5 us
    all_to_all x1, blocking collectives, shards(): lax.all_to_all(copies_a, 'col_0', 0, 0, tiled=True)  17.9 us
    all_to_all x1, starting transfers between devices, shards(): lax.all_to_all(both.reshape(-1, mine, both.shape[1]), 'row', 0, 0, tiled=...  9.7 us
    all_gather x1, waiting for transfers between devices, shards(): all_b = lax.all_gather(near, 'col_0', axis=0, tiled=True)  9.13 us
    ppermute x6, starting transfers between devices, send(): return lax.ppermute(v, axis, [(i, (i + step) % n) for i in range(n)])  8.74 us
    all_to_all x1, starting transfers between devices, shards(): got_a = lax.all_to_all(sum_a, 'col_0', 0, 0, tiled=True)  7.67 us
  transfers between devices with their start and end apart: 11, of which 10 were waited for; matrix products, arithmetic and copies ran while one was open for 1% of the time, Pallas kernels for 12%

profile of v8, /device:TPU:1, one launch (start us, length us, event | category | flops | bytes accessed | tf_op | source)
XLA Modules:
  0.0 184.2 jit_solution(6732666453029314188)
XLA Ops:
  7.2 1.6 shard_map.136
  8.8 6.6 %all-to-all-start = ((bf16[8,64,512]{2,1,0:T(8,128)(2,1)}), bf16[8,64,512]{2,1,0:T(8,128)(2,1)S(1)}, u32[]{:S(2)}, u32[]{:S(2)}) async-start(bf16[8,64,512]{2,1,0:T(8,128)(2,1)} %shard_map.136), calls=%async_computation | async-start | bytes 1048576 | tf_op jit(solution)/shard_map/all_to_all | solution.py:379
  15.4 1.4 copy.15.md
  16.8 3.9 %shard_map.137 = (bf16[256,768]{1,0:T(8,128)(2,1)}, bf16[256,768]{1,0:T(8,128)(2,1)}, bf16[768,256]{1,0:T(8,128)(2,1)}, bf16[256,1024]{1,0:T(8,128)(2,1)}, bf16[...) custom-call(s32[2,14]{1,0:T(2,128)} %mg.3, s32[2,14]{1,0:T(2,128)} %mu.3, s32[14,2]{1,0:T(8,128)} %copy.15.md, ...), custom_call_target="tpu_custom_call" | custom-call | bytes 6000000 | tf_op jit(solution)/shard_map/pallas_call | solution.py:33
  20.7 0.7 pad_add_fusion.pos
  21.3 3.6 %all-to-all-done = bf16[8,64,512]{2,1,0:T(8,128)(2,1)S(1)} async-done(((bf16[8,64,512]{2,1,0:T(8,128)(2,1)}), bf16[8,64,512]{2,1,0:T(8,128)(2,1)S(1)}, u32[]{:S(2)}, u32[]{:S(2)}) %all-to-all-start) | async-done | bytes 524320 | tf_op jit(solution)/shard_map/all_to_all | solution.py:379
  24.9 0.8 copy-done.6
  25.7 4.3 %shard_map.138 = bf16[512,3200]{1,0:T(8,128)(2,1)} custom-call(s32[3]{0:T(128)} %pad_add_fusion.pos, bf16[512,512]{1,0:T(8,128)(2,1)} %bitcast.16, f32[1,256]{1,0:T(1,128)} %bitcast.10, bf16[256,1024]{1,0:T(8,128)(2,1)} %get-tuple-element.28.eg.rest_1_, bf16[256,1024]{1,0:T(8,128)(2,1)} %get-tuple-element.29.eu.rest_2_, ...), custom_call_target="tpu_custom_call" | custom-call | flops 805306368 | bytes 5000000 | tf_op jit(solution)/shard_map/pallas_call | solution.py:33
  30.1 3.7 %shard_map.139 = bf16[512,2304]{1,0:T(8,128)(2,1)} custom-call(bf16[512,512]{1,0:T(8,128)(2,1)} %bitcast.17, f32[1,256]{1,0:T(1,128)} %bitcast.11, bf16[256,768]{1,0:T(8,128)(2,1)} %get-tuple-element.31.eg.rest_1_, bf16[256,768]{1,0:T(8,128)(2,1)} %get-tuple-element.32.eu.rest_2_, bf16[768,256]{1,0:T(8,128)(2,1)} %get-tuple-element.33.ed.rest_3_), custom_call_target="tpu_custom_call" | custom-call | flops 603979776 | bytes 4000000 | tf_op jit(solution)/shard_map/pallas_call | solution.py:33
  33.7 31.9 %all_to_all.30.got = bf16[4,128,2304]{2,1,0:T(8,128)(2,1)S(1)} all-to-all(bf16[4,128,2304]{2,1,0:T(8,128)(2,1)} %bitcast.20), channel_id=1, replica_groups=mesh['row'=8,'col_0'=8,'col_1'=4] {'col_1'}, dimensions={0} | all-to-all | bytes 4718592 | tf_op jit(solution)/shard_map/all_to_all | solution.py:412
  65.6 1.1 shard_map.140.after
  66.7 7.7 %all-to-all-start.2 = ((bf16[8,16,2304]{2,1,0:T(8,128)(2,1)}), bf16[8,16,2304]{2,1,0:T(8,128)(2,1)S(1)}, u32[]{:S(2)}, u32[]{:S(2)}) async-start(bf16[8,16,2304]{2,1,0:T(8,128)(2,1)} %shard_map.140.after), calls=%async_computation.3 | async-start | bytes 1179648 | tf_op jit(solution)/shard_map/all_to_all | solution.py:435
  74.4 1.9 %reduce-scatter.2.cloned.1.call-done.mine.part = bf16[64,3200]{1,0:T(8,128)(2,1)} async-done(((bf16[512,3200]{1,0:T(8,128)(2,1)}), bf16[64,3200]{1,0:T(8,128)(2,1)}) %reduce-scatter.2.cloned.1.call-update) | async-done | bytes 409616 | tf_op jit(solution)/shard_map/reduce_scatter | solution.py:413
  76.3 1.0 copy-done
  77.3 1.4 collective-permute-start
  78.7 1.3 collective-permute-start.1
  80.1 1.4 collective-permute-start.2
  82.5 2.9 %collective-permute-done.2.j3 = bf16[16,3200]{1,0:T(8,128)(2,1)S(1)} collective-permute-done((bf16[16,3200]{1,0:T(8,128)(2,1)S(1)}, bf16[16,3200]{1,0:T(8,128)(2,1)S(1)}, u32[]{:S(2)}, u32[]{:S(2)}) %collective-permute-start.2) | collective-permute-done | bytes 102432 | tf_op jit(solution)/shard_map/ppermute | solution.py:344
  85.4 1.0 copy-done.1
  86.7 2.4 %collective-permute-start.4 = (bf16[16,3072]{1,0:T(8,128)(2,1)S(1)}, bf16[16,3072]{1,0:T(8,128)(2,1)S(1)}, u32[]{:S(2)}, u32[]{:S(2)}) collective-permute-start(bf16[16,3072]{1,0:T(8,128)(2,1)S(1)} %get-tuple-element.37.refs_0_), channel_id=1, source_target_pairs={{0,2},{1,3},{2,0},{3,1},{4,6},{5,7},{6,4},{7,5},{8,10},{9,11},{10,... | collective-permute-start | bytes 294920 | tf_op jit(solution)/shard_map/ppermute | solution.py:344
  89.2 2.0 %collective-permute-start.3 = (bf16[16,3072]{1,0:T(8,128)(2,1)S(1)}, bf16[16,3072]{1,0:T(8,128)(2,1)S(1)}, u32[]{:S(2)}, u32[]{:S(2)}) collective-permute-start(bf16[16,3072]{1,0:T(8,128)(2,1)S(1)} %get-tuple-element.37.refs_0_), channel_id=1, source_target_pairs={{0,3},{1,0},{2,1},{3,2},{4,7},{5,4},{6,5},{7,6},{8,11},{9,8},{10,9... | collective-permute-start | bytes 294920 | tf_op jit(solution)/shard_map/ppermute | solution.py:344
  91.2 1.4 collective-permute-done.5.refs_3_
  93.3 0.8 shard_map.143
  94.3 17.9 %all_to_all.31 = bf16[8,16,2432]{2,1,0:T(8,128)(2,1)S(1)} all-to-all(bf16[8,16,2432]{2,1,0:T(8,128)(2,1)S(1)} %shard_map.144), channel_id=1, replica_groups=mesh['row'=8,'col_0'=8,'col_1'=4] {'col_0'}, dimensions={0} | all-to-all | bytes 1245184 | tf_op jit(solution)/shard_map/all_to_all | solution.py:469
  112.4 24.5 %all_to_all.32 = bf16[4,128,2432]{2,1,0:T(8,128)(2,1)} all-to-all(bf16[4,128,2432]{2,1,0:T(8,128)(2,1)S(1)} %broadcast_in_dim.7), channel_id=1, replica_groups=mesh['row'=8,'col_0'=8,'col_1'=4] {'col_1'}, dimensions={0} | all-to-all | bytes 4980736 | tf_op jit(solution)/shard_map/all_to_all | solution.py:349
  136.8 4.8 %shard_map.145 = (f32[512,512]{1,0:T(8,128)}, f32[512,128]{1,0:T(8,128)}, bf16[512,128]{1,0:T(8,128)(2,1)}, f32[64,128]{1,0:T(8,128)}) custom-call(s32[3]{0:T(128)} %pad_add_fusion.pos, bf16[512,2432]{1,0:T(8,128)(2,1)} %bitcast.14, bf16[256,768]{1,0:T(8,128)(2,1)} %get-tuple-element.31.eg.rest_1_, bf16[256,768]{1,0:T(8,128)(2,1)} %get-tuple-element.32.eu.rest_2_, ...), custom_call_target="tpu_custom_call" | custom-call | flops 603979776 | bytes 6000000 | tf_op jit(solution)/shard_map/pallas_call | solution.py:33
  141.6 9.1 %all-gather.2.cloned.1.call-done.rest_0_.rest_2_ = bf16[512,3072]{1,0:T(8,128)(2,1)} async-done(((bf16[64,3072]{1,0:T(8,128)(2,1)}), bf16[512,3072]{1,0:T(8,128)(2,1)}) %all-gather.2.cloned.1.call-update) | async-done | bytes 3145744 | tf_op jit(solution)/shard_map/all_gather | solution.py:468
  150.7 5.2 %shard_map.146 = bf16[512,640]{1,0:T(8,128)(2,1)} custom-call(s32[3]{0:T(128)} %pad_add_fusion.pos, bf16[512,3072]{1,0:T(8,128)(2,1)} %all-gather.2.cloned.1.call-done.rest_0_.rest_2_, bf16[256,1024]{1,0:T(8,128)(2,1)} %get-tuple-element.28.eg.rest_1_, bf16[256,1024]{1,0:T(8,128)(2,1)} %get-tuple-element.29.eu.rest_2_, ...), custom_call_target="tpu_custom_call" | custom-call | flops 805306368 | bytes 8000000 | tf_op jit(solution)/shard_map/pallas_call | solution.py:33
  155.9 9.7 %all-to-all-start.5 = ((bf16[8,64,640]{2,1,0:T(8,128)(2,1)}), bf16[8,64,640]{2,1,0:T(8,128)(2,1)S(1)}, u32[]{:S(2)}, u32[]{:S(2)}) async-start(bf16[8,64,640]{2,1,0:T(8,128)(2,1)} %bitcast.21), calls=%async_computation.6 | async-start | bytes 1310720 | tf_op jit(solution)/shard_map/all_to_all | solution.py:498
  165.6 7.5 %shard_map.148 = (bf16[256,1792]{1,0:T(8,128)(2,1)}, bf16[256,1792]{1,0:T(8,128)(2,1)}, bf16[1792,256]{1,0:T(8,128)(2,1)}) custom-call(s32[3]{0:T(128)} %pad_add_fusion.pos, s32[2,14]{1,0:T(2,128)} %mg.3, s32[2,14]{1,0:T(2,128)} %mu.3, s32[14,2]{1,0:T(8,128)} %copy.15.md, f32[1,256]{1,0:T(1,128)} %bitcast.12, bf16[512,512]{1,0:T(8,128)(2,1)} %bitcast.19, ...), custom_call_target="tpu_custom_call" | custom-call | flops 1409286144 | bytes 9000000 | tf_op jit(solution)/shard_map/pallas_call | solution.py:33
  173.1 3.4 %all-to-all-done.5.got = bf16[8,64,640]{2,1,0:T(8,128)(2,1)S(1)} async-done(((bf16[8,64,640]{2,1,0:T(8,128)(2,1)}), bf16[8,64,640]{2,1,0:T(8,128)(2,1)S(1)}, u32[]{:S(2)}, u32[]{:S(2)}) %all-to-all-start.5) | async-done | bytes 655392 | tf_op jit(solution)/shard_map/all_to_all | solution.py:498
  176.5 0.8 shard_map.147
  (25 shorter events, 2.5 us)
Async XLA Ops:
  8.8 16.1 %all-to-all-start = ((bf16[8,64,512]{2,1,0:T(8,128)(2,1)}), bf16[8,64,512]{2,1,0:T(8,128)(2,1)S(1)}, u32[]{:S(2)}, u32[]{:S(2)}) async-start(bf16[8,64,512]{2,1,0:T(8,128)(2,1)} %shard_map.136), calls=%async_computation | async-start | bytes 1048576 | tf_op jit(solution)/shard_map/all_to_all | solution.py:379
  15.4 60.9 %reduce-scatter.2.cloned.1.call-start = ((), (), s32[]{:S(2)}) async-start(), calls=%async_computation.7 | async-start | bytes 3686400 | tf_op jit(solution)/shard_map/reduce_scatter | solution.py:413
  24.9 0.8 copy-start.6
  66.7 24.6 %all-to-all-start.2 = ((bf16[8,16,2304]{2,1,0:T(8,128)(2,1)}), bf16[8,16,2304]{2,1,0:T(8,128)(2,1)S(1)}, u32[]{:S(2)}, u32[]{:S(2)}) async-start(bf16[8,16,2304]{2,1,0:T(8,128)(2,1)} %shard_map.140.after), calls=%async_computation.3 | async-start | bytes 1179648 | tf_op jit(solution)/shard_map/all_to_all | solution.py:435
  74.3 76.4 %all-gather.2.cloned.1.call-start = ((), (), s32[]{:S(2)}) async-start(), calls=%async_computation.8 | async-start | bytes 3538944 | tf_op jit(solution)/shard_map/all_gather | solution.py:468
  76.3 1.0 copy-start
  77.3 4.8 %collective-permute-start = (bf16[16,3200]{1,0:T(8,128)(2,1)S(1)}, bf16[16,3200]{1,0:T(8,128)(2,1)S(1)}, u32[]{:S(2)}, u32[]{:S(2)}) collective-permute-start(bf16[16,3200]{1,0:T(8,128)(2,1)S(1)} %get-tuple-element.34), channel_id=1, source_target_pairs={{0,1},{1,2},{2,3},{3,0},{4,5},{5,6},{6,7},{7,4},{8,9},{9,10},{10,1... | collective-permute-start | bytes 307208 | tf_op jit(solution)/shard_map/ppermute | solution.py:344
  78.7 3.8 %collective-permute-start.1 = (bf16[16,3200]{1,0:T(8,128)(2,1)S(1)}, bf16[16,3200]{1,0:T(8,128)(2,1)S(1)}, u32[]{:S(2)}, u32[]{:S(2)}) collective-permute-start(bf16[16,3200]{1,0:T(8,128)(2,1)S(1)} %get-tuple-element.35), channel_id=1, source_target_pairs={{0,3},{1,0},{2,1},{3,2},{4,7},{5,4},{6,5},{7,6},{8,11},{9,8},{10,9... | collective-permute-start | bytes 307208 | tf_op jit(solution)/shard_map/ppermute | solution.py:344
  80.1 5.4 %collective-permute-start.2 = (bf16[16,3200]{1,0:T(8,128)(2,1)S(1)}, bf16[16,3200]{1,0:T(8,128)(2,1)S(1)}, u32[]{:S(2)}, u32[]{:S(2)}) collective-permute-start(bf16[16,3200]{1,0:T(8,128)(2,1)S(1)} %get-tuple-element.36), channel_id=1, source_target_pairs={{0,2},{1,3},{2,0},{3,1},{4,6},{5,7},{6,4},{7,5},{8,10},{9,11},{10,... | collective-permute-start | bytes 307208 | tf_op jit(solution)/shard_map/ppermute | solution.py:344
  85.4 1.0 copy-start.1
  86.6 6.1 %collective-permute-start.5 = (bf16[16,3072]{1,0:T(8,128)(2,1)S(1)}, bf16[16,3072]{1,0:T(8,128)(2,1)S(1)}, u32[]{:S(2)}, u32[]{:S(2)}) collective-permute-start(bf16[16,3072]{1,0:T(8,128)(2,1)S(1)} %get-tuple-element.37.refs_0_), channel_id=1, source_target_pairs={{0,1},{1,2},{2,3},{3,0},{4,5},{5,6},{6,7},{7,4},{8,9},{9,10},{10,1... | collective-permute-start | bytes 294920 | tf_op jit(solution)/shard_map/ppermute | solution.py:344
  86.7 6.0 %collective-permute-start.4 = (bf16[16,3072]{1,0:T(8,128)(2,1)S(1)}, bf16[16,3072]{1,0:T(8,128)(2,1)S(1)}, u32[]{:S(2)}, u32[]{:S(2)}) collective-permute-start(bf16[16,3072]{1,0:T(8,128)(2,1)S(1)} %get-tuple-element.37.refs_0_), channel_id=1, source_target_pairs={{0,2},{1,3},{2,0},{3,1},{4,6},{5,7},{6,4},{7,5},{8,10},{9,11},{10,... | collective-permute-start | bytes 294920 | tf_op jit(solution)/shard_map/ppermute | solution.py:344
  89.2 4.1 %collective-permute-start.3 = (bf16[16,3072]{1,0:T(8,128)(2,1)S(1)}, bf16[16,3072]{1,0:T(8,128)(2,1)S(1)}, u32[]{:S(2)}, u32[]{:S(2)}) collective-permute-start(bf16[16,3072]{1,0:T(8,128)(2,1)S(1)} %get-tuple-element.37.refs_0_), channel_id=1, source_target_pairs={{0,3},{1,0},{2,1},{3,2},{4,7},{5,4},{6,5},{7,6},{8,11},{9,8},{10,9... | collective-permute-start | bytes 294920 | tf_op jit(solution)/shard_map/ppermute | solution.py:344
  155.9 20.6 %all-to-all-start.5 = ((bf16[8,64,640]{2,1,0:T(8,128)(2,1)}), bf16[8,64,640]{2,1,0:T(8,128)(2,1)S(1)}, u32[]{:S(2)}, u32[]{:S(2)}) async-start(bf16[8,64,640]{2,1,0:T(8,128)(2,1)} %bitcast.21), calls=%async_computation.6 | async-start | bytes 1310720 | tf_op jit(solution)/shard_map/all_to_all | solution.py:498
  165.6 10.9 %copy-start.2 = (bf16[64,256]{1,0:T(8,128)(2,1)S(1)}, bf16[64,256]{1,0:T(8,128)(2,1)}, u32[]{:S(2)}) copy-start(bf16[64,256]{1,0:T(8,128)(2,1)} %x.3) | copy-start | bytes 98308
  165.6 10.9 %copy-start.3 = (bf16[64,256]{1,0:T(8,128)(2,1)S(1)}, bf16[64,256]{1,0:T(8,128)(2,1)}, u32[]{:S(2)}) copy-start(bf16[64,256]{1,0:T(8,128)(2,1)} %grad.3) | copy-start | bytes 98308
  165.6 10.9 %copy-start.4 = (f32[64,128]{1,0:T(8,128)S(1)}, f32[64,128]{1,0:T(8,128)}, u32[]{:S(2)}) copy-start(f32[64,128]{1,0:T(8,128)} %get-tuple-element.43.scale) | copy-start | bytes 98308
  165.6 10.9 %copy-start.5 = (f32[256]{0:T(256)S(1)}, f32[256]{0:T(256)}, u32[]{:S(2)}) copy-start(f32[256]{0:T(256)} %param.10) | copy-start | bytes 3076
Sparse Core Ops, SparseCore 0:
  30.2 46.0 reduce-scatter.1
  94.2 56.5 all-gather.1
